TPU v7x, 128 devices: a whole 4x4x4 slice. The times are simulated.
128 devices in a mesh: ha: 8 (over z_lo, y), ta: 16 (over x, z_hi, core).
Axes of the slice: x: 4, y: 4, z: 4 (z_hi: 2, z_lo: 2; z = z_hi * 2 + z_lo), core: 2. Of those that a mesh axis runs over, the one named last changes fastest.
Arguments:
- latent: bfloat16 [32, 128, 48, 384], P(None, ('ha', 'ta')), may hold values from -54 to 54
- group_start: int32 [16], replicated, may hold values from 0 to 30, as said below
- norm_gain: float32 [384], replicated, may hold values from 0.1 to 1.9
- conv_weight: bfloat16 [3, 3, 3, 384, 384], replicated, may hold values from -0.0625 to 0.0625
- conv_bias: float32 [384], replicated, may hold values from -3 to 3
Outputs:
- tiles: bfloat16 [64, 128, 48, 384], P('ta', 'ha')
Inputs may be any that keep to these rules, and one draw needn't show every extreme that they name: group_start rises from 0; every group holds 1 to 4 frames and the last ends at 32; the first and the last group hold 2 frames, the second and the second-to-last one frame each, and some group holds exactly 4.
All inputs are finite; a program needn't handle non-finite values.
Results may differ from a plain program's by a relative error of at most 0.0021.
Values may be sent and summed in bfloat16 or wider, within the bound.
No kernel may reach another device: no remote copies, remote signals or barrier semaphores. Data moves between devices by JAX's collectives and lax.ppermute only.
A program may use at most 192 MiB of HBM per device.

v0:
```python
import jax
import jax.numpy as jnp
from jax import lax
from jax.sharding import PartitionSpec as P

FMAX = 4


def shifted(x, axis, by):
    devices = lax.axis_size(axis)
    pairs = [(i, i + by) for i in range(devices) if 0 <= i + by < devices]
    return lax.ppermute(x, axis, pairs)


def with_halo(x, sides, width):
    for axis, dim in sides:
        devices, length = (lax.axis_size(axis), x.shape[dim])
        up = [(i, (i + 1) % devices) for i in range(devices - 1)]
        down = [(j, i) for i, j in up]
        last = lax.slice_in_dim(x, length - width, length, axis=dim)
        first = lax.slice_in_dim(x, 0, width, axis=dim)
        before = lax.ppermute(last, axis, up)
        after = lax.ppermute(first, axis, down)
        x = jnp.concatenate([before, x, after], axis=dim)
    return x


def activate(values, norm_gain):
    widened = values.astype(jnp.float32)
    scaled = (
        widened * lax.rsqrt(jnp.mean(widened * widened, axis=-1, keepdims=True) + 1e-06) * norm_gain
    )
    return jax.nn.silu(scaled).astype(jnp.bfloat16)


def pick_groups(source_frames, group_start, lengths, before):
    time_devices = group_start.shape[0]
    offsets = jnp.arange(FMAX + before, dtype=jnp.int32) - before
    sources = (group_start[:, None] + offsets[None, :]).reshape(-1)
    usable = (
        (offsets[None, :] < lengths[:, None]) & (group_start[:, None] + offsets[None, :] >= 0)
    ).reshape(-1)
    clipped = jnp.clip(sources, 0, source_frames.shape[0] - 1)
    picked = jnp.take(source_frames, clipped, axis=0)
    picked = jnp.where(usable[:, None, None, None], picked, jnp.zeros_like(picked))
    return picked.reshape((time_devices, FMAX + before) + source_frames.shape[1:])


def convolve(padded, conv_weight, frame_count):
    row_count = padded.shape[1] - 2
    col_count = padded.shape[2] - 2
    channels = padded.shape[3]
    running = jnp.zeros((frame_count * row_count * col_count, conv_weight.shape[4]), jnp.float32)
    for time_tap in range(3):
        for row_tap in range(3):
            tapped = jnp.concatenate(
                [
                    padded[
                        time_tap : time_tap + frame_count,
                        row_tap : row_tap + row_count,
                        col_tap : col_tap + col_count,
                    ]
                    for col_tap in range(3)
                ],
                axis=3,
            )
            kernel = conv_weight[time_tap, row_tap].reshape(3 * channels, -1)
            running = running + jnp.dot(
                tapped.reshape(-1, 3 * channels), kernel, preferred_element_type=jnp.float32
            )
    return running.reshape(frame_count, row_count, col_count, -1)


def fix_tail(earlier, latest, latest_length):
    joined = jnp.stack([earlier[1], latest[1]])
    return jnp.where(latest_length >= 2, latest, joined)


def on_device(latent, group_start, norm_gain, conv_weight, conv_bias):
    frame_total = latent.shape[0]
    lengths = jnp.concatenate([group_start[1:], jnp.array([frame_total], jnp.int32)]) - group_start
    position = lax.axis_index("ta")
    own_length = lengths[position]
    outgoing = pick_groups(latent, group_start, lengths, 0)
    arrived = lax.all_to_all(outgoing, "ta", split_axis=0, concat_axis=2, tiled=True)[0]
    activated = activate(arrived, norm_gain)
    blanks = jnp.zeros((2,) + activated.shape[1:], jnp.bfloat16)
    raw_tail = lax.dynamic_slice_in_dim(
        jnp.concatenate([blanks, activated], axis=0), own_length, 2, 0
    )
    near_raw = shifted(raw_tail, "ta", 1)
    far_raw = shifted(raw_tail, "ta", 2)
    prior_length = lengths[jnp.maximum(position - 1, 0)]
    history = fix_tail(far_raw, near_raw, prior_length)
    extended = jnp.concatenate([history, activated], axis=0)
    rimmed = with_halo(extended, (("ha", 1),), 1)
    padded = jnp.pad(rimmed, ((0, 0), (0, 0), (1, 1), (0, 0)))
    convolved = convolve(padded, conv_weight, FMAX)
    summed = arrived.astype(jnp.float32) + convolved + conv_bias
    usable = jnp.arange(FMAX, dtype=jnp.int32) < own_length
    return jnp.where(usable[:, None, None, None], summed, 0.0).astype(jnp.bfloat16)


def solution(mesh):
    placed = (P(None, ("ha", "ta"), None, None), P(), P(), P(), P())
    return jax.shard_map(
        on_device, mesh=mesh, in_specs=placed, out_specs=P("ta", "ha", None, None), check_vma=False
    )
```

profile of v0, /device:TPU:89, one launch (start us, length us, event | category | flops | bytes accessed | tf_op | source)
XLA Modules:
  0.0 247.3 jit_solution(18353345298619882213)
XLA Ops:
  0.0 0.8 slice.139
  0.8 0.7 fusion.18
  1.6 0.7 add_subtract_fusion
  2.3 0.7 fusion.20
  3.1 2.3 gather_fusion
  5.4 3.5 %select_bitcast_fusion = bf16[16,4,1,48,384]{4,3,1,2,0:T(8,128)(2,1)} fusion(bf16[16,4,1,48,384]{4,3,1,0,2:T(8,128)(2,1)} %bitcast.83, pred[16,4]{1,0:T(8,128)(4,1)S(1)} %get-tuple-element.47, pred[16,4]{1,0:T(8,128)(4,1)S(1)} %get-tuple-element.46), kind=kLoop, calls=%fused_computation.41 | loop fusion | flops 2359296 | bytes 4718720 | tf_op jit(solution)/shard_map/jit(_where)/select_n | solution.py:45
  8.9 7.7 %all-to-all-start = ((bf16[16,4,1,48,384]{4,3,1,2,0:T(8,128)(2,1)}), bf16[16,4,1,48,384]{4,3,1,2,0:T(8,128)(2,1)S(1)}, u32[]{:S(2)}, u32[]{:S(2)}) async-start(bf16[16,4,1,48,384]{4,3,1,2,0:T(8,128)(2,1)} %select_bitcast_fusion), calls=%async_computation | async-start | bytes 4718592 | tf_op jit(solution)/shard_map/all_to_all | solution.py:85
  16.6 0.6 fusion.26
  19.3 30.0 %all-to-all-done = bf16[16,4,1,48,384]{4,3,1,2,0:T(8,128)(2,1)S(1)} async-done(((bf16[16,4,1,48,384]{4,3,1,2,0:T(8,128)(2,1)}), bf16[16,4,1,48,384]{4,3,1,2,0:T(8,128)(2,1)S(1)}, u32[]{:S(2)}, u32[]{:S(2)}) %all-to-all-start) | async-done | bytes 2359328 | tf_op jit(solution)/shard_map/all_to_all | solution.py:85
  49.3 0.5 fusion.3
  49.8 0.9 copy-done.2
  50.8 2.8 %fusion.10 = bf16[4,16,48,384]{3,2,1,0:T(8,128)(2,1)S(1)} fusion(f32[384]{0:T(512)S(1)} %copy-done.31, f32[4,16,48]{2,1,0:T(8,128)S(1)} %add_rsqrt_fusion, bf16[16,4,1,48,384]{4,3,1,2,0:T(8,128)(2,1)} %copy-done.2), kind=kLoop, calls=%fused_computation.25 | loop fusion | flops 9437184 | bytes 4732416 | tf_op jit(solution)/shard_map/convert_element_type | solution.py:33
  53.9 1.9 collective-permute-start
  55.8 1.9 collective-permute-start.1
  58.4 5.6 %fusion.22 = (bf16[1,1,3,384,384]{4,3,2,1,0:T(8,128)(2,1)}, bf16[1,1,3,384,384]{4,3,2,1,0:T(8,128)(2,1)}, bf16[1,1,3,384,384]{4,3,2,1,0:T(8,128)(2,1)}, bf16[1,1...) fusion(bf16[3,3,3,384,384]{4,3,2,1,0:T(8,128)(2,1)} %param.9), kind=kLoop, calls=%fused_computation.58 | loop fusion | bytes 15925248 | tf_op jit(solution)/shard_map/slice | solution.py:67
  64.0 14.9 %collective-permute-done = bf16[2,16,48,384]{3,2,1,0:T(8,128)(2,1)S(1)} collective-permute-done((bf16[2,16,48,384]{3,2,1,0:T(8,128)(2,1)S(1)}, bf16[2,16,48,384]{3,2,1,0:T(8,128)(2,1)S(1)}, u32[]{:S(2)}, u32[]{:S(2)}) %collective-permute-start) | collective-permute-done | bytes 1179680 | tf_op jit(solution)/shard_map/ppermute | solution.py:12
  79.0 18.7 %collective-permute-done.1 = bf16[2,16,48,384]{3,2,1,0:T(8,128)(2,1)S(1)} collective-permute-done((bf16[2,16,48,384]{3,2,1,0:T(8,128)(2,1)S(1)}, bf16[2,16,48,384]{3,2,1,0:T(8,128)(2,1)S(1)}, u32[]{:S(2)}, u32[]{:S(2)}) %collective-permute-start.1) | collective-permute-done | bytes 1179680 | tf_op jit(solution)/shard_map/ppermute | solution.py:12
  98.0 3.2 %collective-permute-start.2 = (bf16[6,1,48,384]{3,2,1,0:T(8,128)(2,1)S(1)}, bf16[6,1,48,384]{3,2,1,0:T(8,128)(2,1)S(1)}, u32[]{:S(2)}, u32[]{:S(2)}) collective-permute-start(bf16[6,1,48,384]{3,2,1,0:T(8,128)(2,1)S(1)} %get-tuple-element.40), channel_id=1, source_target_pairs={{0,16},{16,32},{32,48},{48,64},{64,80},{80,96},{96,112},{1,17},{17... | collective-permute-start | bytes 663560 | tf_op jit(solution)/shard_map/ppermute | solution.py:22
  101.3 2.6 %collective-permute-start.3 = (bf16[6,1,48,384]{3,2,1,0:T(8,128)(2,1)S(1)}, bf16[6,1,48,384]{3,2,1,0:T(8,128)(2,1)S(1)}, u32[]{:S(2)}, u32[]{:S(2)}) collective-permute-start(bf16[6,1,48,384]{3,2,1,0:T(8,128)(2,1)S(1)} %get-tuple-element.41), channel_id=1, source_target_pairs={{16,0},{32,16},{48,32},{64,48},{80,64},{96,80},{112,96},{17,1},{33... | collective-permute-start | bytes 663560 | tf_op jit(solution)/shard_map/ppermute | solution.py:23
  103.9 0.7 iota_compare_fusion.3
  104.6 1.7 fusion.17
  106.3 3.8 %collective-permute-done.3 = bf16[6,1,48,384]{3,2,1,0:T(8,128)(2,1)S(1)} collective-permute-done((bf16[6,1,48,384]{3,2,1,0:T(8,128)(2,1)S(1)}, bf16[6,1,48,384]{3,2,1,0:T(8,128)(2,1)S(1)}, u32[]{:S(2)}, u32[]{:S(2)}) %collective-permute-start.3) | collective-permute-done | bytes 221216 | tf_op jit(solution)/shard_map/ppermute | solution.py:23
  110.1 0.7 copy-done.22
  110.7 4.0 %select_maximum_fusion = bf16[6,18,50,384]{3,2,1,0:T(8,128)(2,1)} fusion(bf16[6,1,48,384]{3,2,1,0:T(8,128)(2,1)S(1)} %collective-permute-done.3, bf16[6,1,48,384]{3,2,1,0:T(8,128)(2,1)S(1)} %collective-permute-done.2, bf16[4,16,48,384]{3,2,1,0:T(8,128)(2,1)S(1)} %fusion.10, bf16[2,16,48,384]{3,2,1,0:T(8,128)(2,1)S(1)} %maximum_select_fusion), kind=kLoop, calls=%fused_computation.30 | loop fusion | flops 31104000 | bytes 8128512 | tf_op jit(solution)/shard_map/concatenate | solution.py:24
  114.8 34.5 %fusion.23 = (bf16[4,16,48,384]{3,2,1,0:T(8,128)(2,1)}, bf16[4,16,48,384]{3,2,1,0:T(8,128)(2,1)}, bf16[4,16,48,384]{3,2,1,0:T(8,128)(2,1)}, bf16[4,16,48,384]{3,...) fusion(bf16[6,18,50,384]{3,2,1,0:T(8,128)(2,1)} %select_maximum, ...), kind=kLoop, calls=%fused_computation.59 | loop fusion | bytes 84934656 | tf_op jit(solution)/shard_map/slice | solution.py:58
  149.3 2.7 %pad_maximum_fusion.9 = (bf16[6,17,48,384]{3,2,1,0:T(8,128)(2,1)S(1)}, bf16[6,17,48,384]{3,2,1,0:T(8,128)(2,1)S(1)}) fusion(bf16[6,1,48,384]{3,2,1,0:T(8,128)(2,1)} %copy-done.22, bf16[4,16,48,384]{3,2,1,0:T(8,128)(2,1)S(1)} %fusion.10, bf16[2,16,48,384]{3,2,1,0:T(8,128)(2,1)S(1)} %maximum_select_fusion, bf16[6,1,48,384]{3,2,1,0:T(8,128)(2,1)} %copy-done.21), kind=kLoop, calls=%fused_computation.36 | loop fusion | flops 7520256 | bytes 11501568 | tf_op jit(solution)/shard_map/concatenate | solution.py:24
  152.0 2.2 fusion.24
  154.2 3.3 %pad_maximum_fusion.1 = bf16[4,16,48,1152]{3,2,1,0:T(8,128)(2,1)S(1)} fusion(bf16[4,16,48,384]{3,2,1,0:T(8,128)(2,1)} %get-tuple-element.29, bf16[4,16,48,384]{3,2,1,0:T(8,128)(2,1)S(1)} %get-tuple-element.50, bf16[4,16,48,384]{3,2,1,0:T(8,128)(2,1)} %get-tuple-element.30), kind=kLoop, calls=%fused_computation.7 | loop fusion | flops 21233664 | bytes 14155776 | tf_op jit(solution)/shard_map/concatenate | solution.py:56
  157.6 5.6 %fusion.27 = f32[3072,384]{1,0:T(8,128)} fusion(bf16[3072,1152]{1,0:T(8,128)(2,1)S(1)} %bitcast.86, bf16[1152,384]{1,0:T(8,128)(2,1)S(1)} %bitcast.100), kind=kOutput, calls=%fused_computation.63 | convolution fusion | flops 2717908992 | bytes 12681216 | tf_op jit(solution)/shard_map/dot_general | solution.py:68
  163.3 0.7 pad_maximum_fusion.2
  164.0 0.5 copy-done.29
  164.4 5.7 %fusion.28 = f32[3072,384]{1,0:T(8,128)} fusion(bf16[3072,1152]{1,0:T(8,128)(2,1)S(1)} %bitcast.87, bf16[1152,384]{1,0:T(8,128)(2,1)S(1)} %bitcast.99), kind=kOutput, calls=%fused_computation.64 | convolution fusion | flops 2717908992 | bytes 12681216 | tf_op jit(solution)/shard_map/dot_general | solution.py:68
  170.1 0.7 pad_maximum_fusion.3
  170.8 0.5 copy-done.28
  171.3 5.9 %fusion.29 = f32[3072,384]{1,0:T(8,128)} fusion(bf16[3072,1152]{1,0:T(8,128)(2,1)S(1)} %bitcast.88, bf16[1152,384]{1,0:T(8,128)(2,1)S(1)} %bitcast.98), kind=kOutput, calls=%fused_computation.65 | convolution fusion | flops 2717908992 | bytes 12681216 | tf_op jit(solution)/shard_map/dot_general | solution.py:68
  177.1 0.7 pad_maximum_fusion.4
  177.9 0.4 copy-done.27
  178.3 5.7 %fusion.30 = f32[3072,384]{1,0:T(8,128)} fusion(bf16[3072,1152]{1,0:T(8,128)(2,1)S(1)} %bitcast.89, bf16[1152,384]{1,0:T(8,128)(2,1)S(1)} %bitcast.97), kind=kOutput, calls=%fused_computation.66 | convolution fusion | flops 2717908992 | bytes 12681216 | tf_op jit(solution)/shard_map/dot_general | solution.py:68
  184.1 0.7 pad_maximum_fusion.5
  185.2 5.7 %fusion.32 = f32[3072,384]{1,0:T(8,128)} fusion(bf16[3072,1152]{1,0:T(8,128)(2,1)S(1)} %bitcast.90, bf16[1152,384]{1,0:T(8,128)(2,1)S(1)} %bitcast.96), kind=kOutput, calls=%fused_computation.68 | convolution fusion | flops 2717908992 | bytes 12681216 | tf_op jit(solution)/shard_map/dot_general | solution.py:68
  190.9 0.7 pad_maximum_fusion.6
  192.1 5.6 %fusion.33 = f32[3072,384]{1,0:T(8,128)} fusion(bf16[3072,1152]{1,0:T(8,128)(2,1)S(1)} %bitcast.91, bf16[1152,384]{1,0:T(8,128)(2,1)S(1)} %bitcast.95), kind=kOutput, calls=%fused_computation.69 | convolution fusion | flops 2717908992 | bytes 12681216 | tf_op jit(solution)/shard_map/dot_general | solution.py:68
  197.8 3.9 %fusion.2 = (bf16[4,16,48,1152]{3,2,1,0:T(8,128)(2,1)}, bf16[4,16,48,1152]{3,2,1,0:T(8,128)(2,1)S(1)}) fusion(bf16[4,16,48,384]{3,2,1,0:T(8,128)(2,1)S(1)} %fusion.10, bf16[2,16,48,384]{3,2,1,0:T(8,128)(2,1)S(1)} %maximum_select_fusion, bf16[4,16,48,384]{3,2,1,0:T(8,128)(2,1)S(1)} %copy-done.6, bf16[4,16,48,384]{3,2,1,0:T(8,128)(2,1)S(1)} %copy-done.7, ...), kind=kLoop, calls=%fused_computation.6 | loop fusion | flops 49545216 | bytes 27131904 | tf_op jit(solution)/shard_map/concatenate | solution.py:56
  201.7 9.3 %fusion.31 = f32[3072,384]{1,0:T(8,128)} fusion(bf16[3072,1152]{1,0:T(8,128)(2,1)} %bitcast.85, bf16[1152,384]{1,0:T(8,128)(2,1)S(1)} %bitcast.94), kind=kOutput, calls=%fused_computation.67 | convolution fusion | flops 2717908992 | bytes 12681216 | tf_op jit(solution)/shard_map/dot_general | solution.py:68
  211.0 5.7 %fusion.34 = f32[3072,384]{1,0:T(8,128)} fusion(bf16[3072,1152]{1,0:T(8,128)(2,1)S(1)} %bitcast.84, bf16[1152,384]{1,0:T(8,128)(2,1)S(1)} %bitcast.93), kind=kOutput, calls=%fused_computation.70 | convolution fusion | flops 2717908992 | bytes 12681216 | tf_op jit(solution)/shard_map/dot_general | solution.py:68
  216.7 3.6 %pad_maximum_fusion.8 = bf16[4,16,48,1152]{3,2,1,0:T(8,128)(2,1)} fusion(bf16[4,16,48,384]{3,2,1,0:T(8,128)(2,1)S(1)} %copy-done.9, bf16[4,16,48,384]{3,2,1,0:T(8,128)(2,1)S(1)} %get-tuple-element.32, bf16[4,16,48,384]{3,2,1,0:T(8,128)(2,1)S(1)} %copy-done.8), kind=kLoop, calls=%fused_computation.14 | loop fusion | flops 21233664 | bytes 14155776 | tf_op jit(solution)/shard_map/concatenate | solution.py:56
  220.3 21.3 %add_add_fusion = f32[3072,384]{1,0:T(8,128)} fusion(f32[3072,384]{1,0:T(8,128)} %fusion.34, f32[3072,384]{1,0:T(8,128)} %fusion.33, f32[3072,384]{1,0:T(8,128)} %fusion.32, f32[3072,384]{1,0:T(8,128)} %fusion.31, f32[3072,384]{1,0:T(8,128)} %fusion.30, f32[3072,384]{1,0:T(8,128)} %fusion.29, f32[3072,384]{1,0:T(8,128)} %fusion.27, ...), kind=kOutput, calls=%fused_computation.29 | convolution fusion | flops 2727346176 | bytes 50429952 | tf_op jit(solution)/shard_map/dot_general | solution.py:68
  241.6 5.4 %fusion.13 = bf16[4,16,48,384]{3,2,1,0:T(8,128)(2,1)} fusion(f32[4,16,48,384]{3,2,1,0:T(8,128)} %bitcast.82, f32[384]{0:T(512)S(1)} %copy-done.32, pred[4]{0:T(512)(128)(4,1)S(1)} %iota_compare_fusion.3, bf16[16,4,1,48,384]{4,3,1,2,0:T(8,128)(2,1)} %copy-done.2), kind=kLoop, calls=%fused_computation.28 | loop fusion | flops 5898240 | bytes 9438724 | tf_op jit(solution)/shard_map/convert_element_type | solution.py:101
  (71 shorter events, 1.7 us)
Async XLA Ops:
  0.0 3.1 %copy-start = (bf16[32,1,48,384]{3,2,1,0:T(8,128)(2,1)S(1)}, bf16[32,1,48,384]{3,2,1,0:T(8,128)(2,1)}, u32[]{:S(2)}) copy-start(bf16[32,1,48,384]{3,2,1,0:T(8,128)(2,1)} %param.6) | copy-start | bytes 3538948
  8.9 41.9 %copy-start.31 = (f32[384]{0:T(512)S(1)}, f32[384]{0:T(512)}, u32[]{:S(2)}) copy-start(f32[384]{0:T(512)} %param.8) | copy-start | bytes 4612
  8.9 40.4 %all-to-all-start = ((bf16[16,4,1,48,384]{4,3,1,2,0:T(8,128)(2,1)}), bf16[16,4,1,48,384]{4,3,1,2,0:T(8,128)(2,1)S(1)}, u32[]{:S(2)}, u32[]{:S(2)}) async-start(bf16[16,4,1,48,384]{4,3,1,2,0:T(8,128)(2,1)} %select_bitcast_fusion), calls=%async_computation | async-start | bytes 4718592 | tf_op jit(solution)/shard_map/all_to_all | solution.py:85
  49.3 1.5 copy-start.2
  53.9 25.0 %collective-permute-start = (bf16[2,16,48,384]{3,2,1,0:T(8,128)(2,1)S(1)}, bf16[2,16,48,384]{3,2,1,0:T(8,128)(2,1)S(1)}, u32[]{:S(2)}, u32[]{:S(2)}) collective-permute-start(bf16[2,16,48,384]{3,2,1,0:T(8,128)(2,1)S(1)} %pad_dynamic-slice_fusion), channel_id=1, source_target_pairs={{0,1},{1,2},{2,3},{3,4},{4,5},{5,6},{6,7},{7,8},{8,9},{9,10},{10,1... | collective-permute-start | bytes 3538952 | tf_op jit(solution)/shard_map/ppermute | solution.py:12
  55.8 41.9 %collective-permute-start.1 = (bf16[2,16,48,384]{3,2,1,0:T(8,128)(2,1)S(1)}, bf16[2,16,48,384]{3,2,1,0:T(8,128)(2,1)S(1)}, u32[]{:S(2)}, u32[]{:S(2)}) collective-permute-start(bf16[2,16,48,384]{3,2,1,0:T(8,128)(2,1)S(1)} %pad_dynamic-slice_fusion), channel_id=1, source_target_pairs={{0,2},{1,3},{2,4},{3,5},{4,6},{5,7},{6,8},{7,9},{8,10},{9,11},{10,... | collective-permute-start | bytes 3538952 | tf_op jit(solution)/shard_map/ppermute | solution.py:12
  98.0 8.2 %collective-permute-start.2 = (bf16[6,1,48,384]{3,2,1,0:T(8,128)(2,1)S(1)}, bf16[6,1,48,384]{3,2,1,0:T(8,128)(2,1)S(1)}, u32[]{:S(2)}, u32[]{:S(2)}) collective-permute-start(bf16[6,1,48,384]{3,2,1,0:T(8,128)(2,1)S(1)} %get-tuple-element.40), channel_id=1, source_target_pairs={{0,16},{16,32},{32,48},{48,64},{64,80},{80,96},{96,112},{1,17},{17... | collective-permute-start | bytes 663560 | tf_op jit(solution)/shard_map/ppermute | solution.py:22
  101.3 8.8 %collective-permute-start.3 = (bf16[6,1,48,384]{3,2,1,0:T(8,128)(2,1)S(1)}, bf16[6,1,48,384]{3,2,1,0:T(8,128)(2,1)S(1)}, u32[]{:S(2)}, u32[]{:S(2)}) collective-permute-start(bf16[6,1,48,384]{3,2,1,0:T(8,128)(2,1)S(1)} %get-tuple-element.41), channel_id=1, source_target_pairs={{16,0},{32,16},{48,32},{64,48},{80,64},{96,80},{112,96},{17,1},{33... | collective-permute-start | bytes 663560 | tf_op jit(solution)/shard_map/ppermute | solution.py:23
  106.3 3.8 %copy-start.21 = (bf16[6,1,48,384]{3,2,1,0:T(8,128)(2,1)}, bf16[6,1,48,384]{3,2,1,0:T(8,128)(2,1)S(1)}, u32[]{:S(2)}) copy-start(bf16[6,1,48,384]{3,2,1,0:T(8,128)(2,1)S(1)} %collective-permute-done.2) | copy-start | bytes 663556
  110.0 0.7 copy-start.22
  154.2 3.4 %copy-start.30 = (bf16[1,1,3,384,384]{4,3,2,1,0:T(8,128)(2,1)S(1)}, bf16[1,1,3,384,384]{4,3,2,1,0:T(8,128)(2,1)}, u32[]{:S(2)}) copy-start(bf16[1,1,3,384,384]{4,3,2,1,0:T(8,128)(2,1)} %get-tuple-element.12) | copy-start | bytes 2654212
  157.6 5.7 %copy-start.3 = (bf16[4,16,48,384]{3,2,1,0:T(8,128)(2,1)S(1)}, bf16[4,16,48,384]{3,2,1,0:T(8,128)(2,1)}, u32[]{:S(2)}) copy-start(bf16[4,16,48,384]{3,2,1,0:T(8,128)(2,1)} %fusion.17) | copy-start | bytes 7077892
  157.6 5.7 %copy-start.18 = (bf16[4,16,48,384]{3,2,1,0:T(8,128)(2,1)S(1)}, bf16[4,16,48,384]{3,2,1,0:T(8,128)(2,1)}, u32[]{:S(2)}) copy-start(bf16[4,16,48,384]{3,2,1,0:T(8,128)(2,1)} %get-tuple-element.27) | copy-start | bytes 7077892
  157.6 5.7 %copy-start.19 = (bf16[4,16,48,384]{3,2,1,0:T(8,128)(2,1)S(1)}, bf16[4,16,48,384]{3,2,1,0:T(8,128)(2,1)}, u32[]{:S(2)}) copy-start(bf16[4,16,48,384]{3,2,1,0:T(8,128)(2,1)} %get-tuple-element.28) | copy-start | bytes 7077892
  163.3 1.2 copy-start.29
  164.4 5.7 %copy-start.16 = (bf16[4,16,48,384]{3,2,1,0:T(8,128)(2,1)S(1)}, bf16[4,16,48,384]{3,2,1,0:T(8,128)(2,1)}, u32[]{:S(2)}) copy-start(bf16[4,16,48,384]{3,2,1,0:T(8,128)(2,1)} %get-tuple-element.25) | copy-start | bytes 7077892
  164.4 5.7 %copy-start.17 = (bf16[4,16,48,384]{3,2,1,0:T(8,128)(2,1)S(1)}, bf16[4,16,48,384]{3,2,1,0:T(8,128)(2,1)}, u32[]{:S(2)}) copy-start(bf16[4,16,48,384]{3,2,1,0:T(8,128)(2,1)} %get-tuple-element.26) | copy-start | bytes 7077892
  170.1 1.2 copy-start.28
  171.3 5.9 %copy-start.14 = (bf16[4,16,48,384]{3,2,1,0:T(8,128)(2,1)S(1)}, bf16[4,16,48,384]{3,2,1,0:T(8,128)(2,1)}, u32[]{:S(2)}) copy-start(bf16[4,16,48,384]{3,2,1,0:T(8,128)(2,1)} %get-tuple-element.23) | copy-start | bytes 7077892
  171.3 5.9 %copy-start.15 = (bf16[4,16,48,384]{3,2,1,0:T(8,128)(2,1)S(1)}, bf16[4,16,48,384]{3,2,1,0:T(8,128)(2,1)}, u32[]{:S(2)}) copy-start(bf16[4,16,48,384]{3,2,1,0:T(8,128)(2,1)} %get-tuple-element.24) | copy-start | bytes 7077892
  177.1 1.2 copy-start.27
  178.3 5.7 %copy-start.12 = (bf16[4,16,48,384]{3,2,1,0:T(8,128)(2,1)S(1)}, bf16[4,16,48,384]{3,2,1,0:T(8,128)(2,1)}, u32[]{:S(2)}) copy-start(bf16[4,16,48,384]{3,2,1,0:T(8,128)(2,1)} %get-tuple-element.19) | copy-start | bytes 7077892
  178.3 5.7 %copy-start.13 = (bf16[4,16,48,384]{3,2,1,0:T(8,128)(2,1)S(1)}, bf16[4,16,48,384]{3,2,1,0:T(8,128)(2,1)}, u32[]{:S(2)}) copy-start(bf16[4,16,48,384]{3,2,1,0:T(8,128)(2,1)} %get-tuple-element.20) | copy-start | bytes 7077892
  184.1 1.2 copy-start.26
  185.2 5.7 %copy-start.10 = (bf16[4,16,48,384]{3,2,1,0:T(8,128)(2,1)S(1)}, bf16[4,16,48,384]{3,2,1,0:T(8,128)(2,1)}, u32[]{:S(2)}) copy-start(bf16[4,16,48,384]{3,2,1,0:T(8,128)(2,1)} %get-tuple-element.17) | copy-start | bytes 7077892
  185.2 5.7 %copy-start.11 = (bf16[4,16,48,384]{3,2,1,0:T(8,128)(2,1)S(1)}, bf16[4,16,48,384]{3,2,1,0:T(8,128)(2,1)}, u32[]{:S(2)}) copy-start(bf16[4,16,48,384]{3,2,1,0:T(8,128)(2,1)} %get-tuple-element.18) | copy-start | bytes 7077892
  190.9 1.2 copy-start.25
  192.1 5.7 %copy-start.4 = (bf16[4,16,48,384]{3,2,1,0:T(8,128)(2,1)S(1)}, bf16[4,16,48,384]{3,2,1,0:T(8,128)(2,1)}, u32[]{:S(2)}) copy-start(bf16[4,16,48,384]{3,2,1,0:T(8,128)(2,1)} %get-tuple-element.15) | copy-start | bytes 7077892
  192.1 5.7 %copy-start.5 = (bf16[4,16,48,384]{3,2,1,0:T(8,128)(2,1)S(1)}, bf16[4,16,48,384]{3,2,1,0:T(8,128)(2,1)}, u32[]{:S(2)}) copy-start(bf16[4,16,48,384]{3,2,1,0:T(8,128)(2,1)} %get-tuple-element.16) | copy-start | bytes 7077892
  192.1 5.7 %copy-start.6 = (bf16[4,16,48,384]{3,2,1,0:T(8,128)(2,1)S(1)}, bf16[4,16,48,384]{3,2,1,0:T(8,128)(2,1)}, u32[]{:S(2)}) copy-start(bf16[4,16,48,384]{3,2,1,0:T(8,128)(2,1)} %get-tuple-element.21) | copy-start | bytes 7077892
  192.1 5.7 %copy-start.7 = (bf16[4,16,48,384]{3,2,1,0:T(8,128)(2,1)S(1)}, bf16[4,16,48,384]{3,2,1,0:T(8,128)(2,1)}, u32[]{:S(2)}) copy-start(bf16[4,16,48,384]{3,2,1,0:T(8,128)(2,1)} %get-tuple-element.22) | copy-start | bytes 7077892
  197.8 3.9 %copy-start.24 = (bf16[1,1,3,384,384]{4,3,2,1,0:T(8,128)(2,1)S(1)}, bf16[1,1,3,384,384]{4,3,2,1,0:T(8,128)(2,1)}, u32[]{:S(2)}) copy-start(bf16[1,1,3,384,384]{4,3,2,1,0:T(8,128)(2,1)} %get-tuple-element.8) | copy-start | bytes 2654212
  201.7 9.3 %copy-start.23 = (bf16[1,1,3,384,384]{4,3,2,1,0:T(8,128)(2,1)S(1)}, bf16[1,1,3,384,384]{4,3,2,1,0:T(8,128)(2,1)}, u32[]{:S(2)}) copy-start(bf16[1,1,3,384,384]{4,3,2,1,0:T(8,128)(2,1)} %get-tuple-element.13) | copy-start | bytes 2654212
  211.0 5.7 %copy-start.8 = (bf16[4,16,48,384]{3,2,1,0:T(8,128)(2,1)S(1)}, bf16[4,16,48,384]{3,2,1,0:T(8,128)(2,1)}, u32[]{:S(2)}) copy-start(bf16[4,16,48,384]{3,2,1,0:T(8,128)(2,1)} %get-tuple-element.14) | copy-start | bytes 7077892
  211.0 5.7 %copy-start.9 = (bf16[4,16,48,384]{3,2,1,0:T(8,128)(2,1)S(1)}, bf16[4,16,48,384]{3,2,1,0:T(8,128)(2,1)}, u32[]{:S(2)}) copy-start(bf16[4,16,48,384]{3,2,1,0:T(8,128)(2,1)} %get-tuple-element.31) | copy-start | bytes 7077892
  216.7 3.6 %copy-start.20 = (bf16[1,1,3,384,384]{4,3,2,1,0:T(8,128)(2,1)S(1)}, bf16[1,1,3,384,384]{4,3,2,1,0:T(8,128)(2,1)}, u32[]{:S(2)}) copy-start(bf16[1,1,3,384,384]{4,3,2,1,0:T(8,128)(2,1)} %get-tuple-element.5) | copy-start | bytes 2654212
  220.3 21.3 %copy-start.32 = (f32[384]{0:T(512)S(1)}, f32[384]{0:T(512)}, u32[]{:S(2)}) copy-start(f32[384]{0:T(512)} %param.10) | copy-start | bytes 4612
  241.6 5.4 %copy-start.1 = (bf16[32,1,48,384]{3,2,1,0:T(8,128)(2,1)S(1)}, bf16[32,1,48,384]{3,2,1,0:T(8,128)(2,1)}, u32[]{:S(2)}) copy-start(bf16[32,1,48,384]{3,2,1,0:T(8,128)(2,1)} %param.6) | copy-start | bytes 3538948
where the time goes:
time: 252 us; the launch traced here: 247 us
  matrix products  70.5 us (28%)
  waiting for transfers between devices  67.4 us (27%)
  local copies, waits for them, and re-layouts  50.5 us (20%)
  other arithmetic  38.2 us (15%)
  starting transfers between devices  17.4 us (7%)
  between operations  3.26 us (1%)
    dot_general x9, matrix products, convolve(): jnp.dot(tapped.reshape(-1, 3 * channels), kernel, preferred_element_type=...  70.5 us
    slice x2, local copies, waits for them, and re-layouts, convolve(): padded[time_tap:time_tap + frame_count, row_tap:row_tap + row_count, col_...  36.7 us
    ppermute x2, waiting for transfers between devices, shifted(): return lax.ppermute(x, axis, pairs)  33.6 us
    all_to_all x1, waiting for transfers between devices, on_device(): lax.all_to_all(outgoing, 'ta', split_axis=0, concat_axis=2, tiled=True)[0]  30 us
    concatenate x8, other arithmetic, convolve(): jnp.concatenate([padded[time_tap:time_tap + frame_count, row_tap:row_tap...  14.4 us
    all_to_all x1, starting transfers between devices, on_device(): lax.all_to_all(outgoing, 'ta', split_axis=0, concat_axis=2, tiled=True)[0]  7.72 us
    concatenate x2, other arithmetic, with_halo(): x = jnp.concatenate([before, x, after], axis=dim)  6.73 us
    slice x1, local copies, waits for them, and re-layouts, convolve(): kernel = conv_weight[time_tap, row_tap].reshape(3 * channels, -1)  5.64 us
  transfers between devices with their start and end apart: 5, of which 4 were waited for; matrix products, arithmetic and copies ran while one was open for 4% of the time, Pallas kernels for 0%

commit v1 on v0

v1 whole, which is shorter than its diff:
```python
import functools

import jax
import jax.numpy as jnp
from jax import lax
from jax.experimental import pallas as pl
from jax.experimental.pallas import tpu as pltpu
from jax.sharding import Mesh, PartitionSpec as P

FMAX = 4
HIST = 2
SPAN = FMAX + HIST


def activate(raw, gain):
    wide = raw.astype(jnp.float32)
    power = jnp.mean(wide * wide, axis=-1, keepdims=True)
    scaled = wide * lax.rsqrt(power + 1e-06) * gain
    return (scaled / (1.0 + jnp.exp(-scaled))).astype(jnp.bfloat16)


def pack_kernel(bases, frames, packed, sems):
    chips, window = packed.shape[:2]
    copies = [
        pltpu.make_async_copy(frames.at[pl.ds(bases[c], window)], packed.at[c], sems.at[c])
        for c in range(chips)
    ]
    for copy in copies:
        copy.start()
    for copy in copies:
        copy.wait()


def pack(frames, bases, window):
    chips = bases.shape[0]
    return pl.pallas_call(
        pack_kernel,
        out_shape=jax.ShapeDtypeStruct((chips, window) + frames.shape[1:], frames.dtype),
        in_specs=[
            pl.BlockSpec(memory_space=pltpu.SMEM),
            pl.BlockSpec(memory_space=pl.ANY),
        ],
        out_specs=pl.BlockSpec(memory_space=pl.ANY),
        scratch_shapes=[pltpu.SemaphoreType.DMA((chips,))],
    )(bases, frames)


def conv_kernel(
    plan, own, other, own_rim, other_rim, weight, gain, bias, out,
    taps, raw, act, sums, result, weight_sems, frame_sems, out_sems,
):
    pairs = own.shape[0]
    rows, cols, chans = 2 * pairs, own.shape[2], own.shape[3]
    length, skip, base, core, history = (plan[i] for i in range(5))

    def arrivals(i):
        index = jnp.clip(i + skip, 0, SPAN - 1)
        return [
            pltpu.make_async_copy(
                own.at[:, base + index], raw.at[i, pl.ds(core, pairs), 1 - core], frame_sems.at[i, 0]
            ),
            pltpu.make_async_copy(
                other.at[:, index], raw.at[i, pl.ds(1 - core, pairs), core], frame_sems.at[i, 1]
            ),
            pltpu.make_async_copy(
                own_rim.at[base + index], raw.at[i, pairs * (1 - core), 1 - core], frame_sems.at[i, 2]
            ),
            pltpu.make_async_copy(
                other_rim.at[index], raw.at[i, pairs * core, core], frame_sems.at[i, 3]
            ),
        ]

    incoming = [arrivals(i) for i in range(SPAN)]
    for copies in incoming:
        for copy in copies:
            copy.start()
    tap_copies = []
    for a in range(3):
        for b in range(3):
            for e in range(3):
                tap_copies.append(
                    pltpu.make_async_copy(
                        weight.at[a, b, e],
                        taps.at[pl.ds((3 * a + b) * chans, chans), pl.ds(e * chans, chans)],
                        weight_sems.at[9 * a + 3 * b + e],
                    )
                )
    for copy in tap_copies:
        copy.start()

    sums[0, :, 7:8, :] = jnp.zeros((rows, 1, chans), jnp.float32)
    sums[2, :, cols + 8 : cols + 9, :] = jnp.zeros((rows, 1, chans), jnp.float32)

    def activated(i):
        return activate(raw[i].reshape(rows + 2, cols, chans), gain[...])

    for i in range(3):
        for copy in incoming[i]:
            copy.wait()
    act[2] = activated(2)

    @pl.when(history > 0)
    def _():
        act[0] = activated(0)
        act[1] = activated(1)

    @pl.when(history == 0)
    def _():
        act[0] = jnp.zeros(act.shape[1:], act.dtype)
        act[1] = jnp.zeros(act.shape[1:], act.dtype)

    for i in range(3, SPAN):
        for copy in incoming[i]:
            copy.wait()
    for copy in tap_copies:
        copy.wait()

    def one_frame(k, carry):
        lhs = jnp.concatenate(
            [
                act[k + a, pl.ds(b, rows)].reshape(rows * cols, chans)
                for a in range(3)
                for b in range(3)
            ],
            axis=1,
        )
        for e in range(3):
            part = jnp.dot(
                lhs, taps[:, pl.ds(e * chans, chans)], preferred_element_type=jnp.float32
            )
            sums[e, :, 8 : cols + 8, :] = part.reshape(rows, cols, chans)
        later = jnp.minimum(k + 3, SPAN - 1)
        act[later] = activated(later)
        convolved = (
            sums[0, :, 7 : cols + 7, :] + sums[1, :, 8 : cols + 8, :] + sums[2, :, 9 : cols + 9, :]
        )
        latent = raw[k + 2].reshape(rows + 2, cols, chans)[1 : rows + 1].astype(jnp.float32)
        result[k] = (latent + convolved + bias[...]).astype(result.dtype)
        pltpu.make_async_copy(result.at[k], out.at[k], out_sems.at[k]).start()
        return carry

    lax.fori_loop(0, length, one_frame, 0)

    def blank_frame(k, carry):
        result[k] = jnp.zeros(result.shape[1:], result.dtype)
        pltpu.make_async_copy(result.at[k], out.at[k], out_sems.at[k]).start()
        return carry

    lax.fori_loop(length, FMAX, blank_frame, 0)
    for k in range(FMAX):
        pltpu.make_async_copy(result.at[k], out.at[k], out_sems.at[k]).wait()


def conv(plan, own, other, own_rim, other_rim, weight, gain, bias):
    pairs, _, cols, chans = own.shape
    rows = 2 * pairs
    hbm = pl.BlockSpec(memory_space=pl.ANY)
    vmem = pl.BlockSpec(memory_space=pltpu.VMEM)
    return pl.pallas_call(
        conv_kernel,
        out_shape=jax.ShapeDtypeStruct((FMAX, rows, cols, chans), own.dtype),
        in_specs=[pl.BlockSpec(memory_space=pltpu.SMEM)] + [hbm] * 5 + [vmem] * 2,
        out_specs=hbm,
        scratch_shapes=[
            pltpu.VMEM((9 * chans, 3 * chans), jnp.bfloat16),
            pltpu.VMEM((SPAN, pairs + 1, 2, cols, chans), jnp.bfloat16),
            pltpu.VMEM((SPAN, rows + 2, cols, chans), jnp.bfloat16),
            pltpu.VMEM((3, rows, cols + 16, chans), jnp.float32),
            pltpu.VMEM((FMAX, rows, cols, chans), jnp.bfloat16),
            pltpu.SemaphoreType.DMA((27,)),
            pltpu.SemaphoreType.DMA((SPAN, 4)),
            pltpu.SemaphoreType.DMA((FMAX,)),
        ],
        compiler_params=pltpu.CompilerParams(vmem_limit_bytes=56 * 2**20),
    )(plan, own, other, own_rim, other_rim, weight, gain.reshape(1, chans), bias.reshape(1, chans))


def on_device(window, latent, group_start, norm_gain, conv_weight, conv_bias):
    frame_total = latent.shape[0]
    ends = jnp.concatenate([group_start[1:], jnp.array([frame_total], jnp.int32)])
    lengths = ends - group_start
    cores = lax.axis_size("core")
    stripes = lax.axis_size("ha")
    core = lax.axis_index("core")
    chip = lax.axis_index("tc")
    bases = jnp.clip(group_start[::cores] - HIST, 0, frame_total - window)
    packed = pack(latent[:, 0], bases, window)
    arrived = lax.all_to_all(packed, "tc", split_axis=0, concat_axis=0, tiled=True)

    rim = jnp.where(core == 0, arrived[0], arrived[-1])
    pairs = [((h + 1) * cores, h * cores) for h in range(stripes - 1)]
    pairs += [(h * cores + 1, (h + 1) * cores + 1) for h in range(stripes - 1)]
    own_rim = lax.ppermute(rim, ("ha", "core"), pairs)

    offsets = lax.dynamic_slice_in_dim(group_start, chip * cores, cores) - HIST - bases[chip]
    firsts = jnp.clip(offsets, 0, window - SPAN)
    swap = [(0, 1), (1, 0)]
    other = lax.ppermute(
        lax.dynamic_slice_in_dim(arrived, firsts[1 - core], SPAN, 1), "core", swap
    )
    other_rim = lax.ppermute(
        lax.dynamic_slice_in_dim(own_rim, firsts[1 - core], SPAN, 0), "core", swap
    )
    group = chip * cores + core
    plan = jnp.stack(
        [
            lengths[group],
            offsets[core] - firsts[core],
            firsts[core],
            core,
            group,
        ]
    ).astype(jnp.int32)
    return conv(plan, arrived, other, own_rim, other_rim, conv_weight, norm_gain, conv_bias)


def solution(mesh):
    devices = mesh.devices
    fine = Mesh(
        devices.reshape(devices.shape[0], devices.shape[1] // 2, 2), ("ha", "tc", "core")
    )
    placed = (P(None, ("ha", "tc", "core"), None, None), P(), P(), P(), P())
    return jax.shard_map(
        functools.partial(on_device, 2 * FMAX + HIST),
        mesh=fine,
        in_specs=placed,
        out_specs=P(("tc", "core"), "ha", None, None),
        check_vma=False,
    )
```

time: 252 us -> 204 us (0.81)
  the two profiles are of different devices: /device:TPU:89 before, /device:TPU:30 now
where the time goes in v1:
time: 204 us; the launch traced here: 203 us
  Pallas kernels  135 us (66%)
  waiting for transfers between devices  43.3 us (21%)
  starting transfers between devices  10.7 us (5%)
  local copies, waits for them, and re-layouts  9.26 us (5%)
  between operations  3.33 us (2%)
  other arithmetic  2.12 us (1%)
    pallas_call x1, Pallas kernels, pack(): pl.pallas_call(pack_kernel, out_shape=jax.ShapeDtypeStruct((chips, window...  91.2 us
    pallas_call x1, Pallas kernels, conv(): pl.pallas_call(conv_kernel, out_shape=jax.ShapeDtypeStruct((FMAX, rows, c...  43.5 us
    all_to_all x1, waiting for transfers between devices, on_device(): lax.all_to_all(packed, 'tc', split_axis=0, concat_axis=0, tiled=True)  36.1 us
    all_to_all x1, starting transfers between devices, on_device(): lax.all_to_all(packed, 'tc', split_axis=0, concat_axis=0, tiled=True)  8.1 us
    ppermute x1, waiting for transfers between devices, on_device(): own_rim = lax.ppermute(rim, ('ha', 'core'), pairs)  7.17 us
  transfers between devices with their start and end apart: 4, of which 2 were waited for; matrix products, arithmetic and copies ran while one was open for 4% of the time, Pallas kernels for 0%

profile of v1, /device:TPU:30, one launch (start us, length us, event | category | flops | bytes accessed | tf_op | source)
XLA Modules:
  0.0 203.4 jit_solution(12468432345139265643)
XLA Ops:
  0.0 0.7 slice.13
  0.7 0.5 add_clamp_fusion.bases
  1.3 91.2 %shard_map.64 = bf16[8,10,48,384]{3,2,1,0:T(8,128)(2,1)} custom-call(s32[8]{0:T(128)} %add_clamp_fusion.bases, bf16[32,48,384]{2,1,0:T(8,128)(2,1)} %bitcast.7), custom_call_target="tpu_custom_call" | custom-call | tf_op jit(solution)/shard_map/pallas_call | solution.py:36
  92.4 0.0 copy-start.6
  92.5 0.0 copy-start.5
  92.5 8.1 %all-to-all-start = ((bf16[8,10,48,384]{3,2,1,0:T(8,128)(2,1)}), bf16[8,10,48,384]{3,2,1,0:T(8,128)(2,1)S(1)}, u32[]{:S(2)}, u32[]{:S(2)}) async-start(bf16[8,10,48,384]{3,2,1,0:T(8,128)(2,1)} %shard_map.64), calls=%async_computation | async-start | bytes 5898240 | tf_op jit(solution)/shard_map/all_to_all | solution.py:188
  100.6 0.0 copy-start.3
  100.6 0.0 copy-start.4
  100.6 0.0 copy-done.6
  100.6 0.6 dynamic_slice.28
  101.2 0.0 copy-done.5
  101.2 0.7 broadcast_clamp_fusion
  101.9 0.6 fusion.1
  104.5 36.1 %all-to-all-done.own = bf16[8,10,48,384]{3,2,1,0:T(8,128)(2,1)S(1)} async-done(((bf16[8,10,48,384]{3,2,1,0:T(8,128)(2,1)}), bf16[8,10,48,384]{3,2,1,0:T(8,128)(2,1)S(1)}, u32[]{:S(2)}, u32[]{:S(2)}) %all-to-all-start) | async-done | bytes 2949152 | tf_op jit(solution)/shard_map/all_to_all | solution.py:188
  140.6 0.0 copy-start
  140.6 1.5 constant_dynamic-slice_fusion.1
  142.1 0.0 collective-permute-start
  142.1 0.8 fusion
  142.9 2.6 %collective-permute-start.1 = (bf16[10,48,384]{2,1,0:T(8,128)(2,1)}, bf16[10,48,384]{2,1,0:T(8,128)(2,1)S(1)}, u32[]{:S(2)}, u32[]{:S(2)}) collective-permute-start(bf16[10,48,384]{2,1,0:T(8,128)(2,1)} %fusion), channel_id=1, source_target_pairs={{16,0},{32,16},{48,32},{64,48},{80,64},{96,80},{112,96},{1,17},{17... | collective-permute-start | bytes 1105928 | tf_op jit(solution)/shard_map/ppermute | solution.py:193
  145.6 0.1 slice.12
  145.7 0.7 dynamic_slice.29
  146.3 0.0 copy-done.3
  146.3 0.6 reshape.10.gain
  146.9 0.0 copy-done.4
  146.9 0.6 reshape.11.bias
  147.5 7.2 %collective-permute-done.1.own_rim = bf16[10,48,384]{2,1,0:T(8,128)(2,1)S(1)} collective-permute-done((bf16[10,48,384]{2,1,0:T(8,128)(2,1)}, bf16[10,48,384]{2,1,0:T(8,128)(2,1)S(1)}, u32[]{:S(2)}, u32[]{:S(2)}) %collective-permute-start.1) | collective-permute-done | bytes 368672 | tf_op jit(solution)/shard_map/ppermute | solution.py:193
  154.7 0.0 copy-start.1
  154.7 0.8 constant_dynamic-slice_fusion
  155.4 0.0 collective-permute-start.2
  155.4 0.1 add_subtract_fusion
  155.5 0.6 dynamic_slice.26
  157.4 1.9 stack.12.plan
  159.3 0.0 collective-permute-done.2.other_rim
  159.3 0.0 copy-start.2
  159.3 0.0 collective-permute-done.other
  159.3 0.0 copy-done
  159.3 0.0 copy-done.1
  159.3 0.7 copy-done.2
  159.9 43.5 %shard_map.65 = bf16[4,16,48,384]{3,2,1,0:T(8,128)(2,1)} custom-call(s32[5]{0:T(128)} %stack.12.plan, bf16[8,10,48,384]{3,2,1,0:T(8,128)(2,1)} %copy-done, bf16[8,6,48,384]{3,2,1,0:T(8,128)(2,1)} %collective-permute-done.other, bf16[10,48,384]{2,1,0:T(8,128)(2,1)} %copy-done.1, bf16[6,48,384]{2,1,0:T(8,128)(2,1)} %copy-done.2, ...), custom_call_target="tpu_custom_call" | custom-call | tf_op jit(solution)/shard_map/pallas_call | solution.py:159
Async XLA Ops:
  92.4 8.1 %copy-start.6 = (s32[8]{0:T(128)S(1)}, s32[8]{0:T(128)}, u32[]{:S(2)}) copy-start(s32[8]{0:T(128)} %add_clamp_fusion.bases) | copy-start | bytes 100
  92.5 8.7 %copy-start.5 = (s32[16]{0:T(128)S(1)}, s32[16]{0:T(128)}, u32[]{:S(2)}) copy-start(s32[16]{0:T(128)} %param.7) | copy-start | bytes 196
  92.5 48.2 %all-to-all-start = ((bf16[8,10,48,384]{3,2,1,0:T(8,128)(2,1)}), bf16[8,10,48,384]{3,2,1,0:T(8,128)(2,1)S(1)}, u32[]{:S(2)}, u32[]{:S(2)}) async-start(bf16[8,10,48,384]{3,2,1,0:T(8,128)(2,1)} %shard_map.64), calls=%async_computation | async-start | bytes 5898240 | tf_op jit(solution)/shard_map/all_to_all | solution.py:188
  100.6 45.7 %copy-start.3 = (f32[384]{0:T(512)S(1)}, f32[384]{0:T(512)}, u32[]{:S(2)}) copy-start(f32[384]{0:T(512)} %param.8) | copy-start | bytes 4612
  100.6 46.3 %copy-start.4 = (f32[384]{0:T(512)S(1)}, f32[384]{0:T(512)}, u32[]{:S(2)}) copy-start(f32[384]{0:T(512)} %param.10) | copy-start | bytes 4612
  140.6 18.6 %copy-start = (bf16[8,10,48,384]{3,2,1,0:T(8,128)(2,1)}, bf16[8,10,48,384]{3,2,1,0:T(8,128)(2,1)S(1)}, u32[]{:S(2)}) copy-start(bf16[8,10,48,384]{3,2,1,0:T(8,128)(2,1)S(1)} %all-to-all-done.own) | copy-start | bytes 8847364
  142.1 17.1 %collective-permute-start = (bf16[8,6,48,384]{3,2,1,0:T(8,128)(2,1)}, bf16[8,6,48,384]{3,2,1,0:T(8,128)(2,1)}, u32[]{:S(2)}, u32[]{:S(2)}) collective-permute-start(bf16[8,6,48,384]{3,2,1,0:T(8,128)(2,1)} %constant_dynamic-slice_fusion.1), channel_id=1, source_target_pairs={{0,1},{1,0},{2,3},{3,2},{4,5},{5,4},{6,7},{7,6},{8,9},{9,8},{10,11... | collective-permute-start | bytes 5308424 | tf_op jit(solution)/shard_map/ppermute | solution.py:198
  142.9 11.7 %collective-permute-start.1 = (bf16[10,48,384]{2,1,0:T(8,128)(2,1)}, bf16[10,48,384]{2,1,0:T(8,128)(2,1)S(1)}, u32[]{:S(2)}, u32[]{:S(2)}) collective-permute-start(bf16[10,48,384]{2,1,0:T(8,128)(2,1)} %fusion), channel_id=1, source_target_pairs={{16,0},{32,16},{48,32},{64,48},{80,64},{96,80},{112,96},{1,17},{17... | collective-permute-start | bytes 1105928 | tf_op jit(solution)/shard_map/ppermute | solution.py:193
  154.7 4.6 %copy-start.1 = (bf16[10,48,384]{2,1,0:T(8,128)(2,1)}, bf16[10,48,384]{2,1,0:T(8,128)(2,1)S(1)}, u32[]{:S(2)}) copy-start(bf16[10,48,384]{2,1,0:T(8,128)(2,1)S(1)} %collective-permute-done.1.own_rim) | copy-start | bytes 1105924
  155.4 3.8 %collective-permute-start.2 = (bf16[6,48,384]{2,1,0:T(8,128)(2,1)}, bf16[6,48,384]{2,1,0:T(8,128)(2,1)S(1)}, u32[]{:S(2)}, u32[]{:S(2)}) collective-permute-start(bf16[6,48,384]{2,1,0:T(8,128)(2,1)} %constant_dynamic-slice_fusion), channel_id=1, source_target_pairs={{0,1},{1,0},{2,3},{3,2},{4,5},{5,4},{6,7},{7,6},{8,9},{9,8},{10,11... | collective-permute-start | bytes 663560 | tf_op jit(solution)/shard_map/ppermute | solution.py:201
  159.3 0.7 copy-start.2

commit v2 on v1

v2 whole, which is shorter than its diff:
```python
import functools

import jax
import jax.numpy as jnp
from jax import lax
from jax.experimental import pallas as pl
from jax.experimental.pallas import tpu as pltpu
from jax.sharding import Mesh, PartitionSpec as P

FMAX = 4
HIST = 2
SPAN = FMAX + HIST
VMEM_BYTES = 56 * 2**20


def activate(raw, gain):
    wide = raw.astype(jnp.float32)
    power = jnp.mean(wide * wide, axis=-1, keepdims=True)
    half = wide * lax.rsqrt(power + 1e-06) * (0.5 * gain)
    return (half + half * jnp.tanh(half)).astype(jnp.bfloat16)


def first_held(starts, group, odd, groups, total, slots):
    after = jnp.where(group + 1 < groups, starts[jnp.minimum(group + 1, groups - 1)], total)
    wanted = jnp.where(odd, after - slots, starts[group] - HIST)
    return jnp.clip(wanted, 0, total - slots)


def pack_kernel(starts, frames, packed, sems):
    groups, slots = packed.shape[:2]
    total = frames.shape[0]
    copies = []
    for group in range(groups):
        first = first_held(starts, group, group % 2 == 1, groups, total, slots)
        copies.append(
            pltpu.make_async_copy(frames.at[pl.ds(first, slots)], packed.at[group], sems.at[group])
        )
    for copy in copies:
        copy.start()
    for copy in copies:
        copy.wait()


def pack(starts, frames, slots):
    groups = starts.shape[0]
    return pl.pallas_call(
        pack_kernel,
        out_shape=jax.ShapeDtypeStruct((groups, slots) + frames.shape[1:], frames.dtype),
        in_specs=[
            pl.BlockSpec(memory_space=pltpu.SMEM),
            pl.BlockSpec(memory_space=pltpu.VMEM),
        ],
        out_specs=pl.BlockSpec(memory_space=pl.ANY),
        scratch_shapes=[pltpu.SemaphoreType.DMA((groups,))],
    )(starts, frames)


def tap_copies(weight, taps, sems):
    chans = weight.shape[-1]
    return [
        pltpu.make_async_copy(
            weight.at[a, b, e],
            taps.at[pl.ds((3 * a + b) * chans, chans), pl.ds(e * chans, chans)],
            sems.at[9 * a + 3 * b + e],
        )
        for a in range(3)
        for b in range(3)
        for e in range(3)
    ]


def place(starts, total, slots):
    groups = starts.shape[0]
    group = lax.axis_index("tc") * 2 + lax.axis_index("core")
    odd = lax.axis_index("core") == 1
    held = first_held(starts, group, odd, groups, total, slots)
    after = jnp.where(group + 1 < groups, starts[jnp.minimum(group + 1, groups - 1)], total)
    extra = jnp.where(odd, held - (SPAN - slots), held + slots)
    return group, starts[group], after - starts[group], held, extra


def locate(i, start, held, extra, slots):
    frame = start - HIST + i
    slot = frame - held
    inside = jnp.logical_and(slot >= 0, slot < slots)
    inside = jnp.logical_or(inside, frame < 0)
    return inside, jnp.clip(slot, 0, slots - 1), jnp.clip(frame - extra, 0, SPAN - slots - 1)


def column_sums(sums, cols):
    return (
        sums[0, :, 7 : cols + 7, :] + sums[1, :, 8 : cols + 8, :] + sums[2, :, 9 : cols + 9, :]
    )


def clear_sides(sums, cols):
    shape = (sums.shape[1], 1, sums.shape[3])
    sums[0, :, 7:8, :] = jnp.zeros(shape, jnp.float32)
    sums[2, :, cols + 8 : cols + 9, :] = jnp.zeros(shape, jnp.float32)


def inner_kernel(
    total, starts, own, other, weight, gain, bias, out,
    taps, raw, act, sums, result, weight_sems, frame_sems, out_sems,
):
    rows, slots, cols, chans = own.shape
    inner = rows - 2
    group, start, length, held, extra = place(starts, total, slots)
    weights = tap_copies(weight, taps, weight_sems)
    for i in range(SPAN):
        inside, slot, spare = locate(i, start, held, extra, slots)

        @pl.when(inside)
        def _():
            pltpu.make_async_copy(own.at[:, slot], raw.at[i], frame_sems.at[i]).start()

        @pl.when(jnp.logical_not(inside))
        def _():
            pltpu.make_async_copy(other.at[:, spare], raw.at[i], frame_sems.at[i]).start()

        if i == 2:
            for copy in weights:
                copy.start()

    def arrived(i):
        pltpu.make_async_copy(own.at[:, 0], raw.at[i], frame_sems.at[i]).wait()

    clear_sides(sums, cols)

    for i in range(3):
        arrived(i)
    act[2] = activate(raw[2], gain[...])

    @pl.when(group > 0)
    def _():
        act[0] = activate(raw[0], gain[...])
        act[1] = activate(raw[1], gain[...])

    @pl.when(group == 0)
    def _():
        act[0] = jnp.zeros(act.shape[1:], act.dtype)
        act[1] = jnp.zeros(act.shape[1:], act.dtype)

    for i in range(3, SPAN):
        arrived(i)
    for copy in weights:
        copy.wait()

    def one_frame(k, carry):
        lhs = jnp.concatenate(
            [
                act[k + a, pl.ds(b, inner)].reshape(inner * cols, chans)
                for a in range(3)
                for b in range(3)
            ],
            axis=1,
        )
        part = jnp.dot(lhs, taps[...], preferred_element_type=jnp.float32)
        for e in range(3):
            sums[e, :, 8 : cols + 8, :] = part[:, e * chans : (e + 1) * chans].reshape(
                inner, cols, chans
            )
        later = jnp.minimum(k + 3, SPAN - 1)
        act[later] = activate(raw[later], gain[...])
        latent = raw[k + HIST, pl.ds(1, inner)].astype(jnp.float32)
        result[k, pl.ds(1, inner)] = (latent + column_sums(sums, cols) + bias[...]).astype(
            result.dtype
        )
        pltpu.make_async_copy(result.at[k], out.at[k], out_sems.at[k]).start()
        return carry

    def blank_frame(k, carry):
        result[k] = jnp.zeros(result.shape[1:], result.dtype)
        pltpu.make_async_copy(result.at[k], out.at[k], out_sems.at[k]).start()
        return carry

    lax.fori_loop(length, FMAX, blank_frame, 0)
    lax.fori_loop(0, length, one_frame, 0)
    for k in range(FMAX):
        pltpu.make_async_copy(result.at[k], out.at[k], out_sems.at[k]).wait()


def edge_kernel(
    total, starts, own, other, above, below, weight, gain, bias, partial, out,
    taps, raw, act, sums, result, weight_sems, frame_sems, out_sems,
):
    del partial
    rows, slots, cols, chans = own.shape
    group, start, length, held, extra = place(starts, total, slots)
    weights = tap_copies(weight, taps, weight_sems)

    def copies(i, source, index, rim):
        return [
            pltpu.make_async_copy(above.at[rim], raw.at[i, 0, 0], frame_sems.at[i, 0]),
            pltpu.make_async_copy(
                source.at[pl.ds(0, 2), index], raw.at[i, 0, pl.ds(1, 2)], frame_sems.at[i, 1]
            ),
            pltpu.make_async_copy(
                source.at[pl.ds(rows - 2, 2), index], raw.at[i, 1, pl.ds(0, 2)], frame_sems.at[i, 2]
            ),
            pltpu.make_async_copy(below.at[rim], raw.at[i, 1, 2], frame_sems.at[i, 3]),
        ]

    for i in range(SPAN):
        inside, slot, spare = locate(i, start, held, extra, slots)

        @pl.when(inside)
        def _():
            for copy in copies(i, own, slot, slot):
                copy.start()

        @pl.when(jnp.logical_not(inside))
        def _():
            for copy in copies(i, other, spare, slots + spare):
                copy.start()

    for copy in weights:
        copy.start()
    clear_sides(sums, cols)
    for i in range(SPAN):
        for copy in copies(i, own, 0, 0):
            copy.wait()
        act[i] = activate(raw[i], gain[...])

    @pl.when(group == 0)
    def _():
        for i in range(HIST):
            act[i] = jnp.zeros(act.shape[1:], act.dtype)

    for copy in weights:
        copy.wait()
    lhs = jnp.concatenate(
        [
            act[a : a + FMAX, :, b].reshape(FMAX * 2 * cols, chans)
            for a in range(3)
            for b in range(3)
        ],
        axis=1,
    )
    part = jnp.dot(lhs, taps[...], preferred_element_type=jnp.float32)
    for e in range(3):
        sums[e, :, 8 : cols + 8, :] = part[:, e * chans : (e + 1) * chans].reshape(
            FMAX * 2, cols, chans
        )
    convolved = column_sums(sums, cols).reshape(FMAX, 2, cols, chans)
    for k in range(FMAX):
        for side in range(2):
            latent = raw[k + HIST, side, 1].astype(jnp.float32)
            total_sum = (latent + convolved[k, side] + bias[...]).astype(result.dtype)
            result[k, side] = jnp.where(k < length, total_sum, jnp.zeros_like(total_sum))
    finished = [
        pltpu.make_async_copy(
            result.at[k, side], out.at[k, side * (rows - 1)], out_sems.at[k, side]
        )
        for k in range(FMAX)
        for side in range(2)
    ]
    for copy in finished:
        copy.start()
    for copy in finished:
        copy.wait()


def inner_rows(total, starts, own, other, weight, gain, bias):
    rows, _, cols, chans = own.shape
    hbm = pl.BlockSpec(memory_space=pl.ANY)
    vmem = pl.BlockSpec(memory_space=pltpu.VMEM)
    return pl.pallas_call(
        functools.partial(inner_kernel, total),
        out_shape=jax.ShapeDtypeStruct((FMAX, rows, cols, chans), own.dtype),
        in_specs=[pl.BlockSpec(memory_space=pltpu.SMEM)] + [hbm] * 3 + [vmem] * 2,
        out_specs=hbm,
        scratch_shapes=[
            pltpu.VMEM((9 * chans, 3 * chans), jnp.bfloat16),
            pltpu.VMEM((SPAN, rows, cols, chans), jnp.bfloat16),
            pltpu.VMEM((SPAN, rows, cols, chans), jnp.bfloat16),
            pltpu.VMEM((3, rows - 2, cols + 16, chans), jnp.float32),
            pltpu.VMEM((FMAX, rows, cols, chans), jnp.bfloat16),
            pltpu.SemaphoreType.DMA((27,)),
            pltpu.SemaphoreType.DMA((SPAN,)),
            pltpu.SemaphoreType.DMA((FMAX,)),
        ],
        compiler_params=pltpu.CompilerParams(vmem_limit_bytes=VMEM_BYTES),
    )(starts, own, other, weight, gain, bias)


def edge_rows(total, starts, own, other, above, below, weight, gain, bias, partial):
    rows, _, cols, chans = own.shape
    hbm = pl.BlockSpec(memory_space=pl.ANY)
    vmem = pl.BlockSpec(memory_space=pltpu.VMEM)
    return pl.pallas_call(
        functools.partial(edge_kernel, total),
        out_shape=jax.ShapeDtypeStruct(partial.shape, partial.dtype),
        in_specs=[pl.BlockSpec(memory_space=pltpu.SMEM)] + [hbm] * 5 + [vmem] * 2 + [hbm],
        out_specs=hbm,
        scratch_shapes=[
            pltpu.VMEM((9 * chans, 3 * chans), jnp.bfloat16),
            pltpu.VMEM((SPAN, 2, 3, cols, chans), jnp.bfloat16),
            pltpu.VMEM((SPAN, 2, 3, cols, chans), jnp.bfloat16),
            pltpu.VMEM((3, 2 * FMAX, cols + 16, chans), jnp.float32),
            pltpu.VMEM((FMAX, 2, cols, chans), jnp.bfloat16),
            pltpu.SemaphoreType.DMA((27,)),
            pltpu.SemaphoreType.DMA((SPAN, 4)),
            pltpu.SemaphoreType.DMA((FMAX, 2)),
        ],
        input_output_aliases={8: 0},
        compiler_params=pltpu.CompilerParams(vmem_limit_bytes=VMEM_BYTES),
    )(starts, own, other, above, below, weight, gain, bias, partial)


def on_device(slots, latent, group_start, norm_gain, conv_weight, conv_bias):
    total = latent.shape[0]
    groups = group_start.shape[0]
    missing = SPAN - slots
    stripes = lax.axis_size("ha")
    core = lax.axis_index("core")
    chip = lax.axis_index("tc")
    gain = norm_gain.reshape(1, -1)
    bias = conv_bias.reshape(1, -1)
    packed = pack(group_start, latent[:, 0], slots)
    own = lax.all_to_all(packed, ("tc", "core"), split_axis=0, concat_axis=0, tiled=True)

    front = first_held(group_start, 2 * chip, False, groups, total, slots)
    back = first_held(group_start, 2 * chip + 1, True, groups, total, slots)
    wanted = jnp.where(core == 0, back - missing - front, front + slots - back)
    sent = lax.dynamic_slice_in_dim(own, jnp.clip(wanted, 0, slots - missing), missing, 1)
    other = lax.ppermute(sent, "core", [(0, 1), (1, 0)])

    up = [(h, h + 1) for h in range(stripes - 1)]
    down = [(h + 1, h) for h in range(stripes - 1)]
    above = lax.ppermute(jnp.concatenate([own[-1], other[-1]], axis=0), "ha", up)
    below = lax.ppermute(jnp.concatenate([own[0], other[0]], axis=0), "ha", down)
    partial = inner_rows(total, group_start, own, other, conv_weight, gain, bias)
    return edge_rows(
        total, group_start, own, other, above, below, conv_weight, gain, bias, partial
    )


def solution(mesh):
    devices = mesh.devices
    fine = Mesh(
        devices.reshape(devices.shape[0], devices.shape[1] // 2, 2), ("ha", "tc", "core")
    )
    placed = (P(None, ("ha", "tc", "core"), None, None), P(), P(), P(), P())
    return jax.shard_map(
        functools.partial(on_device, 5),
        mesh=fine,
        in_specs=placed,
        out_specs=P(("tc", "core"), "ha", None, None),
        check_vma=False,
    )
```

time: 204 us -> 105 us (0.51)
  the two profiles are of different devices: /device:TPU:30 before, /device:TPU:39 now
where the time goes in v2:
time: 105 us; the launch traced here: 104 us
  Pallas kernels  45.9 us (44%)
  waiting for transfers between devices  37.2 us (35%)
  starting transfers between devices  15.9 us (15%)
  local copies, waits for them, and re-layouts  3.26 us (3%)
  between operations  1.38 us (1%)
    all_to_all x1, waiting for transfers between devices, on_device(): lax.all_to_all(packed, ('tc', 'core'), split_axis=0, concat_axis=0, tiled...  35.6 us
    pallas_call x1, Pallas kernels, inner_rows(): pl.pallas_call(functools.partial(inner_kernel, total), out_shape=jax.Shap...  33.5 us
    pallas_call x1, Pallas kernels, edge_rows(): pl.pallas_call(functools.partial(edge_kernel, total), out_shape=jax.Shape...  9.45 us
    all_to_all x1, starting transfers between devices, on_device(): lax.all_to_all(packed, ('tc', 'core'), split_axis=0, concat_axis=0, tiled...  7.54 us
    ppermute x1, starting transfers between devices, on_device(): lax.ppermute(jnp.concatenate([own[0], other[0]], axis=0), 'ha', down)  4.19 us
    ppermute x1, starting transfers between devices, on_device(): lax.ppermute(jnp.concatenate([own[-1], other[-1]], axis=0), 'ha', up)  3.2 us
    pallas_call x1, Pallas kernels, pack(): pl.pallas_call(pack_kernel, out_shape=jax.ShapeDtypeStruct((groups, slots...  3.02 us
  transfers between devices with their start and end apart: 4, of which 2 were waited for; matrix products, arithmetic and copies ran while one was open for 2% of the time, Pallas kernels for 32%

profile of v2, /device:TPU:39, one launch (start us, length us, event | category | flops | bytes accessed | tf_op | source)
XLA Modules:
  0.0 103.7 jit_solution(6725704038109773802)
XLA Ops:
  0.0 3.0 %shard_map.55 = bf16[16,5,48,384]{3,2,1,0:T(8,128)(2,1)} custom-call(s32[16]{0:T(128)} %starts.5, bf16[32,48,384]{2,1,0:T(8,128)(2,1)} %bitcast.11), custom_call_target="tpu_custom_call" | custom-call | tf_op jit(solution)/shard_map/pallas_call | solution.py:46
  3.0 0.0 copy-start.4
  3.0 7.5 %all-to-all-start = ((bf16[16,5,48,384]{3,2,1,0:T(8,128)(2,1)}), bf16[16,5,48,384]{3,2,1,0:T(8,128)(2,1)S(1)}, u32[]{:S(2)}, u32[]{:S(2)}) async-start(bf16[16,5,48,384]{3,2,1,0:T(8,128)(2,1)} %shard_map.55), calls=%async_computation | async-start | bytes 5898240 | tf_op jit(solution)/shard_map/all_to_all | solution.py:321
  10.6 0.0 copy-start.5
  10.6 0.0 copy-start.6
  10.6 0.0 copy-done.4
  10.6 0.6 fusion
  12.5 35.6 %all-to-all-done.own = bf16[16,5,48,384]{3,2,1,0:T(8,128)(2,1)S(1)} async-done(((bf16[16,5,48,384]{3,2,1,0:T(8,128)(2,1)}), bf16[16,5,48,384]{3,2,1,0:T(8,128)(2,1)S(1)}, u32[]{:S(2)}, u32[]{:S(2)}) %all-to-all-start) | async-done | bytes 2949152 | tf_op jit(solution)/shard_map/all_to_all | solution.py:321
  48.1 0.0 copy-start
  48.1 0.1 constant_dynamic-slice_fusion
  48.1 0.9 collective-permute-start
  49.1 1.6 %collective-permute-done.other = bf16[16,1,48,384]{3,2,1,0:T(8,128)(2,1)S(1)} collective-permute-done((bf16[16,1,48,384]{3,2,1,0:T(8,128)(2,1)S(1)}, bf16[16,1,48,384]{3,2,1,0:T(8,128)(2,1)S(1)}, u32[]{:S(2)}, u32[]{:S(2)}) %collective-permute-start) | collective-permute-done | bytes 589856 | tf_op jit(solution)/shard_map/ppermute | solution.py:327
  50.7 0.0 copy-start.1
  50.8 3.2 %collective-permute-start.1 = (bf16[6,48,384]{2,1,0:T(8,128)(2,1)S(1)}, bf16[6,48,384]{2,1,0:T(8,128)(2,1)S(1)}, u32[]{:S(2)}, u32[]{:S(2)}) collective-permute-start(bf16[6,48,384]{2,1,0:T(8,128)(2,1)S(1)} %pad_maximum_fusion), channel_id=1, source_target_pairs={{0,16},{16,32},{32,48},{48,64},{64,80},{80,96},{96,112},{1,17},{17... | collective-permute-start | bytes 663560 | tf_op jit(solution)/shard_map/ppermute | solution.py:331
  54.0 4.2 %collective-permute-start.2 = (bf16[6,48,384]{2,1,0:T(8,128)(2,1)S(1)}, bf16[6,48,384]{2,1,0:T(8,128)(2,1)S(1)}, u32[]{:S(2)}, u32[]{:S(2)}) collective-permute-start(bf16[6,48,384]{2,1,0:T(8,128)(2,1)S(1)} %pad_maximum_fusion.1), channel_id=1, source_target_pairs={{16,0},{32,16},{48,32},{64,48},{80,64},{96,80},{112,96},{17,1},{33... | collective-permute-start | bytes 663560 | tf_op jit(solution)/shard_map/ppermute | solution.py:332
  58.2 0.0 copy-done.5
  58.2 0.6 reshape.12.gain
  58.8 0.0 copy-done.6
  58.8 0.6 reshape.13.bias
  59.4 0.0 copy-done
  59.4 0.0 copy-done.1
  59.4 33.5 %shard_map.56.partial = bf16[4,16,48,384]{3,2,1,0:T(8,128)(2,1)} custom-call(s32[16]{0:T(128)} %starts.5, bf16[16,5,48,384]{3,2,1,0:T(8,128)(2,1)} %copy-done, bf16[16,1,48,384]{3,2,1,0:T(8,128)(2,1)} %copy-done.1, bf16[3,3,3,384,384]{4,3,2,1,0:T(8,128)(2,1)} %weight.3, f32[1,384]{1,0:T(1,128)} %reshape.12.gain, f32[1,384]{1,0:T(1,128)} %reshape.13.bias), custom_call_target="tpu_custom_call" | custom-call | tf_op jit(solution)/shard_map/pallas_call | solution.py:268
  92.9 0.0 collective-permute-done.1.above
  92.9 0.0 copy-start.2
  92.9 0.0 collective-permute-done.2.below
  92.9 0.7 copy-done.2
  93.6 0.0 copy-start.3
  93.6 0.7 copy-done.3
  94.3 9.4 %shard_map.57 = bf16[4,16,48,384]{3,2,1,0:T(8,128)(2,1)} custom-call(s32[16]{0:T(128)} %starts.5, bf16[16,5,48,384]{3,2,1,0:T(8,128)(2,1)} %copy-done, bf16[16,1,48,384]{3,2,1,0:T(8,128)(2,1)} %copy-done.1, bf16[6,48,384]{2,1,0:T(8,128)(2,1)} %copy-done.2, bf16[6,48,384]{2,1,0:T(8,128)(2,1)} %copy-done.3, ...), custom_call_target="tpu_custom_call", output_to_operand_aliasing={{}: (8, {})} | custom-call | tf_op jit(solution)/shard_map/pallas_call | solution.py:291
  (4 shorter events, 0.1 us)
Async XLA Ops:
  3.0 7.6 %copy-start.4 = (s32[16]{0:T(128)S(1)}, s32[16]{0:T(128)}, u32[]{:S(2)}) copy-start(s32[16]{0:T(128)} %starts.5) | copy-start | bytes 196
  3.0 45.0 %all-to-all-start = ((bf16[16,5,48,384]{3,2,1,0:T(8,128)(2,1)}), bf16[16,5,48,384]{3,2,1,0:T(8,128)(2,1)S(1)}, u32[]{:S(2)}, u32[]{:S(2)}) async-start(bf16[16,5,48,384]{3,2,1,0:T(8,128)(2,1)} %shard_map.55), calls=%async_computation | async-start | bytes 5898240 | tf_op jit(solution)/shard_map/all_to_all | solution.py:321
  10.6 47.6 %copy-start.5 = (f32[384]{0:T(512)S(1)}, f32[384]{0:T(512)}, u32[]{:S(2)}) copy-start(f32[384]{0:T(512)} %param.7) | copy-start | bytes 4612
  10.6 48.2 %copy-start.6 = (f32[384]{0:T(512)S(1)}, f32[384]{0:T(512)}, u32[]{:S(2)}) copy-start(f32[384]{0:T(512)} %param.9) | copy-start | bytes 4612
  48.1 11.3 %copy-start = (bf16[16,5,48,384]{3,2,1,0:T(8,128)(2,1)}, bf16[16,5,48,384]{3,2,1,0:T(8,128)(2,1)S(1)}, u32[]{:S(2)}) copy-start(bf16[16,5,48,384]{3,2,1,0:T(8,128)(2,1)S(1)} %all-to-all-done.own) | copy-start | bytes 8847364
  48.1 2.6 %collective-permute-start = (bf16[16,1,48,384]{3,2,1,0:T(8,128)(2,1)S(1)}, bf16[16,1,48,384]{3,2,1,0:T(8,128)(2,1)S(1)}, u32[]{:S(2)}, u32[]{:S(2)}) collective-permute-start(bf16[16,1,48,384]{3,2,1,0:T(8,128)(2,1)S(1)} %constant_dynamic-slice_fusion), channel_id=1, source_target_pairs={{0,1},{1,0},{2,3},{3,2},{4,5},{5,4},{6,7},{7,6},{8,9},{9,8},{10,11... | collective-permute-start | bytes 1769480 | tf_op jit(solution)/shard_map/ppermute | solution.py:327
  50.7 8.7 %copy-start.1 = (bf16[16,1,48,384]{3,2,1,0:T(8,128)(2,1)}, bf16[16,1,48,384]{3,2,1,0:T(8,128)(2,1)S(1)}, u32[]{:S(2)}) copy-start(bf16[16,1,48,384]{3,2,1,0:T(8,128)(2,1)S(1)} %collective-permute-done.other) | copy-start | bytes 1769476
  50.8 42.1 %collective-permute-start.1 = (bf16[6,48,384]{2,1,0:T(8,128)(2,1)S(1)}, bf16[6,48,384]{2,1,0:T(8,128)(2,1)S(1)}, u32[]{:S(2)}, u32[]{:S(2)}) collective-permute-start(bf16[6,48,384]{2,1,0:T(8,128)(2,1)S(1)} %pad_maximum_fusion), channel_id=1, source_target_pairs={{0,16},{16,32},{32,48},{48,64},{64,80},{80,96},{96,112},{1,17},{17... | collective-permute-start | bytes 663560 | tf_op jit(solution)/shard_map/ppermute | solution.py:331
  54.0 38.9 %collective-permute-start.2 = (bf16[6,48,384]{2,1,0:T(8,128)(2,1)S(1)}, bf16[6,48,384]{2,1,0:T(8,128)(2,1)S(1)}, u32[]{:S(2)}, u32[]{:S(2)}) collective-permute-start(bf16[6,48,384]{2,1,0:T(8,128)(2,1)S(1)} %pad_maximum_fusion.1), channel_id=1, source_target_pairs={{16,0},{32,16},{48,32},{64,48},{80,64},{96,80},{112,96},{17,1},{33... | collective-permute-start | bytes 663560 | tf_op jit(solution)/shard_map/ppermute | solution.py:332
  92.9 0.7 copy-start.2
  93.6 0.7 copy-start.3

commit v3 on v2

--- a/solution.py
+++ b/solution.py
@@ -10,7 +10,7 @@
 FMAX = 4
 HIST = 2
 SPAN = FMAX + HIST
-VMEM_BYTES = 56 * 2**20
+VMEM_BYTES = 30 * 2**20
 
 
 def activate(raw, gain):
@@ -55,18 +55,15 @@
     )(starts, frames)
 
 
-def tap_copies(weight, taps, sems):
-    chans = weight.shape[-1]
-    return [
-        pltpu.make_async_copy(
-            weight.at[a, b, e],
-            taps.at[pl.ds((3 * a + b) * chans, chans), pl.ds(e * chans, chans)],
-            sems.at[9 * a + 3 * b + e],
-        )
-        for a in range(3)
-        for b in range(3)
-        for e in range(3)
-    ]
+def all_taps(weight):
+    return jnp.concatenate(
+        [
+            jnp.concatenate([weight[a, b, e] for e in range(3)], axis=1)
+            for a in range(3)
+            for b in range(3)
+        ],
+        axis=0,
+    )
 
 
 def place(starts, total, slots):
@@ -101,12 +98,11 @@
 
 def inner_kernel(
     total, starts, own, other, weight, gain, bias, out,
-    taps, raw, act, sums, result, weight_sems, frame_sems, out_sems,
+    raw, act, sums, result, frame_sems, out_sems,
 ):
     rows, slots, cols, chans = own.shape
     inner = rows - 2
     group, start, length, held, extra = place(starts, total, slots)
-    weights = tap_copies(weight, taps, weight_sems)
     for i in range(SPAN):
         inside, slot, spare = locate(i, start, held, extra, slots)
 
@@ -117,10 +113,6 @@
         @pl.when(jnp.logical_not(inside))
         def _():
             pltpu.make_async_copy(other.at[:, spare], raw.at[i], frame_sems.at[i]).start()
-
-        if i == 2:
-            for copy in weights:
-                copy.start()
 
     def arrived(i):
         pltpu.make_async_copy(own.at[:, 0], raw.at[i], frame_sems.at[i]).wait()
@@ -143,8 +135,6 @@
 
     for i in range(3, SPAN):
         arrived(i)
-    for copy in weights:
-        copy.wait()
 
     def one_frame(k, carry):
         lhs = jnp.concatenate(
@@ -155,7 +145,7 @@
             ],
             axis=1,
         )
-        part = jnp.dot(lhs, taps[...], preferred_element_type=jnp.float32)
+        part = jnp.dot(lhs, all_taps(weight), preferred_element_type=jnp.float32)
         for e in range(3):
             sums[e, :, 8 : cols + 8, :] = part[:, e * chans : (e + 1) * chans].reshape(
                 inner, cols, chans
@@ -182,12 +172,11 @@
 
 def edge_kernel(
     total, starts, own, other, above, below, weight, gain, bias, partial, out,
-    taps, raw, act, sums, result, weight_sems, frame_sems, out_sems,
+    raw, act, sums, result, frame_sems, out_sems,
 ):
     del partial
     rows, slots, cols, chans = own.shape
     group, start, length, held, extra = place(starts, total, slots)
-    weights = tap_copies(weight, taps, weight_sems)
 
     def copies(i, source, index, rim):
         return [
@@ -214,8 +203,6 @@
             for copy in copies(i, other, spare, slots + spare):
                 copy.start()
 
-    for copy in weights:
-        copy.start()
     clear_sides(sums, cols)
     for i in range(SPAN):
         for copy in copies(i, own, 0, 0):
@@ -227,8 +214,6 @@
         for i in range(HIST):
             act[i] = jnp.zeros(act.shape[1:], act.dtype)
 
-    for copy in weights:
-        copy.wait()
     lhs = jnp.concatenate(
         [
             act[a : a + FMAX, :, b].reshape(FMAX * 2 * cols, chans)
@@ -237,7 +222,7 @@
         ],
         axis=1,
     )
-    part = jnp.dot(lhs, taps[...], preferred_element_type=jnp.float32)
+    part = jnp.dot(lhs, all_taps(weight), preferred_element_type=jnp.float32)
     for e in range(3):
         sums[e, :, 8 : cols + 8, :] = part[:, e * chans : (e + 1) * chans].reshape(
             FMAX * 2, cols, chans
@@ -263,20 +248,18 @@
 
 def inner_rows(total, starts, own, other, weight, gain, bias):
     rows, _, cols, chans = own.shape
-    hbm = pl.BlockSpec(memory_space=pl.ANY)
+    hbm = pl.BlockSpec(memory_space=pltpu.HBM)
     vmem = pl.BlockSpec(memory_space=pltpu.VMEM)
     return pl.pallas_call(
         functools.partial(inner_kernel, total),
         out_shape=jax.ShapeDtypeStruct((FMAX, rows, cols, chans), own.dtype),
-        in_specs=[pl.BlockSpec(memory_space=pltpu.SMEM)] + [hbm] * 3 + [vmem] * 2,
+        in_specs=[pl.BlockSpec(memory_space=pltpu.SMEM)] + [hbm] * 2 + [vmem] * 3,
         out_specs=hbm,
         scratch_shapes=[
-            pltpu.VMEM((9 * chans, 3 * chans), jnp.bfloat16),
             pltpu.VMEM((SPAN, rows, cols, chans), jnp.bfloat16),
             pltpu.VMEM((SPAN, rows, cols, chans), jnp.bfloat16),
             pltpu.VMEM((3, rows - 2, cols + 16, chans), jnp.float32),
             pltpu.VMEM((FMAX, rows, cols, chans), jnp.bfloat16),
-            pltpu.SemaphoreType.DMA((27,)),
             pltpu.SemaphoreType.DMA((SPAN,)),
             pltpu.SemaphoreType.DMA((FMAX,)),
         ],
@@ -286,20 +269,18 @@
 
 def edge_rows(total, starts, own, other, above, below, weight, gain, bias, partial):
     rows, _, cols, chans = own.shape
-    hbm = pl.BlockSpec(memory_space=pl.ANY)
+    hbm = pl.BlockSpec(memory_space=pltpu.HBM)
     vmem = pl.BlockSpec(memory_space=pltpu.VMEM)
     return pl.pallas_call(
         functools.partial(edge_kernel, total),
         out_shape=jax.ShapeDtypeStruct(partial.shape, partial.dtype),
-        in_specs=[pl.BlockSpec(memory_space=pltpu.SMEM)] + [hbm] * 5 + [vmem] * 2 + [hbm],
+        in_specs=[pl.BlockSpec(memory_space=pltpu.SMEM)] + [hbm] * 4 + [vmem] * 3 + [hbm],
         out_specs=hbm,
         scratch_shapes=[
-            pltpu.VMEM((9 * chans, 3 * chans), jnp.bfloat16),
             pltpu.VMEM((SPAN, 2, 3, cols, chans), jnp.bfloat16),
             pltpu.VMEM((SPAN, 2, 3, cols, chans), jnp.bfloat16),
             pltpu.VMEM((3, 2 * FMAX, cols + 16, chans), jnp.float32),
             pltpu.VMEM((FMAX, 2, cols, chans), jnp.bfloat16),
-            pltpu.SemaphoreType.DMA((27,)),
             pltpu.SemaphoreType.DMA((SPAN, 4)),
             pltpu.SemaphoreType.DMA((FMAX, 2)),
         ],
@@ -308,15 +289,13 @@
     )(starts, own, other, above, below, weight, gain, bias, partial)
 
 
-def on_device(slots, latent, group_start, norm_gain, conv_weight, conv_bias):
+def with_slots(slots, latent, group_start, gain, conv_weight, bias):
     total = latent.shape[0]
     groups = group_start.shape[0]
     missing = SPAN - slots
     stripes = lax.axis_size("ha")
     core = lax.axis_index("core")
     chip = lax.axis_index("tc")
-    gain = norm_gain.reshape(1, -1)
-    bias = conv_bias.reshape(1, -1)
     packed = pack(group_start, latent[:, 0], slots)
     own = lax.all_to_all(packed, ("tc", "core"), split_axis=0, concat_axis=0, tiled=True)
 
@@ -336,6 +315,18 @@
     )
 
 
+def on_device(latent, group_start, norm_gain, conv_weight, conv_bias):
+    cores = lax.axis_size("core")
+    chip_starts = jnp.append(group_start[::cores], latent.shape[0])
+    most = jnp.max(chip_starts[1:] - chip_starts[:-1])
+    return lax.cond(
+        most <= 2 * (FMAX - 1),
+        functools.partial(with_slots, FMAX),
+        functools.partial(with_slots, FMAX + 1),
+        latent, group_start, norm_gain.reshape(1, -1), conv_weight, conv_bias.reshape(1, -1),
+    )
+
+
 def solution(mesh):
     devices = mesh.devices
     fine = Mesh(
@@ -343,7 +334,7 @@
     )
     placed = (P(None, ("ha", "tc", "core"), None, None), P(), P(), P(), P())
     return jax.shard_map(
-        functools.partial(on_device, 5),
+        on_device,
         mesh=fine,
         in_specs=placed,
         out_specs=P(("tc", "core"), "ha", None, None),

time: 105 us -> 94.2 us (0.90)
  the two profiles are of different devices: /device:TPU:39 before, /device:TPU:99 now
where the time goes in v3:
time: 94.2 us; the launch traced here: 92.6 us
  Pallas kernels  43.6 us (46%)
  waiting for transfers between devices  28.2 us (30%)
  starting transfers between devices  15.8 us (17%)
  loops' own time  1.69 us (2%)
  local copies, waits for them, and re-layouts  1.57 us (2%)
    pallas_call x1, Pallas kernels, inner_rows(): pl.pallas_call(functools.partial(inner_kernel, total), out_shape=jax.Shap...  33.1 us
    all_to_all x1, waiting for transfers between devices, with_slots(): lax.all_to_all(packed, ('tc', 'core'), split_axis=0, concat_axis=0, tiled...  25.7 us
    pallas_call x1, Pallas kernels, edge_rows(): pl.pallas_call(functools.partial(edge_kernel, total), out_shape=jax.Shape...  7.7 us
    all_to_all x1, starting transfers between devices, with_slots(): lax.all_to_all(packed, ('tc', 'core'), split_axis=0, concat_axis=0, tiled...  7.58 us
    ppermute x1, starting transfers between devices, with_slots(): lax.ppermute(jnp.concatenate([own[0], other[0]], axis=0), 'ha', down)  4.19 us
    ppermute x1, starting transfers between devices, with_slots(): lax.ppermute(jnp.concatenate([own[-1], other[-1]], axis=0), 'ha', up)  3.47 us
    pallas_call x1, Pallas kernels, pack(): pl.pallas_call(pack_kernel, out_shape=jax.ShapeDtypeStruct((groups, slots...  2.82 us
    ppermute x1, waiting for transfers between devices, with_slots(): other = lax.ppermute(sent, 'core', [(0, 1), (1, 0)])  2.44 us
  transfers between devices with their start and end apart: 4, of which 2 were waited for; matrix products, arithmetic and copies ran while one was open for 1% of the time, Pallas kernels for 36%

profile of v3, /device:TPU:99, one launch (start us, length us, event | category | flops | bytes accessed | tf_op | source)
XLA Modules:
  0.0 92.6 jit_solution(1673982793584423023)
XLA Ops:
  0.0 0.7 slice.31
  0.7 0.1 pad_add_fusion
  0.8 0.7 subtract_reduce_fusion
  2.2 90.2 %conditional.1 = (bf16[4,16,48,384]{3,2,1,0:T(8,128)(2,1)}) conditional(s32[]{:T(128)} %convert_element_type.3, (bf16[32,1,48,384]{3,2,1,0:T(8,128)(2,1)}, s32[16]{0:T(128)}, bf16[3,3,3,384,384]{4,3,2,1,0:T(8,128)(2,1)}, f32[384]{0:T(512)}, f32[384]{0:T(512)}) %tuple.11, (bf16[32,1,48,384]{3,2,1,0:T(8,128)(2,1)}, s32[16]{0:T(128)}, ...), branch_computations={%region_1.2_spmd, %region_2.3_spmd} | conditional | flops 221214 | bytes 41601944 | solution.py:322
  2.2 2.8 %branch_1_fun.3 = bf16[16,4,48,384]{3,2,1,0:T(8,128)(2,1)} custom-call(s32[16]{0:T(128)} %get-tuple-element.33.starts, bf16[32,48,384]{2,1,0:T(8,128)(2,1)} %bitcast.29), custom_call_target="tpu_custom_call" | custom-call | tf_op jit(solution)/shard_map/cond/branch_1_fun/pallas_call | solution.py:46
  5.0 0.0 copy-start.1
  5.0 7.6 %all-to-all-start.1 = ((bf16[16,4,48,384]{3,2,1,0:T(8,128)(2,1)}), bf16[16,4,48,384]{3,2,1,0:T(8,128)(2,1)S(1)}, u32[]{:S(2)}, u32[]{:S(2)}) async-start(bf16[16,4,48,384]{3,2,1,0:T(8,128)(2,1)} %branch_1_fun.3), calls=%async_computation.1 | async-start | bytes 4718592 | tf_op jit(solution)/shard_map/cond/branch_1_fun/all_to_all | solution.py:300
  12.6 0.0 copy-start.5
  12.6 0.0 copy-start.3
  12.7 0.0 copy-done.1
  12.7 0.6 fusion.1
  14.6 25.7 %all-to-all-done.1.own = bf16[16,4,48,384]{3,2,1,0:T(8,128)(2,1)S(1)} async-done(((bf16[16,4,48,384]{3,2,1,0:T(8,128)(2,1)}), bf16[16,4,48,384]{3,2,1,0:T(8,128)(2,1)S(1)}, u32[]{:S(2)}, u32[]{:S(2)}) %all-to-all-start.1) | async-done | bytes 2359328 | tf_op jit(solution)/shard_map/cond/branch_1_fun/all_to_all | solution.py:300
  40.3 0.1 constant_dynamic-slice_fusion.1
  40.4 0.6 collective-permute-start.3
  41.0 2.4 %collective-permute-done.3.other = bf16[16,2,48,384]{3,2,1,0:T(8,128)(2,1)S(1)} collective-permute-done((bf16[16,2,48,384]{3,2,1,0:T(8,128)(2,1)S(1)}, bf16[16,2,48,384]{3,2,1,0:T(8,128)(2,1)S(1)}, u32[]{:S(2)}, u32[]{:S(2)}) %collective-permute-start.3) | collective-permute-done | bytes 1179680 | tf_op jit(solution)/shard_map/cond/branch_1_fun/ppermute | solution.py:306
  43.5 0.0 slice-start.2
  43.5 3.5 %collective-permute-start.4 = (bf16[6,48,384]{2,1,0:T(8,128)(2,1)S(1)}, bf16[6,48,384]{2,1,0:T(8,128)(2,1)S(1)}, u32[]{:S(2)}, u32[]{:S(2)}) collective-permute-start(bf16[6,48,384]{2,1,0:T(8,128)(2,1)S(1)} %pad_maximum_fusion.2), channel_id=1, source_target_pairs={{0,16},{16,32},{32,48},{48,64},{64,80},{80,96},{96,112},{1,17},{17... | collective-permute-start | bytes 663560 | tf_op jit(solution)/shard_map/cond/branch_1_fun/ppermute | solution.py:310
  47.1 4.2 %collective-permute-start.5 = (bf16[6,48,384]{2,1,0:T(8,128)(2,1)S(1)}, bf16[6,48,384]{2,1,0:T(8,128)(2,1)S(1)}, u32[]{:S(2)}, u32[]{:S(2)}) collective-permute-start(bf16[6,48,384]{2,1,0:T(8,128)(2,1)S(1)} %pad_maximum_fusion.3), channel_id=1, source_target_pairs={{16,0},{32,16},{48,32},{64,48},{80,64},{96,80},{112,96},{17,1},{33... | collective-permute-start | bytes 663560 | tf_op jit(solution)/shard_map/cond/branch_1_fun/ppermute | solution.py:311
  51.2 0.0 copy-done.5
  51.3 0.0 copy-done.3
  51.3 0.0 slice-start.3
  51.3 33.1 %branch_1_fun.4.partial = bf16[4,16,48,384]{3,2,1,0:T(8,128)(2,1)} custom-call(s32[16]{0:T(128)S(1)} %copy-done.1, bf16[16,4,48,384]{3,2,1,0:T(8,128)(2,1)S(1)} %all-to-all-done.1.own, bf16[16,2,48,384]{3,2,1,0:T(8,128)(2,1)S(1)} %collective-permute-done.3.other, bf16[3,3,3,384,384]{4,3,2,1,0:T(8,128)(2,1)} %get-tuple-element.50.weight, ...), custom_call_target="tpu_custom_call" | custom-call | tf_op jit(solution)/shard_map/cond/branch_1_fun/pallas_call | solution.py:253
  84.4 0.0 collective-permute-done.4.above
  84.4 0.0 collective-permute-done.5.below
  84.4 0.0 slice-done.2
  84.4 0.0 slice-done.3
  84.5 7.7 %branch_1_fun.5 = bf16[4,16,48,384]{3,2,1,0:T(8,128)(2,1)} custom-call(s32[16]{0:T(128)S(1)} %copy-done.1, bf16[16,4,48,384]{3,2,1,0:T(8,128)(2,1)S(1)} %all-to-all-done.1.own, bf16[16,2,48,384]{3,2,1,0:T(8,128)(2,1)S(1)} %collective-permute-done.3.other, bf16[6,48,384]{2,1,0:T(8,128)(2,1)S(1)} %collective-permute-done.4.above, ...), custom_call_target="tpu_custom_call", output_to_operand_aliasing={{}: (8, {})} | custom-call | tf_op jit(solution)/shard_map/cond/branch_1_fun/pallas_call | solution.py:274
  (7 shorter events, 0.1 us)
Async XLA Ops:
  5.0 7.6 %copy-start.1 = (s32[16]{0:T(128)S(1)}, s32[16]{0:T(128)}, u32[]{:S(2)}) copy-start(s32[16]{0:T(128)} %get-tuple-element.33.starts) | copy-start | bytes 196 | tf_op jit(solution)/shard_map/cond
  5.0 35.2 %all-to-all-start.1 = ((bf16[16,4,48,384]{3,2,1,0:T(8,128)(2,1)}), bf16[16,4,48,384]{3,2,1,0:T(8,128)(2,1)S(1)}, u32[]{:S(2)}, u32[]{:S(2)}) async-start(bf16[16,4,48,384]{3,2,1,0:T(8,128)(2,1)} %branch_1_fun.3), calls=%async_computation.1 | async-start | bytes 4718592 | tf_op jit(solution)/shard_map/cond/branch_1_fun/all_to_all | solution.py:300
  12.6 38.6 %copy-start.5 = (f32[384]{0:T(512)S(1)}, f32[384]{0:T(512)}, u32[]{:S(2)}) copy-start(f32[384]{0:T(512)} %get-tuple-element.58) | copy-start | bytes 4612 | tf_op jit(solution)/shard_map/cond
  12.6 38.6 %copy-start.3 = (f32[384]{0:T(512)S(1)}, f32[384]{0:T(512)}, u32[]{:S(2)}) copy-start(f32[384]{0:T(512)} %get-tuple-element.56) | copy-start | bytes 4612 | tf_op jit(solution)/shard_map/cond
  40.4 3.1 %collective-permute-start.3 = (bf16[16,2,48,384]{3,2,1,0:T(8,128)(2,1)S(1)}, bf16[16,2,48,384]{3,2,1,0:T(8,128)(2,1)S(1)}, u32[]{:S(2)}, u32[]{:S(2)}) collective-permute-start(bf16[16,2,48,384]{3,2,1,0:T(8,128)(2,1)S(1)} %constant_dynamic-slice_fusion.1), channel_id=1, source_target_pairs={{0,1},{1,0},{2,3},{3,2},{4,5},{5,4},{6,7},{7,6},{8,9},{9,8},{10,11... | collective-permute-start | bytes 3538952 | tf_op jit(solution)/shard_map/cond/branch_1_fun/ppermute | solution.py:306
  43.5 40.9 %slice-start.2 = ((s8[7962624]{0:T(1024)(128)(4,1)}), s8[4194304]{0:T(1024)(128)(4,1)S(1)}, s32[]{:S(2)}) async-start(s8[7962624]{0:T(1024)(128)(4,1)} %bitcast.26), calls=%async_computation.4 | async-start | bytes 8388608 | tf_op jit(solution)/shard_map/cond
  43.5 40.9 %collective-permute-start.4 = (bf16[6,48,384]{2,1,0:T(8,128)(2,1)S(1)}, bf16[6,48,384]{2,1,0:T(8,128)(2,1)S(1)}, u32[]{:S(2)}, u32[]{:S(2)}) collective-permute-start(bf16[6,48,384]{2,1,0:T(8,128)(2,1)S(1)} %pad_maximum_fusion.2), channel_id=1, source_target_pairs={{0,16},{16,32},{32,48},{48,64},{64,80},{80,96},{96,112},{1,17},{17... | collective-permute-start | bytes 663560 | tf_op jit(solution)/shard_map/cond/branch_1_fun/ppermute | solution.py:310
  47.1 37.4 %collective-permute-start.5 = (bf16[6,48,384]{2,1,0:T(8,128)(2,1)S(1)}, bf16[6,48,384]{2,1,0:T(8,128)(2,1)S(1)}, u32[]{:S(2)}, u32[]{:S(2)}) collective-permute-start(bf16[6,48,384]{2,1,0:T(8,128)(2,1)S(1)} %pad_maximum_fusion.3), channel_id=1, source_target_pairs={{16,0},{32,16},{48,32},{64,48},{80,64},{96,80},{112,96},{17,1},{33... | collective-permute-start | bytes 663560 | tf_op jit(solution)/shard_map/cond/branch_1_fun/ppermute | solution.py:311
  51.3 33.2 %slice-start.3 = ((s8[7962624]{0:T(1024)(128)(4,1)}), s8[3768320]{0:T(1024)(128)(4,1)S(1)}, s32[]{:S(2)}) async-start(s8[7962624]{0:T(1024)(128)(4,1)} %bitcast.26), calls=%async_computation.5 | async-start | bytes 7536640 | tf_op jit(solution)/shard_map/cond

commit v4 on v3

--- a/solution.py
+++ b/solution.py
@@ -11,6 +11,7 @@
 HIST = 2
 SPAN = FMAX + HIST
 VMEM_BYTES = 30 * 2**20
+EDGE_VMEM_BYTES = 50 * 2**20
 
 
 def activate(raw, gain):
@@ -171,12 +172,17 @@
 
 
 def edge_kernel(
-    total, starts, own, other, above, below, weight, gain, bias, partial, out,
+    total, starts, own, other, rims, weight, gain, bias, partial, out,
     raw, act, sums, result, frame_sems, out_sems,
 ):
     del partial
     rows, slots, cols, chans = own.shape
     group, start, length, held, extra = place(starts, total, slots)
+
+    stripes = rims.shape[0]
+    stripe = lax.axis_index("ha")
+    above = rims.at[jnp.maximum(stripe - 1, 0), 1]
+    below = rims.at[jnp.minimum(stripe + 1, stripes - 1), 0]
 
     def copies(i, source, index, rim):
         return [
@@ -213,6 +219,13 @@
     def _():
         for i in range(HIST):
             act[i] = jnp.zeros(act.shape[1:], act.dtype)
+
+    for side, last in ((0, 0), (1, stripes - 1)):
+
+        @pl.when(stripe == last)
+        def _():
+            for i in range(SPAN):
+                act[i, side, 2 * side] = jnp.zeros(act.shape[3:], act.dtype)
 
     lhs = jnp.concatenate(
         [
@@ -267,14 +280,14 @@
     )(starts, own, other, weight, gain, bias)
 
 
-def edge_rows(total, starts, own, other, above, below, weight, gain, bias, partial):
+def edge_rows(total, starts, own, other, rims, weight, gain, bias, partial):
     rows, _, cols, chans = own.shape
     hbm = pl.BlockSpec(memory_space=pltpu.HBM)
     vmem = pl.BlockSpec(memory_space=pltpu.VMEM)
     return pl.pallas_call(
         functools.partial(edge_kernel, total),
         out_shape=jax.ShapeDtypeStruct(partial.shape, partial.dtype),
-        in_specs=[pl.BlockSpec(memory_space=pltpu.SMEM)] + [hbm] * 4 + [vmem] * 3 + [hbm],
+        in_specs=[pl.BlockSpec(memory_space=pltpu.SMEM)] + [hbm] * 3 + [vmem] * 3 + [hbm],
         out_specs=hbm,
         scratch_shapes=[
             pltpu.VMEM((SPAN, 2, 3, cols, chans), jnp.bfloat16),
@@ -284,16 +297,15 @@
             pltpu.SemaphoreType.DMA((SPAN, 4)),
             pltpu.SemaphoreType.DMA((FMAX, 2)),
         ],
-        input_output_aliases={8: 0},
-        compiler_params=pltpu.CompilerParams(vmem_limit_bytes=VMEM_BYTES),
-    )(starts, own, other, above, below, weight, gain, bias, partial)
+        input_output_aliases={7: 0},
+        compiler_params=pltpu.CompilerParams(vmem_limit_bytes=EDGE_VMEM_BYTES),
+    )(starts, own, other, rims, weight, gain, bias, partial)
 
 
 def with_slots(slots, latent, group_start, gain, conv_weight, bias):
     total = latent.shape[0]
     groups = group_start.shape[0]
     missing = SPAN - slots
-    stripes = lax.axis_size("ha")
     core = lax.axis_index("core")
     chip = lax.axis_index("tc")
     packed = pack(group_start, latent[:, 0], slots)
@@ -305,13 +317,16 @@
     sent = lax.dynamic_slice_in_dim(own, jnp.clip(wanted, 0, slots - missing), missing, 1)
     other = lax.ppermute(sent, "core", [(0, 1), (1, 0)])
 
-    up = [(h, h + 1) for h in range(stripes - 1)]
-    down = [(h + 1, h) for h in range(stripes - 1)]
-    above = lax.ppermute(jnp.concatenate([own[-1], other[-1]], axis=0), "ha", up)
-    below = lax.ppermute(jnp.concatenate([own[0], other[0]], axis=0), "ha", down)
+    rim = jnp.stack(
+        [
+            jnp.concatenate([own[0], other[0]], axis=0),
+            jnp.concatenate([own[-1], other[-1]], axis=0),
+        ]
+    )
+    rims = lax.all_gather(rim, "ha", axis=0)
     partial = inner_rows(total, group_start, own, other, conv_weight, gain, bias)
     return edge_rows(
-        total, group_start, own, other, above, below, conv_weight, gain, bias, partial
+        total, group_start, own, other, rims, conv_weight, gain, bias, partial
     )
 
 

time: 94.2 us -> 121 us (1.28)
  the two profiles are of different devices: /device:TPU:99 before, /device:TPU:1 now
where the time goes in v4:
time: 121 us; the launch traced here: 120 us
  waiting for transfers between devices  65.4 us (54%)
  Pallas kernels  25.5 us (21%)
  between operations  14.1 us (12%)
  starting transfers between devices  10.4 us (9%)
  other arithmetic  1.66 us (1%)
  loops' own time  1.65 us (1%)
  local copies, waits for them, and re-layouts  1.6 us (1%)
    all_gather x1, waiting for transfers between devices, with_slots(): rims = lax.all_gather(rim, 'ha', axis=0)  33.9 us
    all_to_all x1, waiting for transfers between devices, with_slots(): lax.all_to_all(packed, ('tc', 'core'), split_axis=0, concat_axis=0, tiled...  29 us
    pallas_call x1, Pallas kernels, inner_rows(): pl.pallas_call(functools.partial(inner_kernel, total), out_shape=jax.Shap...  12.6 us
    pallas_call x1, Pallas kernels, edge_rows(): pl.pallas_call(functools.partial(edge_kernel, total), out_shape=jax.Shape...  10.1 us
    all_to_all x1, starting transfers between devices, with_slots(): lax.all_to_all(packed, ('tc', 'core'), split_axis=0, concat_axis=0, tiled...  9.14 us
    pallas_call x1, Pallas kernels, pack(): pl.pallas_call(pack_kernel, out_shape=jax.ShapeDtypeStruct((groups, slots...  2.82 us
    ppermute x1, waiting for transfers between devices, with_slots(): other = lax.ppermute(sent, 'core', [(0, 1), (1, 0)])  2.44 us
  transfers between devices with their start and end apart: 3, of which 3 were waited for; matrix products, arithmetic and copies ran while one was open for 1% of the time, Pallas kernels for 11%

profile of v4, /device:TPU:1, one launch (start us, length us, event | category | flops | bytes accessed | tf_op | source)
XLA Modules:
  0.0 120.3 jit_solution(12803833396447426679)
XLA Ops:
  6.5 0.7 slice.31
  7.3 0.1 pad_add_fusion
  7.4 0.7 subtract_reduce_fusion
  8.7 104.7 %conditional.1 = (bf16[4,16,48,384]{3,2,1,0:T(8,128)(2,1)}) conditional(s32[]{:T(128)} %convert_element_type.3, (bf16[32,1,48,384]{3,2,1,0:T(8,128)(2,1)}, s32[16]{0:T(128)}, bf16[3,3,3,384,384]{4,3,2,1,0:T(8,128)(2,1)}, f32[384]{0:T(512)}, f32[384]{0:T(512)}) %tuple.11, (bf16[32,1,48,384]{3,2,1,0:T(8,128)(2,1)}, s32[16]{0:T(128)}, ...), branch_computations={%region_1.2_spmd, %region_2.3_spmd} | conditional | flops 442398 | bytes 28773184 | solution.py:337
  8.7 2.8 %branch_1_fun.3 = bf16[16,4,48,384]{3,2,1,0:T(8,128)(2,1)} custom-call(s32[16]{0:T(128)} %get-tuple-element.33.starts, bf16[32,48,384]{2,1,0:T(8,128)(2,1)} %bitcast.35), custom_call_target="tpu_custom_call" | custom-call | tf_op jit(solution)/shard_map/cond/branch_1_fun/pallas_call | solution.py:47
  11.6 0.0 copy-start.1
  11.6 9.1 %all-to-all-start.1 = ((bf16[16,4,48,384]{3,2,1,0:T(8,128)(2,1)}), bf16[16,4,48,384]{3,2,1,0:T(8,128)(2,1)S(1)}, u32[]{:S(2)}, u32[]{:S(2)}) async-start(bf16[16,4,48,384]{3,2,1,0:T(8,128)(2,1)} %branch_1_fun.3), calls=%async_computation.1 | async-start | bytes 4718592 | tf_op jit(solution)/shard_map/cond/branch_1_fun/all_to_all | solution.py:312
  20.7 0.2 all-gather.7.cloned.1.call-start
  21.0 0.0 copy-done.1
  21.0 0.7 fusion.1
  22.9 0.0 copy-start.5
  22.9 0.0 copy-start.3
  22.9 29.0 %all-to-all-done.1.own = bf16[16,4,48,384]{3,2,1,0:T(8,128)(2,1)S(1)} async-done(((bf16[16,4,48,384]{3,2,1,0:T(8,128)(2,1)}), bf16[16,4,48,384]{3,2,1,0:T(8,128)(2,1)S(1)}, u32[]{:S(2)}, u32[]{:S(2)}) %all-to-all-start.1) | async-done | bytes 2359328 | tf_op jit(solution)/shard_map/cond/branch_1_fun/all_to_all | solution.py:312
  52.0 0.1 constant_dynamic-slice_fusion.1
  52.1 1.0 collective-permute-start.1
  53.1 2.4 %collective-permute-done.1.other = bf16[16,2,48,384]{3,2,1,0:T(8,128)(2,1)S(1)} collective-permute-done((bf16[16,2,48,384]{3,2,1,0:T(8,128)(2,1)S(1)}, bf16[16,2,48,384]{3,2,1,0:T(8,128)(2,1)S(1)}, u32[]{:S(2)}, u32[]{:S(2)}) %collective-permute-start.1) | collective-permute-done | bytes 1179680 | tf_op jit(solution)/shard_map/cond/branch_1_fun/ppermute | solution.py:318
  55.6 0.1 maximum_bitcast_fusion.2
  55.6 0.8 pad_maximum_fusion.1
  56.5 0.0 all-gather.7.cloned.1.call-update
  56.5 0.0 copy-done.5
  56.5 0.0 copy-done.3
  56.5 12.6 %branch_1_fun.4.partial = bf16[4,16,48,384]{3,2,1,0:T(8,128)(2,1)} custom-call(s32[16]{0:T(128)S(1)} %copy-done.1, bf16[16,4,48,384]{3,2,1,0:T(8,128)(2,1)S(1)} %all-to-all-done.1.own, bf16[16,2,48,384]{3,2,1,0:T(8,128)(2,1)S(1)} %collective-permute-done.1.other, bf16[3,3,3,384,384]{4,3,2,1,0:T(8,128)(2,1)} %get-tuple-element.50.weight, ...), custom_call_target="tpu_custom_call" | custom-call | tf_op jit(solution)/shard_map/cond/branch_1_fun/pallas_call | solution.py:266
  69.2 33.9 %all-gather.7.cloned.1.call-done = bf16[16,6,48,384]{3,2,1,0:T(8,128)(2,1)} async-done(((bf16[2,6,48,384]{3,2,1,0:T(8,128)(2,1)}), bf16[16,6,48,384]{3,2,1,0:T(8,128)(2,1)}) %all-gather.7.cloned.1.call-update) | async-done | bytes 3538960 | tf_op jit(solution)/shard_map/cond/branch_1_fun/all_gather | solution.py:326
  103.1 10.1 %branch_1_fun.5 = bf16[4,16,48,384]{3,2,1,0:T(8,128)(2,1)} custom-call(s32[16]{0:T(128)S(1)} %copy-done.1, bf16[16,4,48,384]{3,2,1,0:T(8,128)(2,1)S(1)} %all-to-all-done.1.own, bf16[16,2,48,384]{3,2,1,0:T(8,128)(2,1)S(1)} %collective-permute-done.1.other, bf16[8,2,6,48,384]{4,3,2,1,0:T(8,128)(2,1)} %bitcast.37, ...), custom_call_target="tpu_custom_call", output_to_operand_aliasing={{}: (7, {})} | custom-call | tf_op jit(solution)/shard_map/cond/branch_1_fun/pallas_call | solution.py:287
  (4 shorter events, 0.1 us)
Async XLA Ops:
  11.6 9.4 %copy-start.1 = (s32[16]{0:T(128)S(1)}, s32[16]{0:T(128)}, u32[]{:S(2)}) copy-start(s32[16]{0:T(128)} %get-tuple-element.33.starts) | copy-start | bytes 196 | tf_op jit(solution)/shard_map/cond
  11.6 40.4 %all-to-all-start.1 = ((bf16[16,4,48,384]{3,2,1,0:T(8,128)(2,1)}), bf16[16,4,48,384]{3,2,1,0:T(8,128)(2,1)S(1)}, u32[]{:S(2)}, u32[]{:S(2)}) async-start(bf16[16,4,48,384]{3,2,1,0:T(8,128)(2,1)} %branch_1_fun.3), calls=%async_computation.1 | async-start | bytes 4718592 | tf_op jit(solution)/shard_map/cond/branch_1_fun/all_to_all | solution.py:312
  20.7 82.4 %all-gather.7.cloned.1.call-start = ((), (), s32[]{:S(2)}) async-start(), calls=%async_computation.3 | async-start | bytes 3981312 | tf_op jit(solution)/shard_map/cond/branch_1_fun/all_gather | solution.py:326
  22.9 33.6 %copy-start.5 = (f32[384]{0:T(512)S(1)}, f32[384]{0:T(512)}, u32[]{:S(2)}) copy-start(f32[384]{0:T(512)} %get-tuple-element.58) | copy-start | bytes 4612 | tf_op jit(solution)/shard_map/cond
  22.9 33.6 %copy-start.3 = (f32[384]{0:T(512)S(1)}, f32[384]{0:T(512)}, u32[]{:S(2)}) copy-start(f32[384]{0:T(512)} %get-tuple-element.56) | copy-start | bytes 4612 | tf_op jit(solution)/shard_map/cond
  52.1 3.5 %collective-permute-start.1 = (bf16[16,2,48,384]{3,2,1,0:T(8,128)(2,1)S(1)}, bf16[16,2,48,384]{3,2,1,0:T(8,128)(2,1)S(1)}, u32[]{:S(2)}, u32[]{:S(2)}) collective-permute-start(bf16[16,2,48,384]{3,2,1,0:T(8,128)(2,1)S(1)} %constant_dynamic-slice_fusion.1), channel_id=1, source_target_pairs={{0,1},{1,0},{2,3},{3,2},{4,5},{5,4},{6,7},{7,6},{8,9},{9,8},{10,11... | collective-permute-start | bytes 3538952 | tf_op jit(solution)/shard_map/cond/branch_1_fun/ppermute | solution.py:318
Sparse Core Ops, SparseCore 0:
  56.6 46.4 all-gather.6

commit v5 on v0

v5 whole, which is shorter than its diff:
```python
import functools

import jax
import jax.numpy as jnp
from jax import lax
from jax.experimental import pallas as pl
from jax.experimental.pallas import tpu as pltpu
from jax.sharding import Mesh, PartitionSpec as P

FMAX = 4
HIST = 2
STEP = 8
VMEM_BYTES = 30 * 2**20
SMEM_SPEC = pl.BlockSpec(memory_space=pltpu.SMEM)
VMEM_SPEC = pl.BlockSpec(memory_space=pltpu.VMEM)
HBM_SPEC = pl.BlockSpec(memory_space=pltpu.HBM)


def activate(raw, gain):
    wide = raw.astype(jnp.float32)
    power = jnp.mean(wide * wide, axis=-1, keepdims=True)
    half = wide * lax.rsqrt(power + 1e-06) * (0.5 * gain)
    return (half + half * jnp.tanh(half)).astype(jnp.bfloat16)


def taps_of(weight, row_taps):
    return jnp.concatenate(
        [
            jnp.concatenate([weight[a, b, e] for e in range(3)], axis=1)
            for b in row_taps
            for a in range(3)
        ],
        axis=0,
    )


def convolve(acts, first, count, weight, row_taps, sums):
    cols, chans = acts[0].shape[1:]
    lhs = jnp.concatenate(
        [
            act[pl.ds(first + a, count)].reshape(count * cols, chans)
            for act in acts
            for a in range(3)
        ],
        axis=1,
    )
    part = jnp.dot(lhs, taps_of(weight, row_taps), preferred_element_type=jnp.float32)
    for e in range(3):
        sums[e, pl.ds(0, count), 8 : cols + 8, :] = part[:, e * chans : (e + 1) * chans].reshape(
            count, cols, chans
        )
    return (
        sums[0, pl.ds(0, count), 7 : cols + 7, :]
        + sums[1, pl.ds(0, count), 8 : cols + 8, :]
        + sums[2, pl.ds(0, count), 9 : cols + 9, :]
    )


def clear_sides(sums, cols):
    shape = (sums.shape[1], 1, sums.shape[3])
    sums[0, :, 7:8, :] = jnp.zeros(shape, jnp.float32)
    sums[2, :, cols + 8 : cols + 9, :] = jnp.zeros(shape, jnp.float32)


def near_kernel(own, twin, weight, gain, bias, partial, own_act, twin_act, sums):
    total, cols, _ = own.shape
    core = lax.axis_index("core")
    clear_sides(sums, cols)
    for act in (own_act, twin_act):
        act[pl.ds(0, HIST)] = jnp.zeros((HIST,) + act.shape[1:], act.dtype)

    def prepare(i, carry):
        frames = pl.ds(i * STEP, STEP)
        later = pl.ds(i * STEP + HIST, STEP)
        own_act[later] = activate(own[frames], gain[...])
        twin_act[later] = activate(twin[frames], gain[...])
        return carry

    lax.fori_loop(0, total // STEP, prepare, 0)

    def step(i, carry):
        frames = pl.ds(i * STEP, STEP)
        convolved = convolve(
            (own_act, twin_act), i * STEP, STEP, weight, (1, 2 * (1 - core)), sums
        )
        partial[frames] = own[frames].astype(jnp.float32) + convolved + bias[...]
        return carry

    lax.fori_loop(0, total // STEP, step, 0)


def near_rows(own, twin, weight, gain, bias):
    total, cols, chans = own.shape
    return pl.pallas_call(
        near_kernel,
        out_shape=jax.ShapeDtypeStruct(own.shape, jnp.float32),
        in_specs=[VMEM_SPEC] * 5,
        out_specs=VMEM_SPEC,
        scratch_shapes=[
            pltpu.VMEM((HIST + total, cols, chans), jnp.bfloat16),
            pltpu.VMEM((HIST + total, cols, chans), jnp.bfloat16),
            pltpu.VMEM((3, STEP, cols + 16, chans), jnp.float32),
        ],
        compiler_params=pltpu.CompilerParams(vmem_limit_bytes=VMEM_BYTES),
    )(own, twin, weight, gain, bias)


def far_frames(begin, far, recent, partial, weight, gain, act, sums):
    count, cols, chans = far.shape
    core = lax.axis_index("core")
    row = lax.axis_index("ha") * lax.axis_size("tc") + lax.axis_index("tc")
    row = row * lax.axis_size("core") + core
    rows = lax.axis_size("ha") * lax.axis_size("tc") * lax.axis_size("core")
    clear_sides(sums, cols)
    if recent is None:
        act[pl.ds(0, HIST)] = jnp.zeros((HIST, cols, chans), act.dtype)
    else:
        act[pl.ds(0, HIST)] = activate(recent[pl.ds(recent.shape[0] - HIST, HIST)], gain[...])
    act[pl.ds(HIST, count)] = activate(far[...], gain[...])

    @pl.when(jnp.logical_or(row == 0, row == rows - 1))
    def _():
        act[...] = jnp.zeros(act.shape, act.dtype)

    convolved = convolve((act,), 0, count, weight, (2 * core,), sums)
    return (partial[pl.ds(begin, count)] + convolved).astype(jnp.bfloat16)


def early_kernel(far, partial, weight, gain, out, act, sums):
    out[...] = far_frames(0, far, None, partial, weight, gain, act, sums)


def late_kernel(starts, early_far, far, early, partial, weight, gain, packed,
                act, sums, result, early_sem, sems):
    cut = early.shape[0]
    count, cols, chans = far.shape
    groups = packed.shape[0]
    copy = pltpu.make_async_copy(early, result.at[pl.ds(0, cut)], early_sem)
    copy.start()
    result[pl.ds(cut + count, FMAX)] = jnp.zeros((FMAX, cols, chans), result.dtype)
    result[pl.ds(cut, count)] = far_frames(
        cut, far, early_far, partial, weight, gain, act, sums
    )
    copy.wait()
    copies = [
        pltpu.make_async_copy(
            result.at[pl.ds(jnp.clip(starts[j], 0, cut + count), FMAX)], packed.at[j], sems.at[j]
        )
        for j in range(groups)
    ]
    for copy in copies:
        copy.start()
    for copy in copies:
        copy.wait()


def far_scratch(count, cols, chans):
    return [
        pltpu.VMEM((HIST + count, cols, chans), jnp.bfloat16),
        pltpu.VMEM((3, count, cols + 16, chans), jnp.float32),
    ]


def early_rows(far, partial, weight, gain):
    return pl.pallas_call(
        early_kernel,
        out_shape=jax.ShapeDtypeStruct(far.shape, jnp.bfloat16),
        in_specs=[VMEM_SPEC] * 4,
        out_specs=VMEM_SPEC,
        scratch_shapes=far_scratch(*far.shape),
        compiler_params=pltpu.CompilerParams(vmem_limit_bytes=VMEM_BYTES),
    )(far, partial, weight, gain)


def late_rows(starts, early_far, far, early, partial, weight, gain):
    groups = starts.shape[0]
    total, cols, chans = partial.shape
    return pl.pallas_call(
        late_kernel,
        out_shape=jax.ShapeDtypeStruct((groups, FMAX, cols, chans), jnp.bfloat16),
        in_specs=[SMEM_SPEC] + [VMEM_SPEC] * 6,
        out_specs=HBM_SPEC,
        scratch_shapes=far_scratch(*far.shape)
        + [
            pltpu.VMEM((total + FMAX, cols, chans), jnp.bfloat16),
            pltpu.SemaphoreType.DMA,
            pltpu.SemaphoreType.DMA((groups,)),
        ],
        compiler_params=pltpu.CompilerParams(vmem_limit_bytes=VMEM_BYTES),
    )(starts, early_far, far, early, partial, weight, gain)


def unpack_kernel(total, starts, arrived, out, blank, sems):
    groups = starts.shape[0]
    group = lax.axis_index("tc") * lax.axis_size("core") + lax.axis_index("core")
    after = jnp.where(group + 1 < groups, starts[jnp.minimum(group + 1, groups - 1)], total)
    length = after - starts[group]
    blank[...] = jnp.zeros(blank.shape, blank.dtype)
    for k in range(FMAX):

        @pl.when(k < length)
        def _():
            pltpu.make_async_copy(arrived.at[:, k], out.at[k], sems.at[k]).start()

        @pl.when(k >= length)
        def _():
            pltpu.make_async_copy(blank, out.at[k], sems.at[k]).start()

    for k in range(FMAX):
        pltpu.make_async_copy(blank, out.at[k], sems.at[k]).wait()


def unpack(total, starts, arrived):
    rows, _, cols, chans = arrived.shape
    return pl.pallas_call(
        functools.partial(unpack_kernel, total),
        out_shape=jax.ShapeDtypeStruct((FMAX, rows, cols, chans), arrived.dtype),
        in_specs=[SMEM_SPEC, VMEM_SPEC],
        out_specs=HBM_SPEC,
        scratch_shapes=[
            pltpu.VMEM((rows, cols, chans), arrived.dtype),
            pltpu.SemaphoreType.DMA((FMAX,)),
        ],
    )(starts, arrived)


def on_device(latent, group_start, norm_gain, conv_weight, conv_bias):
    total = latent.shape[0]
    own = latent[:, 0]
    rows = lax.axis_size("ha") * lax.axis_size("tc") * lax.axis_size("core")
    gain = norm_gain.reshape(1, -1)
    bias = conv_bias.reshape(1, -1)
    pairs = [(r, (r + 1) % rows if r % 2 else (r - 1) % rows) for r in range(rows)]
    cut = total * 5 // 8
    early_far = lax.ppermute(own[:cut], ("ha", "tc", "core"), pairs)
    late_far = lax.ppermute(own[cut:], ("ha", "tc", "core"), pairs)
    twin = lax.ppermute(own, "core", [(0, 1), (1, 0)])
    partial = near_rows(own, twin, conv_weight, gain, bias)
    early = early_rows(early_far, partial, conv_weight, gain)
    packed = late_rows(group_start, early_far, late_far, early, partial, conv_weight, gain)
    arrived = lax.all_to_all(packed, ("tc", "core"), split_axis=0, concat_axis=0, tiled=True)
    return unpack(total, group_start, arrived)


def solution(mesh):
    devices = mesh.devices
    fine = Mesh(
        devices.reshape(devices.shape[0], devices.shape[1] // 2, 2), ("ha", "tc", "core")
    )
    placed = (P(None, ("ha", "tc", "core"), None, None), P(), P(), P(), P())
    return jax.shard_map(
        on_device,
        mesh=fine,
        in_specs=placed,
        out_specs=P(("tc", "core"), "ha", None, None),
        check_vma=False,
    )
```

time: 252 us -> 81.6 us (0.32)
  the two profiles are of different devices: /device:TPU:89 before, /device:TPU:1 now
where the time goes in v5:
time: 81.6 us; the launch traced here: 81.3 us
  blocking collectives  38.7 us (47%)
  Pallas kernels  25.4 us (31%)
  waiting for transfers between devices  6.29 us (8%)
  local copies, waits for them, and re-layouts  5.53 us (7%)
  starting transfers between devices  5.34 us (7%)
    all_to_all x1, blocking collectives, on_device(): lax.all_to_all(packed, ('tc', 'core'), split_axis=0, concat_axis=0, tiled...  38.7 us
    pallas_call x1, Pallas kernels, near_rows(): pl.pallas_call(near_kernel, out_shape=jax.ShapeDtypeStruct(own.shape, jnp...  11.8 us
    pallas_call x1, Pallas kernels, late_rows(): pl.pallas_call(late_kernel, out_shape=jax.ShapeDtypeStruct((groups, FMAX,...  6.56 us
    ppermute x1, waiting for transfers between devices, on_device(): early_far = lax.ppermute(own[:cut], ('ha', 'tc', 'core'), pairs)  4.78 us
    pallas_call x1, Pallas kernels, early_rows(): pl.pallas_call(early_kernel, out_shape=jax.ShapeDtypeStruct(far.shape, jn...  3.96 us
    ppermute x1, starting transfers between devices, on_device(): early_far = lax.ppermute(own[:cut], ('ha', 'tc', 'core'), pairs)  3.82 us
    unnamed x12, local copies, waits for them, and re-layouts  3.28 us
    pallas_call x1, Pallas kernels, unpack(): pl.pallas_call(functools.partial(unpack_kernel, total), out_shape=jax.Sha...  3.12 us
  transfers between devices with their start and end apart: 3, of which 2 were waited for; matrix products, arithmetic and copies ran while one was open for 3% of the time, Pallas kernels for 19%

profile of v5, /device:TPU:1, one launch (start us, length us, event | category | flops | bytes accessed | tf_op | source)
XLA Modules:
  0.0 81.3 jit_solution(17693578737803662610)
XLA Ops:
  0.0 0.0 copy-start.2
  0.0 0.0 copy-start.4
  0.0 0.0 copy-start.5
  0.0 1.4 %collective-permute-start.2 = (bf16[32,48,384]{2,1,0:T(8,128)(2,1)}, bf16[32,48,384]{2,1,0:T(8,128)(2,1)S(1)}, u32[]{:S(2)}, u32[]{:S(2)}) collective-permute-start(bf16[32,48,384]{2,1,0:T(8,128)(2,1)} %bitcast.6), channel_id=1, source_target_pairs={{0,1},{1,0},{2,3},{3,2},{4,5},{5,4},{6,7},{7,6},{8,9},{9,8},{10,11... | collective-permute-start | bytes 3538952 | tf_op jit(solution)/shard_map/ppermute | solution.py:237
  1.4 1.2 %slice_bitcast_fusion = bf16[20,48,384]{2,1,0:T(8,128)(2,1)S(1)} fusion(bf16[32,1,48,384]{3,2,0,1:T(8,128)(2,1)} %bitcast.7), kind=kLoop, calls=%fused_computation | loop fusion | bytes 1474560 | tf_op jit(solution)/shard_map/slice | solution.py:235
  2.6 3.8 %collective-permute-start = (bf16[20,48,384]{2,1,0:T(8,128)(2,1)S(1)}, bf16[20,48,384]{2,1,0:T(8,128)(2,1)S(1)}, u32[]{:S(2)}, u32[]{:S(2)}) collective-permute-start(bf16[20,48,384]{2,1,0:T(8,128)(2,1)S(1)} %slice_bitcast_fusion), channel_id=1, source_target_pairs={{0,127},{1,2},{2,1},{3,4},{4,3},{5,6},{6,5},{7,8},{8,7},{9,10},{10... | collective-permute-start | bytes 2211848 | tf_op jit(solution)/shard_map/ppermute | solution.py:235
  6.4 1.1 %slice_bitcast_fusion.1 = bf16[12,48,384]{2,1,0:T(8,128)(2,1)S(1)} fusion(bf16[32,1,48,384]{3,2,0,1:T(8,128)(2,1)} %bitcast.8), kind=kLoop, calls=%fused_computation.1 | loop fusion | bytes 884736 | tf_op jit(solution)/shard_map/slice | solution.py:236
  7.5 0.1 collective-permute-start.1
  7.6 0.0 copy-done.4
  7.6 0.0 copy-done.5
  7.6 0.0 collective-permute-done.2.twin
  7.7 0.0 copy-done.2
  7.7 0.0 copy-start
  7.7 3.3 %copy-done = bf16[3,3,3,384,384]{4,3,2,1,0:T(8,128)(2,1)S(1)} copy-done((bf16[3,3,3,384,384]{4,3,2,1,0:T(8,128)(2,1)S(1)}, bf16[3,3,3,384,384]{4,3,2,1,0:T(8,128)(2,1)}, u32[]{:S(2)}) %copy-start) | copy-done | bytes 7962648
  10.9 0.0 copy-start.1
  10.9 11.8 %shard_map.55.partial = f32[32,48,384]{2,1,0:T(8,128)S(1)} custom-call(bf16[32,48,384]{2,1,0:T(8,128)(2,1)S(1)} %bitcast.9, bf16[32,48,384]{2,1,0:T(8,128)(2,1)S(1)} %collective-permute-done.2.twin, bf16[3,3,3,384,384]{4,3,2,1,0:T(8,128)(2,1)S(1)} %copy-done, f32[1,384]{1,0:T(1,128)S(1)} %reshape.8.gain, f32[1,384]{1,0:T(1,128)S(1)} %reshape.9.bias), custom_call_target="tpu_custom_call" | custom-call | tf_op jit(solution)/shard_map/pallas_call | solution.py:94
  22.7 0.0 copy-start.3
  22.7 4.8 %collective-permute-done.far.early_far = bf16[20,48,384]{2,1,0:T(8,128)(2,1)S(1)} collective-permute-done((bf16[20,48,384]{2,1,0:T(8,128)(2,1)S(1)}, bf16[20,48,384]{2,1,0:T(8,128)(2,1)S(1)}, u32[]{:S(2)}, u32[]{:S(2)}) %collective-permute-start) | collective-permute-done | bytes 737312 | tf_op jit(solution)/shard_map/ppermute | solution.py:235
  27.5 0.0 copy-done.1
  27.5 4.0 %shard_map.56.early = bf16[20,48,384]{2,1,0:T(8,128)(2,1)S(1)} custom-call(bf16[20,48,384]{2,1,0:T(8,128)(2,1)S(1)} %collective-permute-done.far.early_far, f32[32,48,384]{2,1,0:T(8,128)S(1)} %shard_map.55.partial, bf16[3,3,3,384,384]{4,3,2,1,0:T(8,128)(2,1)S(1)} %copy-done.1, f32[1,384]{1,0:T(1,128)S(1)} %reshape.8.gain), custom_call_target="tpu_custom_call" | custom-call | tf_op jit(solution)/shard_map/pallas_call | solution.py:165
  31.5 1.5 %collective-permute-done.1.far = bf16[12,48,384]{2,1,0:T(8,128)(2,1)S(1)} collective-permute-done((bf16[12,48,384]{2,1,0:T(8,128)(2,1)S(1)}, bf16[12,48,384]{2,1,0:T(8,128)(2,1)S(1)}, u32[]{:S(2)}, u32[]{:S(2)}) %collective-permute-start.1) | collective-permute-done | bytes 442400 | tf_op jit(solution)/shard_map/ppermute | solution.py:236
  33.0 0.0 copy-done.3
  33.0 6.6 %shard_map.57 = bf16[16,4,48,384]{3,2,1,0:T(8,128)(2,1)S(1)} custom-call(s32[16]{0:T(128)S(1)} %copy-done.3, bf16[20,48,384]{2,1,0:T(8,128)(2,1)S(1)} %collective-permute-done.far.early_far, bf16[12,48,384]{2,1,0:T(8,128)(2,1)S(1)} %collective-permute-done.1.far, bf16[20,48,384]{2,1,0:T(8,128)(2,1)S(1)} %shard_map.56.early, ...), custom_call_target="tpu_custom_call" | custom-call | tf_op jit(solution)/shard_map/pallas_call | solution.py:178
  39.5 38.7 %all_to_all.5.arrived = bf16[16,4,48,384]{3,2,1,0:T(8,128)(2,1)} all-to-all(bf16[16,4,48,384]{3,2,1,0:T(8,128)(2,1)S(1)} %shard_map.57), channel_id=1, replica_groups=mesh['ha'=8,'tc'=8,'core'=2] {'tc','core'}, dimensions={0} | all-to-all | bytes 4718592 | tf_op jit(solution)/shard_map/all_to_all | solution.py:241
  78.2 3.1 %shard_map.58 = bf16[4,16,48,384]{3,2,1,0:T(8,128)(2,1)} custom-call(s32[16]{0:T(128)} %starts.3, bf16[16,4,48,384]{3,2,1,0:T(8,128)(2,1)} %all_to_all.5.arrived), custom_call_target="tpu_custom_call" | custom-call | tf_op jit(solution)/shard_map/pallas_call | solution.py:215
  (2 shorter events, 0.0 us)
Async XLA Ops:
  0.0 7.7 %copy-start.2 = (bf16[32,1,48,384]{3,2,1,0:T(8,128)(2,1)S(1)}, bf16[32,1,48,384]{3,2,1,0:T(8,128)(2,1)}, u32[]{:S(2)}) copy-start(bf16[32,1,48,384]{3,2,1,0:T(8,128)(2,1)} %param.5) | copy-start | bytes 3538948
  0.0 7.6 %copy-start.4 = (f32[384]{0:T(512)S(1)}, f32[384]{0:T(512)}, u32[]{:S(2)}) copy-start(f32[384]{0:T(512)} %param.7) | copy-start | bytes 4612
  0.0 7.6 %copy-start.5 = (f32[384]{0:T(512)S(1)}, f32[384]{0:T(512)}, u32[]{:S(2)}) copy-start(f32[384]{0:T(512)} %param.9) | copy-start | bytes 4612
  0.0 7.6 %collective-permute-start.2 = (bf16[32,48,384]{2,1,0:T(8,128)(2,1)}, bf16[32,48,384]{2,1,0:T(8,128)(2,1)S(1)}, u32[]{:S(2)}, u32[]{:S(2)}) collective-permute-start(bf16[32,48,384]{2,1,0:T(8,128)(2,1)} %bitcast.6), channel_id=1, source_target_pairs={{0,1},{1,0},{2,3},{3,2},{4,5},{5,4},{6,7},{7,6},{8,9},{9,8},{10,11... | collective-permute-start | bytes 3538952 | tf_op jit(solution)/shard_map/ppermute | solution.py:237
  2.6 24.9 %collective-permute-start = (bf16[20,48,384]{2,1,0:T(8,128)(2,1)S(1)}, bf16[20,48,384]{2,1,0:T(8,128)(2,1)S(1)}, u32[]{:S(2)}, u32[]{:S(2)}) collective-permute-start(bf16[20,48,384]{2,1,0:T(8,128)(2,1)S(1)} %slice_bitcast_fusion), channel_id=1, source_target_pairs={{0,127},{1,2},{2,1},{3,4},{4,3},{5,6},{6,5},{7,8},{8,7},{9,10},{10... | collective-permute-start | bytes 2211848 | tf_op jit(solution)/shard_map/ppermute | solution.py:235
  7.5 25.5 %collective-permute-start.1 = (bf16[12,48,384]{2,1,0:T(8,128)(2,1)S(1)}, bf16[12,48,384]{2,1,0:T(8,128)(2,1)S(1)}, u32[]{:S(2)}, u32[]{:S(2)}) collective-permute-start(bf16[12,48,384]{2,1,0:T(8,128)(2,1)S(1)} %slice_bitcast_fusion.1), channel_id=1, source_target_pairs={{0,127},{1,2},{2,1},{3,4},{4,3},{5,6},{6,5},{7,8},{8,7},{9,10},{10... | collective-permute-start | bytes 1327112 | tf_op jit(solution)/shard_map/ppermute | solution.py:236
  7.7 3.3 %copy-start = (bf16[3,3,3,384,384]{4,3,2,1,0:T(8,128)(2,1)S(1)}, bf16[3,3,3,384,384]{4,3,2,1,0:T(8,128)(2,1)}, u32[]{:S(2)}) copy-start(bf16[3,3,3,384,384]{4,3,2,1,0:T(8,128)(2,1)} %weight.5) | copy-start | bytes 23887876
  10.9 16.6 %copy-start.1 = (bf16[3,3,3,384,384]{4,3,2,1,0:T(8,128)(2,1)S(1)}, bf16[3,3,3,384,384]{4,3,2,1,0:T(8,128)(2,1)}, u32[]{:S(2)}) copy-start(bf16[3,3,3,384,384]{4,3,2,1,0:T(8,128)(2,1)} %weight.5) | copy-start | bytes 23887876
  22.7 10.3 %copy-start.3 = (s32[16]{0:T(128)S(1)}, s32[16]{0:T(128)}, u32[]{:S(2)}) copy-start(s32[16]{0:T(128)} %starts.3) | copy-start | bytes 196

commit v6 on v5

--- a/solution.py
+++ b/solution.py
@@ -11,6 +11,7 @@
 HIST = 2
 STEP = 8
 VMEM_BYTES = 30 * 2**20
+UNPACK_VMEM_BYTES = 8 * 2**20
 SMEM_SPEC = pl.BlockSpec(memory_space=pltpu.SMEM)
 VMEM_SPEC = pl.BlockSpec(memory_space=pltpu.VMEM)
 HBM_SPEC = pl.BlockSpec(memory_space=pltpu.HBM)
@@ -131,26 +132,30 @@
 
 
 def late_kernel(starts, early_far, far, early, partial, weight, gain, packed,
-                act, sums, result, early_sem, sems):
+                act, sums, result, sems):
     cut = early.shape[0]
     count, cols, chans = far.shape
     groups = packed.shape[0]
-    copy = pltpu.make_async_copy(early, result.at[pl.ds(0, cut)], early_sem)
-    copy.start()
-    result[pl.ds(cut + count, FMAX)] = jnp.zeros((FMAX, cols, chans), result.dtype)
-    result[pl.ds(cut, count)] = far_frames(
-        cut, far, early_far, partial, weight, gain, act, sums
-    )
-    copy.wait()
-    copies = [
+    ready = [
         pltpu.make_async_copy(
-            result.at[pl.ds(jnp.clip(starts[j], 0, cut + count), FMAX)], packed.at[j], sems.at[j]
+            early.at[pl.ds(jnp.clip(starts[j], 0, cut - FMAX), FMAX)], packed.at[j], sems.at[j]
         )
         for j in range(groups)
     ]
-    for copy in copies:
-        copy.start()
-    for copy in copies:
+    for j in range(groups):
+        pl.when(starts[j] + FMAX <= cut)(ready[j].start)
+    result[pl.ds(0, FMAX)] = early[pl.ds(cut - FMAX, FMAX)]
+    result[pl.ds(FMAX + count, FMAX)] = jnp.zeros((FMAX, cols, chans), result.dtype)
+    result[pl.ds(FMAX, count)] = far_frames(
+        cut, far, early_far, partial, weight, gain, act, sums
+    )
+    for j in range(groups):
+        index = jnp.clip(starts[j] - (cut - FMAX), 0, FMAX + count)
+        copy = pltpu.make_async_copy(
+            result.at[pl.ds(index, FMAX)], packed.at[j], sems.at[j]
+        )
+        pl.when(starts[j] + FMAX > cut)(copy.start)
+    for copy in ready:
         copy.wait()
 
 
@@ -174,7 +179,7 @@
 
 def late_rows(starts, early_far, far, early, partial, weight, gain):
     groups = starts.shape[0]
-    total, cols, chans = partial.shape
+    count, cols, chans = far.shape
     return pl.pallas_call(
         late_kernel,
         out_shape=jax.ShapeDtypeStruct((groups, FMAX, cols, chans), jnp.bfloat16),
@@ -182,8 +187,7 @@
         out_specs=HBM_SPEC,
         scratch_shapes=far_scratch(*far.shape)
         + [
-            pltpu.VMEM((total + FMAX, cols, chans), jnp.bfloat16),
-            pltpu.SemaphoreType.DMA,
+            pltpu.VMEM((FMAX + count + FMAX, cols, chans), jnp.bfloat16),
             pltpu.SemaphoreType.DMA((groups,)),
         ],
         compiler_params=pltpu.CompilerParams(vmem_limit_bytes=VMEM_BYTES),
@@ -221,6 +225,7 @@
             pltpu.VMEM((rows, cols, chans), arrived.dtype),
             pltpu.SemaphoreType.DMA((FMAX,)),
         ],
+        compiler_params=pltpu.CompilerParams(vmem_limit_bytes=UNPACK_VMEM_BYTES),
     )(starts, arrived)
 
 
@@ -232,7 +237,8 @@
     bias = conv_bias.reshape(1, -1)
     pairs = [(r, (r + 1) % rows if r % 2 else (r - 1) % rows) for r in range(rows)]
     cut = total * 5 // 8
-    early_far = lax.ppermute(own[:cut], ("ha", "tc", "core"), pairs)
+    front, own = lax.optimization_barrier((own[:cut], own))
+    early_far = lax.ppermute(front, ("ha", "tc", "core"), pairs)
     late_far = lax.ppermute(own[cut:], ("ha", "tc", "core"), pairs)
     twin = lax.ppermute(own, "core", [(0, 1), (1, 0)])
     partial = near_rows(own, twin, conv_weight, gain, bias)

time: 81.6 us -> 80.3 us (0.984)
  Pallas kernels: 25.4 us -> 24.2 us
    pallas_call x1, Pallas kernels: 3.12 us -> 1.99 us  [unpack(): pl.pallas_call(functools.partial(unpack_kernel, total), out_shape=jax.Sha...]
  transfers between devices with their start and end apart: 3 -> 3, of which waited for: 2 -> 2; matrix products, arithmetic and copies ran while one was open for 3% -> 1% of each run, Pallas kernels for 19% -> 20%
where the time goes in v6:
time: 80.3 us; the launch traced here: 80 us
  blocking collectives  38.6 us (48%)
  Pallas kernels  24.2 us (30%)
  waiting for transfers between devices  6.29 us (8%)
  local copies, waits for them, and re-layouts  5.63 us (7%)
  starting transfers between devices  5.26 us (7%)
    all_to_all x1, blocking collectives, on_device(): lax.all_to_all(packed, ('tc', 'core'), split_axis=0, concat_axis=0, tiled...  38.6 us
    pallas_call x1, Pallas kernels, near_rows(): pl.pallas_call(near_kernel, out_shape=jax.ShapeDtypeStruct(own.shape, jnp...  11.8 us
    pallas_call x1, Pallas kernels, late_rows(): pl.pallas_call(late_kernel, out_shape=jax.ShapeDtypeStruct((groups, FMAX,...  6.48 us
    ppermute x1, waiting for transfers between devices, on_device(): early_far = lax.ppermute(front, ('ha', 'tc', 'core'), pairs)  4.78 us
    pallas_call x1, Pallas kernels, early_rows(): pl.pallas_call(early_kernel, out_shape=jax.ShapeDtypeStruct(far.shape, jn...  3.96 us
    ppermute x1, starting transfers between devices, on_device(): early_far = lax.ppermute(front, ('ha', 'tc', 'core'), pairs)  3.66 us
    unnamed x12, local copies, waits for them, and re-layouts  3.28 us
    pallas_call x1, Pallas kernels, unpack(): pl.pallas_call(functools.partial(unpack_kernel, total), out_shape=jax.Sha...  1.99 us
  transfers between devices with their start and end apart: 3, of which 2 were waited for; matrix products, arithmetic and copies ran while one was open for 1% of the time, Pallas kernels for 20%

profile of v6, /device:TPU:1, one launch (start us, length us, event | category | flops | bytes accessed | tf_op | source)
XLA Modules:
  0.0 80.0 jit_solution(5151377047774245742)
XLA Ops:
  0.0 0.0 copy-start.2
  0.0 0.0 copy-start.4
  0.0 0.0 copy-start.5
  0.0 1.3 %slice_bitcast_fusion = bf16[20,48,384]{2,1,0:T(8,128)(2,1)S(1)} fusion(bf16[32,1,48,384]{3,2,0,1:T(8,128)(2,1)} %bitcast.4), kind=kLoop, calls=%fused_computation | loop fusion | bytes 1474560 | tf_op jit(solution)/shard_map/slice | solution.py:240
  1.3 1.5 %collective-permute-start.2 = (bf16[32,48,384]{2,1,0:T(8,128)(2,1)}, bf16[32,48,384]{2,1,0:T(8,128)(2,1)S(1)}, u32[]{:S(2)}, u32[]{:S(2)}) collective-permute-start(bf16[32,48,384]{2,1,0:T(8,128)(2,1)} %bitcast.5), channel_id=1, source_target_pairs={{0,1},{1,0},{2,3},{3,2},{4,5},{5,4},{6,7},{7,6},{8,9},{9,8},{10,11... | collective-permute-start | bytes 3538952 | tf_op jit(solution)/shard_map/ppermute | solution.py:243
  2.8 3.7 %collective-permute-start = (bf16[20,48,384]{2,1,0:T(8,128)(2,1)S(1)}, bf16[20,48,384]{2,1,0:T(8,128)(2,1)S(1)}, u32[]{:S(2)}, u32[]{:S(2)}) collective-permute-start(bf16[20,48,384]{2,1,0:T(8,128)(2,1)S(1)} %slice_bitcast_fusion), channel_id=1, source_target_pairs={{0,127},{1,2},{2,1},{3,4},{4,3},{5,6},{6,5},{7,8},{8,7},{9,10},{10... | collective-permute-start | bytes 2211848 | tf_op jit(solution)/shard_map/ppermute | solution.py:241
  6.5 1.1 %slice.11 = bf16[12,48,384]{2,1,0:T(8,128)(2,1)S(1)} slice(bf16[32,48,384]{2,1,0:T(8,128)(2,1)} %bitcast.6), slice={[20:32], [0:48], [0:384]} | slice | bytes 884736 | tf_op jit(solution)/shard_map/slice | solution.py:242
  7.5 0.1 collective-permute-start.1
  7.6 0.0 copy-done.4
  7.6 0.0 copy-done.5
  7.7 0.0 collective-permute-done.2.twin
  7.7 0.0 copy-done.2
  7.7 0.0 copy-start
  7.7 3.3 %copy-done = bf16[3,3,3,384,384]{4,3,2,1,0:T(8,128)(2,1)S(1)} copy-done((bf16[3,3,3,384,384]{4,3,2,1,0:T(8,128)(2,1)S(1)}, bf16[3,3,3,384,384]{4,3,2,1,0:T(8,128)(2,1)}, u32[]{:S(2)}) %copy-start) | copy-done | bytes 7962648
  10.9 0.0 copy-start.1
  10.9 11.8 %shard_map.55.partial = f32[32,48,384]{2,1,0:T(8,128)S(1)} custom-call(bf16[32,48,384]{2,1,0:T(8,128)(2,1)S(1)} %bitcast.7, bf16[32,48,384]{2,1,0:T(8,128)(2,1)S(1)} %collective-permute-done.2.twin, bf16[3,3,3,384,384]{4,3,2,1,0:T(8,128)(2,1)S(1)} %copy-done, f32[1,384]{1,0:T(1,128)S(1)} %reshape.7.gain, f32[1,384]{1,0:T(1,128)S(1)} %reshape.8.bias), custom_call_target="tpu_custom_call" | custom-call | tf_op jit(solution)/shard_map/pallas_call | solution.py:95
  22.7 0.0 copy-start.3
  22.7 4.8 %collective-permute-done.far.early_far = bf16[20,48,384]{2,1,0:T(8,128)(2,1)S(1)} collective-permute-done((bf16[20,48,384]{2,1,0:T(8,128)(2,1)S(1)}, bf16[20,48,384]{2,1,0:T(8,128)(2,1)S(1)}, u32[]{:S(2)}, u32[]{:S(2)}) %collective-permute-start) | collective-permute-done | bytes 737312 | tf_op jit(solution)/shard_map/ppermute | solution.py:241
  27.5 0.0 copy-done.1
  27.5 4.0 %shard_map.56.early = bf16[20,48,384]{2,1,0:T(8,128)(2,1)S(1)} custom-call(bf16[20,48,384]{2,1,0:T(8,128)(2,1)S(1)} %collective-permute-done.far.early_far, f32[32,48,384]{2,1,0:T(8,128)S(1)} %shard_map.55.partial, bf16[3,3,3,384,384]{4,3,2,1,0:T(8,128)(2,1)S(1)} %copy-done.1, f32[1,384]{1,0:T(1,128)S(1)} %reshape.7.gain), custom_call_target="tpu_custom_call" | custom-call | tf_op jit(solution)/shard_map/pallas_call | solution.py:170
  31.5 1.5 %collective-permute-done.1.far = bf16[12,48,384]{2,1,0:T(8,128)(2,1)S(1)} collective-permute-done((bf16[12,48,384]{2,1,0:T(8,128)(2,1)S(1)}, bf16[12,48,384]{2,1,0:T(8,128)(2,1)S(1)}, u32[]{:S(2)}, u32[]{:S(2)}) %collective-permute-start.1) | collective-permute-done | bytes 442400 | tf_op jit(solution)/shard_map/ppermute | solution.py:242
  33.0 0.0 copy-done.3
  33.0 6.5 %shard_map.57 = bf16[16,4,48,384]{3,2,1,0:T(8,128)(2,1)S(1)} custom-call(s32[16]{0:T(128)S(1)} %copy-done.3, bf16[20,48,384]{2,1,0:T(8,128)(2,1)S(1)} %collective-permute-done.far.early_far, bf16[12,48,384]{2,1,0:T(8,128)(2,1)S(1)} %collective-permute-done.1.far, bf16[20,48,384]{2,1,0:T(8,128)(2,1)S(1)} %shard_map.56.early, ...), custom_call_target="tpu_custom_call" | custom-call | tf_op jit(solution)/shard_map/pallas_call | solution.py:183
  39.5 38.6 %all_to_all.5.arrived = bf16[16,4,48,384]{3,2,1,0:T(8,128)(2,1)S(1)} all-to-all(bf16[16,4,48,384]{3,2,1,0:T(8,128)(2,1)S(1)} %shard_map.57), channel_id=1, replica_groups=mesh['ha'=8,'tc'=8,'core'=2] {'tc','core'}, dimensions={0} | all-to-all | bytes 4718592 | tf_op jit(solution)/shard_map/all_to_all | solution.py:247
  78.0 2.0 %shard_map.58 = bf16[4,16,48,384]{3,2,1,0:T(8,128)(2,1)} custom-call(s32[16]{0:T(128)S(1)} %copy-done.3, bf16[16,4,48,384]{3,2,1,0:T(8,128)(2,1)S(1)} %all_to_all.5.arrived), custom_call_target="tpu_custom_call" | custom-call | tf_op jit(solution)/shard_map/pallas_call | solution.py:219
  (2 shorter events, 0.0 us)
Async XLA Ops:
  0.0 7.7 %copy-start.2 = (bf16[32,1,48,384]{3,2,1,0:T(8,128)(2,1)S(1)}, bf16[32,1,48,384]{3,2,1,0:T(8,128)(2,1)}, u32[]{:S(2)}) copy-start(bf16[32,1,48,384]{3,2,1,0:T(8,128)(2,1)} %param.5) | copy-start | bytes 3538948
  0.0 7.6 %copy-start.4 = (f32[384]{0:T(512)S(1)}, f32[384]{0:T(512)}, u32[]{:S(2)}) copy-start(f32[384]{0:T(512)} %param.7) | copy-start | bytes 4612
  0.0 7.6 %copy-start.5 = (f32[384]{0:T(512)S(1)}, f32[384]{0:T(512)}, u32[]{:S(2)}) copy-start(f32[384]{0:T(512)} %param.9) | copy-start | bytes 4612
  1.3 6.4 %collective-permute-start.2 = (bf16[32,48,384]{2,1,0:T(8,128)(2,1)}, bf16[32,48,384]{2,1,0:T(8,128)(2,1)S(1)}, u32[]{:S(2)}, u32[]{:S(2)}) collective-permute-start(bf16[32,48,384]{2,1,0:T(8,128)(2,1)} %bitcast.5), channel_id=1, source_target_pairs={{0,1},{1,0},{2,3},{3,2},{4,5},{5,4},{6,7},{7,6},{8,9},{9,8},{10,11... | collective-permute-start | bytes 3538952 | tf_op jit(solution)/shard_map/ppermute | solution.py:243
  2.8 24.7 %collective-permute-start = (bf16[20,48,384]{2,1,0:T(8,128)(2,1)S(1)}, bf16[20,48,384]{2,1,0:T(8,128)(2,1)S(1)}, u32[]{:S(2)}, u32[]{:S(2)}) collective-permute-start(bf16[20,48,384]{2,1,0:T(8,128)(2,1)S(1)} %slice_bitcast_fusion), channel_id=1, source_target_pairs={{0,127},{1,2},{2,1},{3,4},{4,3},{5,6},{6,5},{7,8},{8,7},{9,10},{10... | collective-permute-start | bytes 2211848 | tf_op jit(solution)/shard_map/ppermute | solution.py:241
  7.5 25.5 %collective-permute-start.1 = (bf16[12,48,384]{2,1,0:T(8,128)(2,1)S(1)}, bf16[12,48,384]{2,1,0:T(8,128)(2,1)S(1)}, u32[]{:S(2)}, u32[]{:S(2)}) collective-permute-start(bf16[12,48,384]{2,1,0:T(8,128)(2,1)S(1)} %slice.11), channel_id=1, source_target_pairs={{0,127},{1,2},{2,1},{3,4},{4,3},{5,6},{6,5},{7,8},{8,7},{9,10},{10... | collective-permute-start | bytes 1327112 | tf_op jit(solution)/shard_map/ppermute | solution.py:242
  7.7 3.3 %copy-start = (bf16[3,3,3,384,384]{4,3,2,1,0:T(8,128)(2,1)S(1)}, bf16[3,3,3,384,384]{4,3,2,1,0:T(8,128)(2,1)}, u32[]{:S(2)}) copy-start(bf16[3,3,3,384,384]{4,3,2,1,0:T(8,128)(2,1)} %weight.5) | copy-start | bytes 23887876
  10.9 16.6 %copy-start.1 = (bf16[3,3,3,384,384]{4,3,2,1,0:T(8,128)(2,1)S(1)}, bf16[3,3,3,384,384]{4,3,2,1,0:T(8,128)(2,1)}, u32[]{:S(2)}) copy-start(bf16[3,3,3,384,384]{4,3,2,1,0:T(8,128)(2,1)} %weight.5) | copy-start | bytes 23887876
  22.7 10.3 %copy-start.3 = (s32[16]{0:T(128)S(1)}, s32[16]{0:T(128)}, u32[]{:S(2)}) copy-start(s32[16]{0:T(128)} %starts.3) | copy-start | bytes 196

commit v7 on v5

--- a/solution.py
+++ b/solution.py
@@ -11,6 +11,7 @@
 HIST = 2
 STEP = 8
 VMEM_BYTES = 30 * 2**20
+UNPACK_VMEM_BYTES = 8 * 2**20
 SMEM_SPEC = pl.BlockSpec(memory_space=pltpu.SMEM)
 VMEM_SPEC = pl.BlockSpec(memory_space=pltpu.VMEM)
 HBM_SPEC = pl.BlockSpec(memory_space=pltpu.HBM)
@@ -130,28 +131,16 @@
     out[...] = far_frames(0, far, None, partial, weight, gain, act, sums)
 
 
-def late_kernel(starts, early_far, far, early, partial, weight, gain, packed,
-                act, sums, result, early_sem, sems):
+def late_kernel(starts, early_far, far, early, partial, weight, gain, packed, act, sums, result):
     cut = early.shape[0]
     count, cols, chans = far.shape
-    groups = packed.shape[0]
-    copy = pltpu.make_async_copy(early, result.at[pl.ds(0, cut)], early_sem)
-    copy.start()
+    result[pl.ds(0, cut)] = early[...]
     result[pl.ds(cut + count, FMAX)] = jnp.zeros((FMAX, cols, chans), result.dtype)
     result[pl.ds(cut, count)] = far_frames(
         cut, far, early_far, partial, weight, gain, act, sums
     )
-    copy.wait()
-    copies = [
-        pltpu.make_async_copy(
-            result.at[pl.ds(jnp.clip(starts[j], 0, cut + count), FMAX)], packed.at[j], sems.at[j]
-        )
-        for j in range(groups)
-    ]
-    for copy in copies:
-        copy.start()
-    for copy in copies:
-        copy.wait()
+    for j in range(packed.shape[0]):
+        packed[j] = result[pl.ds(jnp.clip(starts[j], 0, cut + count), FMAX)]
 
 
 def far_scratch(count, cols, chans):
@@ -173,19 +162,14 @@
 
 
 def late_rows(starts, early_far, far, early, partial, weight, gain):
-    groups = starts.shape[0]
     total, cols, chans = partial.shape
     return pl.pallas_call(
         late_kernel,
-        out_shape=jax.ShapeDtypeStruct((groups, FMAX, cols, chans), jnp.bfloat16),
+        out_shape=jax.ShapeDtypeStruct((starts.shape[0], FMAX, cols, chans), jnp.bfloat16),
         in_specs=[SMEM_SPEC] + [VMEM_SPEC] * 6,
-        out_specs=HBM_SPEC,
+        out_specs=VMEM_SPEC,
         scratch_shapes=far_scratch(*far.shape)
-        + [
-            pltpu.VMEM((total + FMAX, cols, chans), jnp.bfloat16),
-            pltpu.SemaphoreType.DMA,
-            pltpu.SemaphoreType.DMA((groups,)),
-        ],
+        + [pltpu.VMEM((total + FMAX, cols, chans), jnp.bfloat16)],
         compiler_params=pltpu.CompilerParams(vmem_limit_bytes=VMEM_BYTES),
     )(starts, early_far, far, early, partial, weight, gain)
 
@@ -221,6 +205,7 @@
             pltpu.VMEM((rows, cols, chans), arrived.dtype),
             pltpu.SemaphoreType.DMA((FMAX,)),
         ],
+        compiler_params=pltpu.CompilerParams(vmem_limit_bytes=UNPACK_VMEM_BYTES),
     )(starts, arrived)
 
 
@@ -232,9 +217,11 @@
     bias = conv_bias.reshape(1, -1)
     pairs = [(r, (r + 1) % rows if r % 2 else (r - 1) % rows) for r in range(rows)]
     cut = total * 5 // 8
-    early_far = lax.ppermute(own[:cut], ("ha", "tc", "core"), pairs)
-    late_far = lax.ppermute(own[cut:], ("ha", "tc", "core"), pairs)
-    twin = lax.ppermute(own, "core", [(0, 1), (1, 0)])
+    front, rest = lax.optimization_barrier((own[:cut], own))
+    back, rest = lax.optimization_barrier((rest[cut:], rest))
+    early_far = lax.ppermute(front, ("ha", "tc", "core"), pairs)
+    late_far = lax.ppermute(back, ("ha", "tc", "core"), pairs)
+    twin = lax.ppermute(rest, "core", [(0, 1), (1, 0)])
     partial = near_rows(own, twin, conv_weight, gain, bias)
     early = early_rows(early_far, partial, conv_weight, gain)
     packed = late_rows(group_start, early_far, late_far, early, partial, conv_weight, gain)

time: 81.6 us -> 78.1 us (0.957)
  Pallas kernels: 25.4 us -> 21 us
  waiting for transfers between devices: 6.29 us -> 7.32 us
    pallas_call x1, Pallas kernels: 6.56 us -> 3.25 us  [late_rows(): pl.pallas_call(late_kernel, out_shape=jax.ShapeDtypeStruct((starts.shape[...]
    pallas_call x1, Pallas kernels: 3.12 us -> 1.99 us  [unpack(): pl.pallas_call(functools.partial(unpack_kernel, total), out_shape=jax.Sha...]
    ppermute x3, waiting for transfers between devices: 6.29 us -> 7.32 us  [the longest x1 5.81 us: on_device(): early_far = lax.ppermute(front, ('ha', 'tc', 'core'), pairs)]
  transfers between devices with their start and end apart: 3 -> 3, of which waited for: 2 -> 2; matrix products, arithmetic and copies ran while one was open for 3% -> 0% of each run, Pallas kernels for 19% -> 20%
where the time goes in v7:
time: 78.1 us; the launch traced here: 77.9 us
  blocking collectives  38.6 us (49%)
  Pallas kernels  21 us (27%)
  waiting for transfers between devices  7.32 us (9%)
  local copies, waits for them, and re-layouts  5.63 us (7%)
  starting transfers between devices  5.25 us (7%)
    all_to_all x1, blocking collectives, on_device(): lax.all_to_all(packed, ('tc', 'core'), split_axis=0, concat_axis=0, tiled...  38.6 us
    pallas_call x1, Pallas kernels, near_rows(): pl.pallas_call(near_kernel, out_shape=jax.ShapeDtypeStruct(own.shape, jnp...  11.8 us
    ppermute x1, waiting for transfers between devices, on_device(): early_far = lax.ppermute(front, ('ha', 'tc', 'core'), pairs)  5.81 us
    pallas_call x1, Pallas kernels, early_rows(): pl.pallas_call(early_kernel, out_shape=jax.ShapeDtypeStruct(far.shape, jn...  3.96 us
    ppermute x1, starting transfers between devices, on_device(): early_far = lax.ppermute(front, ('ha', 'tc', 'core'), pairs)  3.66 us
    unnamed x12, local copies, waits for them, and re-layouts  3.28 us
    pallas_call x1, Pallas kernels, late_rows(): pl.pallas_call(late_kernel, out_shape=jax.ShapeDtypeStruct((starts.shape[...  3.25 us
    pallas_call x1, Pallas kernels, unpack(): pl.pallas_call(functools.partial(unpack_kernel, total), out_shape=jax.Sha...  1.99 us
  transfers between devices with their start and end apart: 3, of which 2 were waited for; matrix products, arithmetic and copies ran while one was open for 0% of the time, Pallas kernels for 20%

profile of v7, /device:TPU:1, one launch (start us, length us, event | category | flops | bytes accessed | tf_op | source)
XLA Modules:
  0.0 77.9 jit_solution(8920781586227233134)
XLA Ops:
  0.0 0.0 copy-start.2
  0.0 0.0 copy-start.4
  0.0 0.0 copy-start.5
  0.0 1.3 %slice_bitcast_fusion = bf16[20,48,384]{2,1,0:T(8,128)(2,1)S(1)} fusion(bf16[32,1,48,384]{3,2,0,1:T(8,128)(2,1)} %bitcast.4), kind=kLoop, calls=%fused_computation | loop fusion | bytes 1474560 | tf_op jit(solution)/shard_map/slice | solution.py:220
  1.3 1.1 %slice.11 = bf16[12,48,384]{2,1,0:T(8,128)(2,1)S(1)} slice(bf16[32,48,384]{2,1,0:T(8,128)(2,1)} %bitcast.5), slice={[20:32], [0:48], [0:384]} | slice | bytes 884736 | tf_op jit(solution)/shard_map/slice | solution.py:221
  2.4 0.0 copy-done.2
  2.4 1.5 %collective-permute-start.2 = (bf16[32,48,384]{2,1,0:T(8,128)(2,1)S(1)}, bf16[32,48,384]{2,1,0:T(8,128)(2,1)S(1)}, u32[]{:S(2)}, u32[]{:S(2)}) collective-permute-start(bf16[32,48,384]{2,1,0:T(8,128)(2,1)S(1)} %bitcast.6), channel_id=1, source_target_pairs={{0,1},{1,0},{2,3},{3,2},{4,5},{5,4},{6,7},{7,6},{8,9},{9,8},{10,11... | collective-permute-start | bytes 3538952 | tf_op jit(solution)/shard_map/ppermute | solution.py:224
  3.9 3.7 %collective-permute-start = (bf16[20,48,384]{2,1,0:T(8,128)(2,1)S(1)}, bf16[20,48,384]{2,1,0:T(8,128)(2,1)S(1)}, u32[]{:S(2)}, u32[]{:S(2)}) collective-permute-start(bf16[20,48,384]{2,1,0:T(8,128)(2,1)S(1)} %slice_bitcast_fusion), channel_id=1, source_target_pairs={{0,127},{1,2},{2,1},{3,4},{4,3},{5,6},{6,5},{7,8},{8,7},{9,10},{10... | collective-permute-start | bytes 2211848 | tf_op jit(solution)/shard_map/ppermute | solution.py:222
  7.5 0.1 collective-permute-start.1
  7.6 0.0 copy-done.4
  7.6 0.0 copy-done.5
  7.6 0.0 collective-permute-done.2.twin
  7.7 0.0 copy-start
  7.7 3.3 %copy-done = bf16[3,3,3,384,384]{4,3,2,1,0:T(8,128)(2,1)S(1)} copy-done((bf16[3,3,3,384,384]{4,3,2,1,0:T(8,128)(2,1)S(1)}, bf16[3,3,3,384,384]{4,3,2,1,0:T(8,128)(2,1)}, u32[]{:S(2)}) %copy-start) | copy-done | bytes 7962648
  10.9 0.0 copy-start.1
  10.9 11.8 %shard_map.55.partial = f32[32,48,384]{2,1,0:T(8,128)S(1)} custom-call(bf16[32,48,384]{2,1,0:T(8,128)(2,1)S(1)} %bitcast.7, bf16[32,48,384]{2,1,0:T(8,128)(2,1)S(1)} %collective-permute-done.2.twin, bf16[3,3,3,384,384]{4,3,2,1,0:T(8,128)(2,1)S(1)} %copy-done, f32[1,384]{1,0:T(1,128)S(1)} %reshape.7.gain, f32[1,384]{1,0:T(1,128)S(1)} %reshape.8.bias), custom_call_target="tpu_custom_call" | custom-call | tf_op jit(solution)/shard_map/pallas_call | solution.py:95
  22.8 0.0 copy-start.3
  22.8 5.8 %collective-permute-done.far.early_far = bf16[20,48,384]{2,1,0:T(8,128)(2,1)S(1)} collective-permute-done((bf16[20,48,384]{2,1,0:T(8,128)(2,1)S(1)}, bf16[20,48,384]{2,1,0:T(8,128)(2,1)S(1)}, u32[]{:S(2)}, u32[]{:S(2)}) %collective-permute-start) | collective-permute-done | bytes 737312 | tf_op jit(solution)/shard_map/ppermute | solution.py:222
  28.6 0.0 copy-done.1
  28.6 4.0 %shard_map.56.early = bf16[20,48,384]{2,1,0:T(8,128)(2,1)S(1)} custom-call(bf16[20,48,384]{2,1,0:T(8,128)(2,1)S(1)} %collective-permute-done.far.early_far, f32[32,48,384]{2,1,0:T(8,128)S(1)} %shard_map.55.partial, bf16[3,3,3,384,384]{4,3,2,1,0:T(8,128)(2,1)S(1)} %copy-done.1, f32[1,384]{1,0:T(1,128)S(1)} %reshape.7.gain), custom_call_target="tpu_custom_call" | custom-call | tf_op jit(solution)/shard_map/pallas_call | solution.py:154
  32.6 1.5 %collective-permute-done.1.far = bf16[12,48,384]{2,1,0:T(8,128)(2,1)S(1)} collective-permute-done((bf16[12,48,384]{2,1,0:T(8,128)(2,1)S(1)}, bf16[12,48,384]{2,1,0:T(8,128)(2,1)S(1)}, u32[]{:S(2)}, u32[]{:S(2)}) %collective-permute-start.1) | collective-permute-done | bytes 442400 | tf_op jit(solution)/shard_map/ppermute | solution.py:223
  34.1 0.0 copy-done.3
  34.1 3.3 %shard_map.57 = bf16[16,4,48,384]{3,2,1,0:T(8,128)(2,1)S(1)} custom-call(s32[16]{0:T(128)S(1)} %copy-done.3, bf16[20,48,384]{2,1,0:T(8,128)(2,1)S(1)} %collective-permute-done.far.early_far, bf16[12,48,384]{2,1,0:T(8,128)(2,1)S(1)} %collective-permute-done.1.far, bf16[20,48,384]{2,1,0:T(8,128)(2,1)S(1)} %shard_map.56.early, ...), custom_call_target="tpu_custom_call" | custom-call | tf_op jit(solution)/shard_map/pallas_call | solution.py:166
  37.3 38.6 %all_to_all.5.arrived = bf16[16,4,48,384]{3,2,1,0:T(8,128)(2,1)S(1)} all-to-all(bf16[16,4,48,384]{3,2,1,0:T(8,128)(2,1)S(1)} %shard_map.57), channel_id=1, replica_groups=mesh['ha'=8,'tc'=8,'core'=2] {'tc','core'}, dimensions={0} | all-to-all | bytes 4718592 | tf_op jit(solution)/shard_map/all_to_all | solution.py:228
  75.9 2.0 %shard_map.58 = bf16[4,16,48,384]{3,2,1,0:T(8,128)(2,1)} custom-call(s32[16]{0:T(128)S(1)} %copy-done.3, bf16[16,4,48,384]{3,2,1,0:T(8,128)(2,1)S(1)} %all_to_all.5.arrived), custom_call_target="tpu_custom_call" | custom-call | tf_op jit(solution)/shard_map/pallas_call | solution.py:199
  (2 shorter events, 0.0 us)
Async XLA Ops:
  0.0 2.4 %copy-start.2 = (bf16[32,1,48,384]{3,2,1,0:T(8,128)(2,1)S(1)}, bf16[32,1,48,384]{3,2,1,0:T(8,128)(2,1)}, u32[]{:S(2)}) copy-start(bf16[32,1,48,384]{3,2,1,0:T(8,128)(2,1)} %param.5) | copy-start | bytes 3538948
  0.0 7.6 %copy-start.4 = (f32[384]{0:T(512)S(1)}, f32[384]{0:T(512)}, u32[]{:S(2)}) copy-start(f32[384]{0:T(512)} %param.7) | copy-start | bytes 4612
  0.0 7.6 %copy-start.5 = (f32[384]{0:T(512)S(1)}, f32[384]{0:T(512)}, u32[]{:S(2)}) copy-start(f32[384]{0:T(512)} %param.9) | copy-start | bytes 4612
  2.4 5.3 %collective-permute-start.2 = (bf16[32,48,384]{2,1,0:T(8,128)(2,1)S(1)}, bf16[32,48,384]{2,1,0:T(8,128)(2,1)S(1)}, u32[]{:S(2)}, u32[]{:S(2)}) collective-permute-start(bf16[32,48,384]{2,1,0:T(8,128)(2,1)S(1)} %bitcast.6), channel_id=1, source_target_pairs={{0,1},{1,0},{2,3},{3,2},{4,5},{5,4},{6,7},{7,6},{8,9},{9,8},{10,11... | collective-permute-start | bytes 3538952 | tf_op jit(solution)/shard_map/ppermute | solution.py:224
  3.9 24.7 %collective-permute-start = (bf16[20,48,384]{2,1,0:T(8,128)(2,1)S(1)}, bf16[20,48,384]{2,1,0:T(8,128)(2,1)S(1)}, u32[]{:S(2)}, u32[]{:S(2)}) collective-permute-start(bf16[20,48,384]{2,1,0:T(8,128)(2,1)S(1)} %slice_bitcast_fusion), channel_id=1, source_target_pairs={{0,127},{1,2},{2,1},{3,4},{4,3},{5,6},{6,5},{7,8},{8,7},{9,10},{10... | collective-permute-start | bytes 2211848 | tf_op jit(solution)/shard_map/ppermute | solution.py:222
  7.5 26.5 %collective-permute-start.1 = (bf16[12,48,384]{2,1,0:T(8,128)(2,1)S(1)}, bf16[12,48,384]{2,1,0:T(8,128)(2,1)S(1)}, u32[]{:S(2)}, u32[]{:S(2)}) collective-permute-start(bf16[12,48,384]{2,1,0:T(8,128)(2,1)S(1)} %slice.11), channel_id=1, source_target_pairs={{0,127},{1,2},{2,1},{3,4},{4,3},{5,6},{6,5},{7,8},{8,7},{9,10},{10... | collective-permute-start | bytes 1327112 | tf_op jit(solution)/shard_map/ppermute | solution.py:223
  7.7 3.3 %copy-start = (bf16[3,3,3,384,384]{4,3,2,1,0:T(8,128)(2,1)S(1)}, bf16[3,3,3,384,384]{4,3,2,1,0:T(8,128)(2,1)}, u32[]{:S(2)}) copy-start(bf16[3,3,3,384,384]{4,3,2,1,0:T(8,128)(2,1)} %weight.5) | copy-start | bytes 23887876
  10.9 17.7 %copy-start.1 = (bf16[3,3,3,384,384]{4,3,2,1,0:T(8,128)(2,1)S(1)}, bf16[3,3,3,384,384]{4,3,2,1,0:T(8,128)(2,1)}, u32[]{:S(2)}) copy-start(bf16[3,3,3,384,384]{4,3,2,1,0:T(8,128)(2,1)} %weight.5) | copy-start | bytes 23887876
  22.8 11.3 %copy-start.3 = (s32[16]{0:T(128)S(1)}, s32[16]{0:T(128)}, u32[]{:S(2)}) copy-start(s32[16]{0:T(128)} %starts.3) | copy-start | bytes 196

commit v8 on v7

--- a/solution.py
+++ b/solution.py
@@ -131,7 +131,14 @@
     out[...] = far_frames(0, far, None, partial, weight, gain, act, sums)
 
 
-def late_kernel(starts, early_far, far, early, partial, weight, gain, packed, act, sums, result):
+def after_of(starts, group, total):
+    groups = starts.shape[0]
+    return jnp.where(group + 1 < groups, starts[jnp.minimum(group + 1, groups - 1)], total)
+
+
+def late_kernel(
+    fits, starts, early_far, far, early, partial, weight, gain, few, many, act, sums, result
+):
     cut = early.shape[0]
     count, cols, chans = far.shape
     result[pl.ds(0, cut)] = early[...]
@@ -139,8 +146,19 @@
     result[pl.ds(cut, count)] = far_frames(
         cut, far, early_far, partial, weight, gain, act, sums
     )
-    for j in range(packed.shape[0]):
-        packed[j] = result[pl.ds(jnp.clip(starts[j], 0, cut + count), FMAX)]
+    total = cut + count
+
+    @pl.when(fits[0] == 0)
+    def _():
+        for j in range(many.shape[0]):
+            many[j] = result[pl.ds(jnp.clip(starts[j], 0, total), FMAX)]
+
+    @pl.when(fits[0] == 1)
+    def _():
+        slots = few.shape[1]
+        for j in range(few.shape[0]):
+            first = after_of(starts, j, total) - slots if j % 2 else starts[j]
+            few[j] = result[pl.ds(jnp.clip(first, 0, total - slots), slots)]
 
 
 def far_scratch(count, cols, chans):
@@ -161,52 +179,81 @@
     )(far, partial, weight, gain)
 
 
-def late_rows(starts, early_far, far, early, partial, weight, gain):
+def late_rows(fits, starts, early_far, far, early, partial, weight, gain):
     total, cols, chans = partial.shape
     return pl.pallas_call(
         late_kernel,
-        out_shape=jax.ShapeDtypeStruct((starts.shape[0], FMAX, cols, chans), jnp.bfloat16),
-        in_specs=[SMEM_SPEC] + [VMEM_SPEC] * 6,
-        out_specs=VMEM_SPEC,
+        out_shape=[
+            jax.ShapeDtypeStruct((starts.shape[0], slots, cols, chans), jnp.bfloat16)
+            for slots in (FMAX - 1, FMAX)
+        ],
+        in_specs=[SMEM_SPEC] * 2 + [VMEM_SPEC] * 6,
+        out_specs=[VMEM_SPEC] * 2,
         scratch_shapes=far_scratch(*far.shape)
         + [pltpu.VMEM((total + FMAX, cols, chans), jnp.bfloat16)],
         compiler_params=pltpu.CompilerParams(vmem_limit_bytes=VMEM_BYTES),
-    )(starts, early_far, far, early, partial, weight, gain)
-
-
-def unpack_kernel(total, starts, arrived, out, blank, sems):
-    groups = starts.shape[0]
-    group = lax.axis_index("tc") * lax.axis_size("core") + lax.axis_index("core")
-    after = jnp.where(group + 1 < groups, starts[jnp.minimum(group + 1, groups - 1)], total)
-    length = after - starts[group]
-    blank[...] = jnp.zeros(blank.shape, blank.dtype)
+    )(fits, starts, early_far, far, early, partial, weight, gain)
+
+
+def unpack_kernel(total, starts, arrived, other, out):
+    slots = arrived.shape[1]
+    core = lax.axis_index("core")
+    group = lax.axis_index("tc") * lax.axis_size("core") + core
+    start = starts[group]
+    after = after_of(starts, group, total)
+    length = after - start
+    held = start
+    if slots < FMAX:
+        held = jnp.clip(jnp.where(core == 1, after - slots, start), 0, total - slots)
     for k in range(FMAX):
-
-        @pl.when(k < length)
+        slot = start + k - held
+        inside = jnp.logical_and(slot >= 0, slot < slots)
+
+        @pl.when(jnp.logical_and(k < length, inside))
         def _():
-            pltpu.make_async_copy(arrived.at[:, k], out.at[k], sems.at[k]).start()
+            out[k] = arrived[:, jnp.clip(slot, 0, slots - 1)]
+
+        @pl.when(jnp.logical_and(k < length, jnp.logical_not(inside)))
+        def _():
+            out[k] = other[:, 0]
 
         @pl.when(k >= length)
         def _():
-            pltpu.make_async_copy(blank, out.at[k], sems.at[k]).start()
-
-    for k in range(FMAX):
-        pltpu.make_async_copy(blank, out.at[k], sems.at[k]).wait()
-
-
-def unpack(total, starts, arrived):
+            out[k] = jnp.zeros(out.shape[1:], out.dtype)
+
+
+def unpack(total, starts, arrived, other):
     rows, _, cols, chans = arrived.shape
     return pl.pallas_call(
         functools.partial(unpack_kernel, total),
         out_shape=jax.ShapeDtypeStruct((FMAX, rows, cols, chans), arrived.dtype),
-        in_specs=[SMEM_SPEC, VMEM_SPEC],
-        out_specs=HBM_SPEC,
-        scratch_shapes=[
-            pltpu.VMEM((rows, cols, chans), arrived.dtype),
-            pltpu.SemaphoreType.DMA((FMAX,)),
-        ],
+        in_specs=[SMEM_SPEC, VMEM_SPEC, VMEM_SPEC],
+        out_specs=VMEM_SPEC,
         compiler_params=pltpu.CompilerParams(vmem_limit_bytes=UNPACK_VMEM_BYTES),
-    )(starts, arrived)
+    )(starts, arrived, other)
+
+
+def regroup(packed):
+    return lax.all_to_all(packed, ("tc", "core"), split_axis=0, concat_axis=0, tiled=True)
+
+
+def send_few(total, few, many, starts):
+    del many
+    slots = few.shape[1]
+    arrived = regroup(few)
+    chip, core = lax.axis_index("tc"), lax.axis_index("core")
+    begin = starts[2 * chip]
+    held = after_of(starts, 2 * chip + 1, total) - begin
+    wanted = jnp.where(core == 0, held - slots - 1, 2 * slots - held)
+    sent = lax.dynamic_slice_in_dim(arrived, jnp.clip(wanted, 0, slots - 1), 1, 1)
+    other = lax.ppermute(sent, "core", [(0, 1), (1, 0)])
+    return unpack(total, starts, arrived, other)
+
+
+def send_many(total, few, many, starts):
+    del few
+    arrived = regroup(many)
+    return unpack(total, starts, arrived, arrived[:, :1])
 
 
 def on_device(latent, group_start, norm_gain, conv_weight, conv_bias):
@@ -216,17 +263,23 @@
     gain = norm_gain.reshape(1, -1)
     bias = conv_bias.reshape(1, -1)
     pairs = [(r, (r + 1) % rows if r % 2 else (r - 1) % rows) for r in range(rows)]
-    cut = total * 5 // 8
-    front, rest = lax.optimization_barrier((own[:cut], own))
-    back, rest = lax.optimization_barrier((rest[cut:], rest))
+    cut = total * 11 // 16
+    front, own = lax.optimization_barrier((own[:cut], own))
     early_far = lax.ppermute(front, ("ha", "tc", "core"), pairs)
-    late_far = lax.ppermute(back, ("ha", "tc", "core"), pairs)
-    twin = lax.ppermute(rest, "core", [(0, 1), (1, 0)])
+    late_far = lax.ppermute(own[cut:], ("ha", "tc", "core"), pairs)
+    twin = lax.ppermute(own, "core", [(0, 1), (1, 0)])
     partial = near_rows(own, twin, conv_weight, gain, bias)
     early = early_rows(early_far, partial, conv_weight, gain)
-    packed = late_rows(group_start, early_far, late_far, early, partial, conv_weight, gain)
-    arrived = lax.all_to_all(packed, ("tc", "core"), split_axis=0, concat_axis=0, tiled=True)
-    return unpack(total, group_start, arrived)
+    bounds = jnp.append(group_start[:: lax.axis_size("core")], total)
+    fits = jnp.all(bounds[1:] - bounds[:-1] <= 2 * (FMAX - 1)).astype(jnp.int32).reshape(1)
+    few, many = late_rows(
+        fits, group_start, early_far, late_far, early, partial, conv_weight, gain
+    )
+    return lax.switch(
+        fits[0],
+        [functools.partial(send_many, total), functools.partial(send_few, total)],
+        few, many, group_start,
+    )
 
 
 def solution(mesh):

time: 78.1 us -> 79.5 us (1.018)
  waiting for transfers between devices: 7.32 us -> 3.94 us
  local copies, waits for them, and re-layouts: 5.63 us -> 7.4 us
  Pallas kernels: 21 us -> 22.3 us
  other arithmetic: 0 us -> 0.86 us
    ppermute x1, waiting for transfers between devices: 5.81 us -> 3.65 us  [on_device(): early_far = lax.ppermute(front, ('ha', 'tc', 'core'), pairs)]
    slice x2 -> x4, local copies, waits for them, and re-layouts: 2.35 us -> 4.12 us  [the longest x1 2.2 us: on_device(): front, own = lax.optimization_barrier((own[:cut], own))]
    ppermute x2, waiting for transfers between devices: 1.51 us -> 0.3 us  [the longest x1 0.29 us: on_device(): late_far = lax.ppermute(own[cut:], ('ha', 'tc', 'core'), pairs)]
    pallas_call x1, Pallas kernels: 3.25 us -> 4.11 us  [late_rows(): pl.pallas_call(late_kernel, out_shape=[jax.ShapeDtypeStruct((starts.shape...]
  transfers between devices with their start and end apart: 3 -> 3, of which waited for: 2 -> 2; matrix products, arithmetic and copies ran while one was open for 0% -> 3% of each run, Pallas kernels for 20% -> 20%
where the time goes in v8:
time: 79.5 us; the launch traced here: 79.2 us
  blocking collectives  38.9 us (49%)
  Pallas kernels  22.3 us (28%)
  local copies, waits for them, and re-layouts  7.4 us (9%)
  starting transfers between devices  4.99 us (6%)
  waiting for transfers between devices  3.94 us (5%)
  other arithmetic  0.86 us (1%)
    all_to_all x1, blocking collectives, regroup(): lax.all_to_all(packed, ('tc', 'core'), split_axis=0, concat_axis=0, tiled...  38.9 us
    pallas_call x1, Pallas kernels, near_rows(): pl.pallas_call(near_kernel, out_shape=jax.ShapeDtypeStruct(own.shape, jnp...  11.8 us
    pallas_call x1, Pallas kernels, early_rows(): pl.pallas_call(early_kernel, out_shape=jax.ShapeDtypeStruct(far.shape, jn...  4.28 us
    pallas_call x1, Pallas kernels, late_rows(): pl.pallas_call(late_kernel, out_shape=[jax.ShapeDtypeStruct((starts.shape...  4.11 us
    ppermute x1, waiting for transfers between devices, on_device(): early_far = lax.ppermute(front, ('ha', 'tc', 'core'), pairs)  3.65 us
    ppermute x1, starting transfers between devices, on_device(): early_far = lax.ppermute(front, ('ha', 'tc', 'core'), pairs)  3.58 us
    unnamed x12, local copies, waits for them, and re-layouts  3.27 us
    slice x1, local copies, waits for them, and re-layouts, on_device(): front, own = lax.optimization_barrier((own[:cut], own))  2.2 us
  transfers between devices with their start and end apart: 3, of which 2 were waited for; matrix products, arithmetic and copies ran while one was open for 3% of the time, Pallas kernels for 20%

profile of v8, /device:TPU:1, one launch (start us, length us, event | category | flops | bytes accessed | tf_op | source)
XLA Modules:
  0.0 79.2 jit_solution(5846922659832583294)
XLA Ops:
  0.0 0.0 copy-start.2
  0.0 0.0 copy-start.3
  0.0 0.0 copy-start.4
  0.0 0.0 copy-start.5
  0.0 2.2 %slice_bitcast_fusion = bf16[22,48,384]{2,1,0:T(8,128)(2,1)} fusion(bf16[32,1,48,384]{3,2,0,1:T(8,128)(2,1)} %bitcast.7), kind=kLoop, calls=%fused_computation.1 | loop fusion | bytes 1622016 | tf_op jit(solution)/shard_map/slice | solution.py:267
  2.2 1.4 %collective-permute-start.3 = (bf16[32,48,384]{2,1,0:T(8,128)(2,1)}, bf16[32,48,384]{2,1,0:T(8,128)(2,1)S(1)}, u32[]{:S(2)}, u32[]{:S(2)}) collective-permute-start(bf16[32,48,384]{2,1,0:T(8,128)(2,1)} %bitcast.8), channel_id=1, source_target_pairs={{0,1},{1,0},{2,3},{3,2},{4,5},{5,4},{6,7},{7,6},{8,9},{9,8},{10,11... | collective-permute-start | bytes 3538952 | tf_op jit(solution)/shard_map/ppermute | solution.py:270
  3.6 3.6 %collective-permute-start.1 = (bf16[22,48,384]{2,1,0:T(8,128)(2,1)}, bf16[22,48,384]{2,1,0:T(8,128)(2,1)S(1)}, u32[]{:S(2)}, u32[]{:S(2)}) collective-permute-start(bf16[22,48,384]{2,1,0:T(8,128)(2,1)} %slice_bitcast_fusion), channel_id=1, source_target_pairs={{0,127},{1,2},{2,1},{3,4},{4,3},{5,6},{6,5},{7,8},{8,7},{9,10},{10... | collective-permute-start | bytes 2433032 | tf_op jit(solution)/shard_map/ppermute | solution.py:268
  7.2 1.8 %slice.23 = bf16[10,48,384]{2,1,0:T(8,128)(2,1)} slice(bf16[32,48,384]{2,1,0:T(8,128)(2,1)} %bitcast.9), slice={[22:32], [0:48], [0:384]} | slice | bytes 737280 | tf_op jit(solution)/shard_map/slice | solution.py:269
  9.0 0.0 collective-permute-start.2
  9.0 0.0 copy-done.3
  9.0 0.1 slice.19
  9.1 0.1 pad_add_fusion
  9.2 0.8 compare_reduce_fusion
  10.6 0.0 copy-done.4
  10.6 0.0 copy-done.5
  10.7 0.0 collective-permute-done.3.twin
  10.7 0.0 copy-done.2
  10.7 0.0 copy-start
  10.7 3.3 %copy-done = bf16[3,3,3,384,384]{4,3,2,1,0:T(8,128)(2,1)S(1)} copy-done((bf16[3,3,3,384,384]{4,3,2,1,0:T(8,128)(2,1)S(1)}, bf16[3,3,3,384,384]{4,3,2,1,0:T(8,128)(2,1)}, u32[]{:S(2)}) %copy-start) | copy-done | bytes 7962648
  13.9 0.0 copy-start.1
  13.9 11.8 %shard_map.57.partial = f32[32,48,384]{2,1,0:T(8,128)S(1)} custom-call(bf16[32,48,384]{2,1,0:T(8,128)(2,1)S(1)} %bitcast.10, bf16[32,48,384]{2,1,0:T(8,128)(2,1)S(1)} %collective-permute-done.3.twin, bf16[3,3,3,384,384]{4,3,2,1,0:T(8,128)(2,1)S(1)} %copy-done, f32[1,384]{1,0:T(1,128)S(1)} %reshape.13.gain, f32[1,384]{1,0:T(1,128)S(1)} %reshape.14.bias), custom_call_target="tpu_custom_call" | custom-call | tf_op jit(solution)/shard_map/pallas_call | solution.py:95
  25.7 3.6 %collective-permute-done.1.far.early_far = bf16[22,48,384]{2,1,0:T(8,128)(2,1)S(1)} collective-permute-done((bf16[22,48,384]{2,1,0:T(8,128)(2,1)}, bf16[22,48,384]{2,1,0:T(8,128)(2,1)S(1)}, u32[]{:S(2)}, u32[]{:S(2)}) %collective-permute-start.1) | collective-permute-done | bytes 811040 | tf_op jit(solution)/shard_map/ppermute | solution.py:268
  29.4 0.0 copy-done.1
  29.4 4.3 %shard_map.58.early = bf16[22,48,384]{2,1,0:T(8,128)(2,1)S(1)} custom-call(bf16[22,48,384]{2,1,0:T(8,128)(2,1)S(1)} %collective-permute-done.1.far.early_far, f32[32,48,384]{2,1,0:T(8,128)S(1)} %shard_map.57.partial, bf16[3,3,3,384,384]{4,3,2,1,0:T(8,128)(2,1)S(1)} %copy-done.1, f32[1,384]{1,0:T(1,128)S(1)} %reshape.13.gain), custom_call_target="tpu_custom_call" | custom-call | tf_op jit(solution)/shard_map/pallas_call | solution.py:172
  33.7 0.3 collective-permute-done.2.far
  33.9 4.1 %shard_map.59 = (bf16[16,3,48,384]{3,2,1,0:T(8,128)(2,1)}, bf16[16,4,48,384]{3,2,1,0:T(8,128)(2,1)S(1)}) custom-call(s32[1]{0:T(128)} %bitcast.2.fits, s32[16]{0:T(128)S(1)} %copy-done.3, bf16[22,48,384]{2,1,0:T(8,128)(2,1)S(1)} %collective-permute-done.1.far.early_far, bf16[10,48,384]{2,1,0:T(8,128)(2,1)S(1)} %collective-permute-done.2.far, ...), custom_call_target="tpu_custom_call" | custom-call | tf_op jit(solution)/shard_map/pallas_call | solution.py:184
  38.1 41.2 %conditional.1 = (bf16[4,16,48,384]{3,2,1,0:T(8,128)(2,1)}) conditional(s32[]{:T(128)} %clamp.3, (bf16[16,4,48,384]{3,2,1,0:T(8,128)(2,1)S(1)}, s32[16]{0:T(128)S(1)}) %tuple.20, (bf16[16,3,48,384]{3,2,1,0:T(8,128)(2,1)}, s32[16]{0:T(128)S(1)}) %tuple.21), branch_computations={%region_1.2_spmd, %region_2.3_spmd} | conditional | flops 23 | bytes 8847728 | solution.py:278
  38.1 38.9 %all_to_all.8.arrived = bf16[16,4,48,384]{3,2,1,0:T(8,128)(2,1)S(1)} all-to-all(bf16[16,4,48,384]{3,2,1,0:T(8,128)(2,1)S(1)} %get-tuple-element.17), channel_id=1, replica_groups=mesh['ha'=8,'tc'=8,'core'=2] {'tc','core'}, dimensions={0} | all-to-all | bytes 4718592 | tf_op jit(solution)/shard_map/cond/branch_0_fun/all_to_all | solution.py:237
  77.0 0.1 slice.24.other
  77.0 2.2 %branch_0_fun.1 = bf16[4,16,48,384]{3,2,1,0:T(8,128)(2,1)} custom-call(s32[16]{0:T(128)S(1)} %get-tuple-element.16.starts, bf16[16,4,48,384]{3,2,1,0:T(8,128)(2,1)S(1)} %all_to_all.8.arrived, bf16[16,1,48,384]{3,2,1,0:T(8,128)(2,1)S(1)} %slice.24.other), custom_call_target="tpu_custom_call" | custom-call | tf_op jit(solution)/shard_map/cond/branch_0_fun/pallas_call | solution.py:227
  (2 shorter events, 0.0 us)
Async XLA Ops:
  0.0 10.7 %copy-start.2 = (bf16[32,1,48,384]{3,2,1,0:T(8,128)(2,1)S(1)}, bf16[32,1,48,384]{3,2,1,0:T(8,128)(2,1)}, u32[]{:S(2)}) copy-start(bf16[32,1,48,384]{3,2,1,0:T(8,128)(2,1)} %param.7) | copy-start | bytes 3538948
  0.0 9.0 %copy-start.3 = (s32[16]{0:T(128)S(1)}, s32[16]{0:T(128)}, u32[]{:S(2)}) copy-start(s32[16]{0:T(128)} %starts.1) | copy-start | bytes 196
  0.0 10.6 %copy-start.4 = (f32[384]{0:T(512)S(1)}, f32[384]{0:T(512)}, u32[]{:S(2)}) copy-start(f32[384]{0:T(512)} %param.9) | copy-start | bytes 4612
  0.0 10.6 %copy-start.5 = (f32[384]{0:T(512)S(1)}, f32[384]{0:T(512)}, u32[]{:S(2)}) copy-start(f32[384]{0:T(512)} %param.11) | copy-start | bytes 4612
  2.2 8.4 %collective-permute-start.3 = (bf16[32,48,384]{2,1,0:T(8,128)(2,1)}, bf16[32,48,384]{2,1,0:T(8,128)(2,1)S(1)}, u32[]{:S(2)}, u32[]{:S(2)}) collective-permute-start(bf16[32,48,384]{2,1,0:T(8,128)(2,1)} %bitcast.8), channel_id=1, source_target_pairs={{0,1},{1,0},{2,3},{3,2},{4,5},{5,4},{6,7},{7,6},{8,9},{9,8},{10,11... | collective-permute-start | bytes 3538952 | tf_op jit(solution)/shard_map/ppermute | solution.py:270
  3.6 25.7 %collective-permute-start.1 = (bf16[22,48,384]{2,1,0:T(8,128)(2,1)}, bf16[22,48,384]{2,1,0:T(8,128)(2,1)S(1)}, u32[]{:S(2)}, u32[]{:S(2)}) collective-permute-start(bf16[22,48,384]{2,1,0:T(8,128)(2,1)} %slice_bitcast_fusion), channel_id=1, source_target_pairs={{0,127},{1,2},{2,1},{3,4},{4,3},{5,6},{6,5},{7,8},{8,7},{9,10},{10... | collective-permute-start | bytes 2433032 | tf_op jit(solution)/shard_map/ppermute | solution.py:268
  9.0 25.0 %collective-permute-start.2 = (bf16[10,48,384]{2,1,0:T(8,128)(2,1)}, bf16[10,48,384]{2,1,0:T(8,128)(2,1)S(1)}, u32[]{:S(2)}, u32[]{:S(2)}) collective-permute-start(bf16[10,48,384]{2,1,0:T(8,128)(2,1)} %slice.23), channel_id=1, source_target_pairs={{0,127},{1,2},{2,1},{3,4},{4,3},{5,6},{6,5},{7,8},{8,7},{9,10},{10... | collective-permute-start | bytes 1105928 | tf_op jit(solution)/shard_map/ppermute | solution.py:269
  10.7 3.3 %copy-start = (bf16[3,3,3,384,384]{4,3,2,1,0:T(8,128)(2,1)S(1)}, bf16[3,3,3,384,384]{4,3,2,1,0:T(8,128)(2,1)}, u32[]{:S(2)}) copy-start(bf16[3,3,3,384,384]{4,3,2,1,0:T(8,128)(2,1)} %weight.5) | copy-start | bytes 23887876
  13.9 15.4 %copy-start.1 = (bf16[3,3,3,384,384]{4,3,2,1,0:T(8,128)(2,1)S(1)}, bf16[3,3,3,384,384]{4,3,2,1,0:T(8,128)(2,1)}, u32[]{:S(2)}) copy-start(bf16[3,3,3,384,384]{4,3,2,1,0:T(8,128)(2,1)} %weight.5) | copy-start | bytes 23887876

commit v9 on v8

--- a/solution.py
+++ b/solution.py
@@ -10,7 +10,8 @@
 FMAX = 4
 HIST = 2
 STEP = 8
-VMEM_BYTES = 30 * 2**20
+NEAR_VMEM_BYTES = 14 * 2**20
+FAR_VMEM_BYTES = 20 * 2**20
 UNPACK_VMEM_BYTES = 8 * 2**20
 SMEM_SPEC = pl.BlockSpec(memory_space=pltpu.SMEM)
 VMEM_SPEC = pl.BlockSpec(memory_space=pltpu.VMEM)
@@ -102,7 +103,7 @@
             pltpu.VMEM((HIST + total, cols, chans), jnp.bfloat16),
             pltpu.VMEM((3, STEP, cols + 16, chans), jnp.float32),
         ],
-        compiler_params=pltpu.CompilerParams(vmem_limit_bytes=VMEM_BYTES),
+        compiler_params=pltpu.CompilerParams(vmem_limit_bytes=NEAR_VMEM_BYTES),
     )(own, twin, weight, gain, bias)
 
 
@@ -175,7 +176,7 @@
         in_specs=[VMEM_SPEC] * 4,
         out_specs=VMEM_SPEC,
         scratch_shapes=far_scratch(*far.shape),
-        compiler_params=pltpu.CompilerParams(vmem_limit_bytes=VMEM_BYTES),
+        compiler_params=pltpu.CompilerParams(vmem_limit_bytes=FAR_VMEM_BYTES),
     )(far, partial, weight, gain)
 
 
@@ -191,7 +192,7 @@
         out_specs=[VMEM_SPEC] * 2,
         scratch_shapes=far_scratch(*far.shape)
         + [pltpu.VMEM((total + FMAX, cols, chans), jnp.bfloat16)],
-        compiler_params=pltpu.CompilerParams(vmem_limit_bytes=VMEM_BYTES),
+        compiler_params=pltpu.CompilerParams(vmem_limit_bytes=FAR_VMEM_BYTES),
     )(fits, starts, early_far, far, early, partial, weight, gain)
 
 
@@ -263,7 +264,7 @@
     gain = norm_gain.reshape(1, -1)
     bias = conv_bias.reshape(1, -1)
     pairs = [(r, (r + 1) % rows if r % 2 else (r - 1) % rows) for r in range(rows)]
-    cut = total * 11 // 16
+    cut = total * 5 // 8
     front, own = lax.optimization_barrier((own[:cut], own))
     early_far = lax.ppermute(front, ("ha", "tc", "core"), pairs)
     late_far = lax.ppermute(own[cut:], ("ha", "tc", "core"), pairs)

time: 79.5 us -> 75.8 us (0.953)
  blocking collectives: 38.9 us -> 0 us
  waiting for transfers between devices: 3.94 us -> 28.9 us
  starting transfers between devices: 4.99 us -> 13.3 us
  loops' own time: 0.01 us -> 1.34 us
    all_to_all x1 -> x0, blocking collectives: 38.9 us -> none  [regroup(): lax.all_to_all(packed, ('tc', 'core'), split_axis=0, concat_axis=0, tiled...]
    all_to_all x0 -> x1, waiting for transfers between devices: none -> 23 us  [regroup(): lax.all_to_all(packed, ('tc', 'core'), split_axis=0, concat_axis=0, tiled...]
    all_to_all x0 -> x1, starting transfers between devices: none -> 7.39 us  [regroup(): lax.all_to_all(packed, ('tc', 'core'), split_axis=0, concat_axis=0, tiled...]
    ppermute x0 -> x1, waiting for transfers between devices: none -> 1.63 us  [send_few(): other = lax.ppermute(sent, 'core', [(0, 1), (1, 0)])]
    another operation x1, loops' own time: 0.01 us -> 1.34 us  [on_device(): lax.switch(fits[0], [functools.partial(send_many, total), functools.parti...]
    ppermute x1, waiting for transfers between devices: 0.29 us -> 1.47 us  [on_device(): late_far = lax.ppermute(own[cut:], ('ha', 'tc', 'core'), pairs)]
    ppermute x0 -> x1, starting transfers between devices: none -> 0.95 us  [send_few(): other = lax.ppermute(sent, 'core', [(0, 1), (1, 0)])]
    ppermute x1, waiting for transfers between devices: 3.65 us -> 2.85 us  [on_device(): early_far = lax.ppermute(front, ('ha', 'tc', 'core'), pairs)]
  transfers between devices with their start and end apart: 3 -> 5, of which waited for: 2 -> 4; matrix products, arithmetic and copies ran while one was open for 3% -> 4% of each run, Pallas kernels for 20% -> 21%
where the time goes in v9:
time: 75.8 us; the launch traced here: 75.5 us
  waiting for transfers between devices  28.9 us (38%)
  Pallas kernels  22.3 us (29%)
  starting transfers between devices  13.3 us (18%)
  local copies, waits for them, and re-layouts  8.05 us (11%)
  loops' own time  1.34 us (2%)
  other arithmetic  0.82 us (1%)
    all_to_all x1, waiting for transfers between devices, regroup(): lax.all_to_all(packed, ('tc', 'core'), split_axis=0, concat_axis=0, tiled...  23 us
    pallas_call x1, Pallas kernels, near_rows(): pl.pallas_call(near_kernel, out_shape=jax.ShapeDtypeStruct(own.shape, jnp...  11.8 us
    all_to_all x1, starting transfers between devices, regroup(): lax.all_to_all(packed, ('tc', 'core'), split_axis=0, concat_axis=0, tiled...  7.39 us
    pallas_call x1, Pallas kernels, late_rows(): pl.pallas_call(late_kernel, out_shape=[jax.ShapeDtypeStruct((starts.shape...  4.44 us
    pallas_call x1, Pallas kernels, early_rows(): pl.pallas_call(early_kernel, out_shape=jax.ShapeDtypeStruct(far.shape, jn...  3.89 us
    ppermute x1, starting transfers between devices, on_device(): early_far = lax.ppermute(front, ('ha', 'tc', 'core'), pairs)  3.58 us
    unnamed x12, local copies, waits for them, and re-layouts  3.27 us
    ppermute x1, waiting for transfers between devices, on_device(): early_far = lax.ppermute(front, ('ha', 'tc', 'core'), pairs)  2.85 us
  transfers between devices with their start and end apart: 5, of which 4 were waited for; matrix products, arithmetic and copies ran while one was open for 4% of the time, Pallas kernels for 21%

profile of v9, /device:TPU:1, one launch (start us, length us, event | category | flops | bytes accessed | tf_op | source)
XLA Modules:
  0.0 75.5 jit_solution(8763438483309403064)
XLA Ops:
  0.0 0.0 copy-start.2
  0.0 0.0 copy-start.3
  0.0 0.0 copy-start.4
  0.0 0.0 copy-start.5
  0.0 2.1 %slice_bitcast_fusion = bf16[20,48,384]{2,1,0:T(8,128)(2,1)} fusion(bf16[32,1,48,384]{3,2,0,1:T(8,128)(2,1)} %bitcast.7), kind=kLoop, calls=%fused_computation.1 | loop fusion | bytes 1474560 | tf_op jit(solution)/shard_map/slice | solution.py:268
  2.2 1.4 %collective-permute-start.3 = (bf16[32,48,384]{2,1,0:T(8,128)(2,1)}, bf16[32,48,384]{2,1,0:T(8,128)(2,1)S(1)}, u32[]{:S(2)}, u32[]{:S(2)}) collective-permute-start(bf16[32,48,384]{2,1,0:T(8,128)(2,1)} %bitcast.8), channel_id=1, source_target_pairs={{0,1},{1,0},{2,3},{3,2},{4,5},{5,4},{6,7},{7,6},{8,9},{9,8},{10,11... | collective-permute-start | bytes 3538952 | tf_op jit(solution)/shard_map/ppermute | solution.py:271
  3.6 3.6 %collective-permute-start.1 = (bf16[20,48,384]{2,1,0:T(8,128)(2,1)}, bf16[20,48,384]{2,1,0:T(8,128)(2,1)S(1)}, u32[]{:S(2)}, u32[]{:S(2)}) collective-permute-start(bf16[20,48,384]{2,1,0:T(8,128)(2,1)} %slice_bitcast_fusion), channel_id=1, source_target_pairs={{0,127},{1,2},{2,1},{3,4},{4,3},{5,6},{6,5},{7,8},{8,7},{9,10},{10... | collective-permute-start | bytes 2211848 | tf_op jit(solution)/shard_map/ppermute | solution.py:269
  7.2 1.8 %slice.23 = bf16[12,48,384]{2,1,0:T(8,128)(2,1)} slice(bf16[32,48,384]{2,1,0:T(8,128)(2,1)} %bitcast.9), slice={[20:32], [0:48], [0:384]} | slice | bytes 884736 | tf_op jit(solution)/shard_map/slice | solution.py:270
  9.0 0.0 collective-permute-start.2
  9.0 0.0 copy-done.3
  9.0 0.1 slice.19
  9.1 0.1 pad_add_fusion
  9.2 0.7 compare_reduce_fusion
  10.5 0.0 copy-done.4
  10.6 0.0 copy-done.5
  10.6 0.0 collective-permute-done.3.twin
  10.6 0.0 copy-done.2
  10.6 0.0 copy-start
  10.6 3.3 %copy-done = bf16[3,3,3,384,384]{4,3,2,1,0:T(8,128)(2,1)S(1)} copy-done((bf16[3,3,3,384,384]{4,3,2,1,0:T(8,128)(2,1)S(1)}, bf16[3,3,3,384,384]{4,3,2,1,0:T(8,128)(2,1)}, u32[]{:S(2)}) %copy-start) | copy-done | bytes 7962648
  13.9 0.0 copy-start.1
  13.9 11.8 %shard_map.57.partial = f32[32,48,384]{2,1,0:T(8,128)S(1)} custom-call(bf16[32,48,384]{2,1,0:T(8,128)(2,1)S(1)} %bitcast.10, bf16[32,48,384]{2,1,0:T(8,128)(2,1)S(1)} %collective-permute-done.3.twin, bf16[3,3,3,384,384]{4,3,2,1,0:T(8,128)(2,1)S(1)} %copy-done, f32[1,384]{1,0:T(1,128)S(1)} %reshape.13.gain, f32[1,384]{1,0:T(1,128)S(1)} %reshape.14.bias), custom_call_target="tpu_custom_call" | custom-call | tf_op jit(solution)/shard_map/pallas_call | solution.py:96
  25.7 2.8 %collective-permute-done.1.far.early_far = bf16[20,48,384]{2,1,0:T(8,128)(2,1)S(1)} collective-permute-done((bf16[20,48,384]{2,1,0:T(8,128)(2,1)}, bf16[20,48,384]{2,1,0:T(8,128)(2,1)S(1)}, u32[]{:S(2)}, u32[]{:S(2)}) %collective-permute-start.1) | collective-permute-done | bytes 737312 | tf_op jit(solution)/shard_map/ppermute | solution.py:269
  28.5 0.0 copy-done.1
  28.5 3.9 %shard_map.58.early = bf16[20,48,384]{2,1,0:T(8,128)(2,1)S(1)} custom-call(bf16[20,48,384]{2,1,0:T(8,128)(2,1)S(1)} %collective-permute-done.1.far.early_far, f32[32,48,384]{2,1,0:T(8,128)S(1)} %shard_map.57.partial, bf16[3,3,3,384,384]{4,3,2,1,0:T(8,128)(2,1)S(1)} %copy-done.1, f32[1,384]{1,0:T(1,128)S(1)} %reshape.13.gain), custom_call_target="tpu_custom_call" | custom-call | tf_op jit(solution)/shard_map/pallas_call | solution.py:173
  32.4 1.5 %collective-permute-done.2.far = bf16[12,48,384]{2,1,0:T(8,128)(2,1)S(1)} collective-permute-done((bf16[12,48,384]{2,1,0:T(8,128)(2,1)}, bf16[12,48,384]{2,1,0:T(8,128)(2,1)S(1)}, u32[]{:S(2)}, u32[]{:S(2)}) %collective-permute-start.2) | collective-permute-done | bytes 442400 | tf_op jit(solution)/shard_map/ppermute | solution.py:270
  33.9 4.4 %shard_map.59 = (bf16[16,3,48,384]{3,2,1,0:T(8,128)(2,1)}, bf16[16,4,48,384]{3,2,1,0:T(8,128)(2,1)S(1)}) custom-call(s32[1]{0:T(128)} %bitcast.2.fits, s32[16]{0:T(128)S(1)} %copy-done.3, bf16[20,48,384]{2,1,0:T(8,128)(2,1)S(1)} %collective-permute-done.1.far.early_far, bf16[12,48,384]{2,1,0:T(8,128)(2,1)S(1)} %collective-permute-done.2.far, ...), custom_call_target="tpu_custom_call" | custom-call | tf_op jit(solution)/shard_map/pallas_call | solution.py:185
  38.3 37.2 %conditional.1 = (bf16[4,16,48,384]{3,2,1,0:T(8,128)(2,1)}) conditional(s32[]{:T(128)} %clamp.3, (bf16[16,4,48,384]{3,2,1,0:T(8,128)(2,1)S(1)}, s32[16]{0:T(128)S(1)}) %tuple.20, (bf16[16,3,48,384]{3,2,1,0:T(8,128)(2,1)}, s32[16]{0:T(128)S(1)}) %tuple.21), branch_computations={%region_1.2_spmd, %region_2.3_spmd} | conditional | flops 23 | bytes 8847728 | solution.py:279
  38.3 7.4 %all-to-all-start.1 = ((bf16[16,3,48,384]{3,2,1,0:T(8,128)(2,1)}), bf16[16,3,48,384]{3,2,1,0:T(8,128)(2,1)S(1)}, u32[]{:S(2)}, u32[]{:S(2)}) async-start(bf16[16,3,48,384]{3,2,1,0:T(8,128)(2,1)} %get-tuple-element.19), calls=%async_computation.1 | async-start | bytes 3538944 | tf_op jit(solution)/shard_map/cond/branch_1_fun/all_to_all | solution.py:238
  45.7 0.6 fusion
  47.7 23.0 %all-to-all-done.1.arrived = bf16[16,3,48,384]{3,2,1,0:T(8,128)(2,1)S(1)} async-done(((bf16[16,3,48,384]{3,2,1,0:T(8,128)(2,1)}), bf16[16,3,48,384]{3,2,1,0:T(8,128)(2,1)S(1)}, u32[]{:S(2)}, u32[]{:S(2)}) %all-to-all-start.1) | async-done | bytes 1769504 | tf_op jit(solution)/shard_map/cond/branch_1_fun/all_to_all | solution.py:238
  70.6 0.1 constant_dynamic-slice_fusion
  70.7 1.0 %collective-permute-start = (bf16[16,1,48,384]{3,2,1,0:T(8,128)(2,1)S(1)}, bf16[16,1,48,384]{3,2,1,0:T(8,128)(2,1)S(1)}, u32[]{:S(2)}, u32[]{:S(2)}) collective-permute-start(bf16[16,1,48,384]{3,2,1,0:T(8,128)(2,1)S(1)} %constant_dynamic-slice_fusion), channel_id=1, source_target_pairs={{0,1},{1,0},{2,3},{3,2},{4,5},{5,4},{6,7},{7,6},{8,9},{9,8},{10,11... | collective-permute-start | bytes 1769480 | tf_op jit(solution)/shard_map/cond/branch_1_fun/ppermute | solution.py:250
  71.7 1.6 %collective-permute-done.other = bf16[16,1,48,384]{3,2,1,0:T(8,128)(2,1)S(1)} collective-permute-done((bf16[16,1,48,384]{3,2,1,0:T(8,128)(2,1)S(1)}, bf16[16,1,48,384]{3,2,1,0:T(8,128)(2,1)S(1)}, u32[]{:S(2)}, u32[]{:S(2)}) %collective-permute-start) | collective-permute-done | bytes 589856 | tf_op jit(solution)/shard_map/cond/branch_1_fun/ppermute | solution.py:250
  73.3 2.2 %branch_1_fun.1 = bf16[4,16,48,384]{3,2,1,0:T(8,128)(2,1)} custom-call(s32[16]{0:T(128)S(1)} %get-tuple-element.18.starts, bf16[16,3,48,384]{3,2,1,0:T(8,128)(2,1)S(1)} %all-to-all-done.1.arrived, bf16[16,1,48,384]{3,2,1,0:T(8,128)(2,1)S(1)} %collective-permute-done.other), custom_call_target="tpu_custom_call" | custom-call | tf_op jit(solution)/shard_map/cond/branch_1_fun/pallas_call | solution.py:228
  (2 shorter events, 0.0 us)
Async XLA Ops:
  0.0 10.6 %copy-start.2 = (bf16[32,1,48,384]{3,2,1,0:T(8,128)(2,1)S(1)}, bf16[32,1,48,384]{3,2,1,0:T(8,128)(2,1)}, u32[]{:S(2)}) copy-start(bf16[32,1,48,384]{3,2,1,0:T(8,128)(2,1)} %param.7) | copy-start | bytes 3538948
  0.0 9.0 %copy-start.3 = (s32[16]{0:T(128)S(1)}, s32[16]{0:T(128)}, u32[]{:S(2)}) copy-start(s32[16]{0:T(128)} %starts.1) | copy-start | bytes 196
  0.0 10.5 %copy-start.4 = (f32[384]{0:T(512)S(1)}, f32[384]{0:T(512)}, u32[]{:S(2)}) copy-start(f32[384]{0:T(512)} %param.9) | copy-start | bytes 4612
  0.0 10.6 %copy-start.5 = (f32[384]{0:T(512)S(1)}, f32[384]{0:T(512)}, u32[]{:S(2)}) copy-start(f32[384]{0:T(512)} %param.11) | copy-start | bytes 4612
  2.2 8.4 %collective-permute-start.3 = (bf16[32,48,384]{2,1,0:T(8,128)(2,1)}, bf16[32,48,384]{2,1,0:T(8,128)(2,1)S(1)}, u32[]{:S(2)}, u32[]{:S(2)}) collective-permute-start(bf16[32,48,384]{2,1,0:T(8,128)(2,1)} %bitcast.8), channel_id=1, source_target_pairs={{0,1},{1,0},{2,3},{3,2},{4,5},{5,4},{6,7},{7,6},{8,9},{9,8},{10,11... | collective-permute-start | bytes 3538952 | tf_op jit(solution)/shard_map/ppermute | solution.py:271
  3.6 24.9 %collective-permute-start.1 = (bf16[20,48,384]{2,1,0:T(8,128)(2,1)}, bf16[20,48,384]{2,1,0:T(8,128)(2,1)S(1)}, u32[]{:S(2)}, u32[]{:S(2)}) collective-permute-start(bf16[20,48,384]{2,1,0:T(8,128)(2,1)} %slice_bitcast_fusion), channel_id=1, source_target_pairs={{0,127},{1,2},{2,1},{3,4},{4,3},{5,6},{6,5},{7,8},{8,7},{9,10},{10... | collective-permute-start | bytes 2211848 | tf_op jit(solution)/shard_map/ppermute | solution.py:269
  9.0 24.9 %collective-permute-start.2 = (bf16[12,48,384]{2,1,0:T(8,128)(2,1)}, bf16[12,48,384]{2,1,0:T(8,128)(2,1)S(1)}, u32[]{:S(2)}, u32[]{:S(2)}) collective-permute-start(bf16[12,48,384]{2,1,0:T(8,128)(2,1)} %slice.23), channel_id=1, source_target_pairs={{0,127},{1,2},{2,1},{3,4},{4,3},{5,6},{6,5},{7,8},{8,7},{9,10},{10... | collective-permute-start | bytes 1327112 | tf_op jit(solution)/shard_map/ppermute | solution.py:270
  10.6 3.3 %copy-start = (bf16[3,3,3,384,384]{4,3,2,1,0:T(8,128)(2,1)S(1)}, bf16[3,3,3,384,384]{4,3,2,1,0:T(8,128)(2,1)}, u32[]{:S(2)}) copy-start(bf16[3,3,3,384,384]{4,3,2,1,0:T(8,128)(2,1)} %weight.5) | copy-start | bytes 23887876
  13.9 14.6 %copy-start.1 = (bf16[3,3,3,384,384]{4,3,2,1,0:T(8,128)(2,1)S(1)}, bf16[3,3,3,384,384]{4,3,2,1,0:T(8,128)(2,1)}, u32[]{:S(2)}) copy-start(bf16[3,3,3,384,384]{4,3,2,1,0:T(8,128)(2,1)} %weight.5) | copy-start | bytes 23887876
  38.3 32.3 %all-to-all-start.1 = ((bf16[16,3,48,384]{3,2,1,0:T(8,128)(2,1)}), bf16[16,3,48,384]{3,2,1,0:T(8,128)(2,1)S(1)}, u32[]{:S(2)}, u32[]{:S(2)}) async-start(bf16[16,3,48,384]{3,2,1,0:T(8,128)(2,1)} %get-tuple-element.19), calls=%async_computation.1 | async-start | bytes 3538944 | tf_op jit(solution)/shard_map/cond/branch_1_fun/all_to_all | solution.py:238
  70.7 2.6 %collective-permute-start = (bf16[16,1,48,384]{3,2,1,0:T(8,128)(2,1)S(1)}, bf16[16,1,48,384]{3,2,1,0:T(8,128)(2,1)S(1)}, u32[]{:S(2)}, u32[]{:S(2)}) collective-permute-start(bf16[16,1,48,384]{3,2,1,0:T(8,128)(2,1)S(1)} %constant_dynamic-slice_fusion), channel_id=1, source_target_pairs={{0,1},{1,0},{2,3},{3,2},{4,5},{5,4},{6,7},{7,6},{8,9},{9,8},{10,11... | collective-permute-start | bytes 1769480 | tf_op jit(solution)/shard_map/cond/branch_1_fun/ppermute | solution.py:250

commit v10 on v9

--- a/solution.py
+++ b/solution.py
@@ -64,9 +64,17 @@
     sums[2, :, cols + 8 : cols + 9, :] = jnp.zeros(shape, jnp.float32)
 
 
-def near_kernel(own, twin, weight, gain, bias, partial, own_act, twin_act, sums):
+def near_kernel(
+    starts, own, twin, weight, gain, bias, partial, fits, own_act, twin_act, sums
+):
     total, cols, _ = own.shape
     core = lax.axis_index("core")
+    groups = starts.shape[0]
+    most = functools.reduce(
+        jnp.maximum,
+        [after_of(starts, j + 1, total) - starts[j] for j in range(0, groups, 2)],
+    )
+    fits[0] = (most <= 2 * (FMAX - 1)).astype(jnp.int32)
     clear_sides(sums, cols)
     for act in (own_act, twin_act):
         act[pl.ds(0, HIST)] = jnp.zeros((HIST,) + act.shape[1:], act.dtype)
@@ -91,20 +99,23 @@
     lax.fori_loop(0, total // STEP, step, 0)
 
 
-def near_rows(own, twin, weight, gain, bias):
+def near_rows(starts, own, twin, weight, gain, bias):
     total, cols, chans = own.shape
     return pl.pallas_call(
         near_kernel,
-        out_shape=jax.ShapeDtypeStruct(own.shape, jnp.float32),
-        in_specs=[VMEM_SPEC] * 5,
-        out_specs=VMEM_SPEC,
+        out_shape=[
+            jax.ShapeDtypeStruct(own.shape, jnp.float32),
+            jax.ShapeDtypeStruct((1,), jnp.int32),
+        ],
+        in_specs=[SMEM_SPEC] + [VMEM_SPEC] * 5,
+        out_specs=[VMEM_SPEC, SMEM_SPEC],
         scratch_shapes=[
             pltpu.VMEM((HIST + total, cols, chans), jnp.bfloat16),
             pltpu.VMEM((HIST + total, cols, chans), jnp.bfloat16),
             pltpu.VMEM((3, STEP, cols + 16, chans), jnp.float32),
         ],
         compiler_params=pltpu.CompilerParams(vmem_limit_bytes=NEAR_VMEM_BYTES),
-    )(own, twin, weight, gain, bias)
+    )(starts, own, twin, weight, gain, bias)
 
 
 def far_frames(begin, far, recent, partial, weight, gain, act, sums):
@@ -238,16 +249,30 @@
     return lax.all_to_all(packed, ("tc", "core"), split_axis=0, concat_axis=0, tiled=True)
 
 
+def pick_kernel(total, starts, arrived, sent):
+    slots = arrived.shape[1]
+    core = lax.axis_index("core")
+    group = lax.axis_index("tc") * lax.axis_size("core")
+    held = after_of(starts, group + 1, total) - starts[group]
+    wanted = jnp.where(core == 0, held - slots - 1, 2 * slots - held)
+    sent[:, 0] = arrived[:, jnp.clip(wanted, 0, slots - 1)]
+
+
+def pick(total, starts, arrived):
+    rows, _, cols, chans = arrived.shape
+    return pl.pallas_call(
+        functools.partial(pick_kernel, total),
+        out_shape=jax.ShapeDtypeStruct((rows, 1, cols, chans), arrived.dtype),
+        in_specs=[SMEM_SPEC, VMEM_SPEC],
+        out_specs=VMEM_SPEC,
+        compiler_params=pltpu.CompilerParams(vmem_limit_bytes=UNPACK_VMEM_BYTES),
+    )(starts, arrived)
+
+
 def send_few(total, few, many, starts):
     del many
-    slots = few.shape[1]
     arrived = regroup(few)
-    chip, core = lax.axis_index("tc"), lax.axis_index("core")
-    begin = starts[2 * chip]
-    held = after_of(starts, 2 * chip + 1, total) - begin
-    wanted = jnp.where(core == 0, held - slots - 1, 2 * slots - held)
-    sent = lax.dynamic_slice_in_dim(arrived, jnp.clip(wanted, 0, slots - 1), 1, 1)
-    other = lax.ppermute(sent, "core", [(0, 1), (1, 0)])
+    other = lax.ppermute(pick(total, starts, arrived), "core", [(0, 1), (1, 0)])
     return unpack(total, starts, arrived, other)
 
 
@@ -269,10 +294,8 @@
     early_far = lax.ppermute(front, ("ha", "tc", "core"), pairs)
     late_far = lax.ppermute(own[cut:], ("ha", "tc", "core"), pairs)
     twin = lax.ppermute(own, "core", [(0, 1), (1, 0)])
-    partial = near_rows(own, twin, conv_weight, gain, bias)
+    partial, fits = near_rows(group_start, own, twin, conv_weight, gain, bias)
     early = early_rows(early_far, partial, conv_weight, gain)
-    bounds = jnp.append(group_start[:: lax.axis_size("core")], total)
-    fits = jnp.all(bounds[1:] - bounds[:-1] <= 2 * (FMAX - 1)).astype(jnp.int32).reshape(1)
     few, many = late_rows(
         fits, group_start, early_far, late_far, early, partial, conv_weight, gain
     )

time: 75.8 us -> 75.1 us (level)
  blocking collectives: 0 us -> 32.3 us
  waiting for transfers between devices: 28.9 us -> 7.04 us
  starting transfers between devices: 13.3 us -> 5.74 us
  loops' own time: 1.34 us -> 0.03 us
  local copies, waits for them, and re-layouts: 8.05 us -> 7.02 us
  other arithmetic: 0.82 us -> 0 us
    all_to_all x0 -> x1, blocking collectives: none -> 32.3 us  [regroup(): lax.all_to_all(packed, ('tc', 'core'), split_axis=0, concat_axis=0, tiled...]
    all_to_all x1 -> x0, waiting for transfers between devices: 23 us -> none  [regroup(): lax.all_to_all(packed, ('tc', 'core'), split_axis=0, concat_axis=0, tiled...]
    all_to_all x1 -> x0, starting transfers between devices: 7.39 us -> none  [regroup(): lax.all_to_all(packed, ('tc', 'core'), split_axis=0, concat_axis=0, tiled...]
    pallas_call x1 -> x2, Pallas kernels: 11.8 us -> 13.3 us  [the longest x1 12.7 us: near_rows(): pl.pallas_call(near_kernel, out_shape=[jax.ShapeDtypeStruct(own.shape, jn...]
    pallas_call x1, Pallas kernels: 2.22 us -> 0.82 us  [unpack(): pl.pallas_call(functools.partial(unpack_kernel, total), out_shape=jax.Sha...]
    unnamed x12 -> x14, local copies, waits for them, and re-layouts: 3.27 us -> 4.67 us
    another operation x1, loops' own time: 1.34 us -> 0.03 us  [on_device(): lax.switch(fits[0], [functools.partial(send_many, total), functools.parti...]
    ppermute x1, waiting for transfers between devices: 2.85 us -> 3.9 us  [on_device(): early_far = lax.ppermute(front, ('ha', 'tc', 'core'), pairs)]
  transfers between devices with their start and end apart: 5 -> 4, of which waited for: 4 -> 3; matrix products, arithmetic and copies ran while one was open for 4% -> 1% of each run, Pallas kernels for 21% -> 22%
where the time goes in v10:
time: 75.1 us; the launch traced here: 74.8 us
  blocking collectives  32.3 us (43%)
  Pallas kernels  21.9 us (29%)
  waiting for transfers between devices  7.04 us (9%)
  local copies, waits for them, and re-layouts  7.02 us (9%)
  starting transfers between devices  5.74 us (8%)
  between operations  0.77 us (1%)
    all_to_all x1, blocking collectives, regroup(): lax.all_to_all(packed, ('tc', 'core'), split_axis=0, concat_axis=0, tiled...  32.3 us
    pallas_call x1, Pallas kernels, near_rows(): pl.pallas_call(near_kernel, out_shape=[jax.ShapeDtypeStruct(own.shape, jn...  12.7 us
    unnamed x14, local copies, waits for them, and re-layouts  4.67 us
    pallas_call x1, Pallas kernels, early_rows(): pl.pallas_call(early_kernel, out_shape=jax.ShapeDtypeStruct(far.shape, jn...  3.96 us
    ppermute x1, waiting for transfers between devices, on_device(): early_far = lax.ppermute(front, ('ha', 'tc', 'core'), pairs)  3.9 us
    pallas_call x1, Pallas kernels, late_rows(): pl.pallas_call(late_kernel, out_shape=[jax.ShapeDtypeStruct((starts.shape...  3.86 us
    ppermute x1, starting transfers between devices, on_device(): early_far = lax.ppermute(front, ('ha', 'tc', 'core'), pairs)  3.67 us
    ppermute x1, waiting for transfers between devices, send_few(): other = lax.ppermute(pick(total, starts, arrived), 'core', [(0, 1), (1, 0)])  1.63 us
  transfers between devices with their start and end apart: 4, of which 3 were waited for; matrix products, arithmetic and copies ran while one was open for 1% of the time, Pallas kernels for 22%

profile of v10, /device:TPU:1, one launch (start us, length us, event | category | flops | bytes accessed | tf_op | source)
XLA Modules:
  0.0 74.8 jit_solution(9227330036017615907)
XLA Ops:
  0.0 0.0 copy-start.2
  0.0 0.0 copy-start.5
  0.0 0.0 copy-start.6
  0.0 0.0 copy-start.4
  0.0 1.3 %slice_bitcast_fusion = bf16[20,48,384]{2,1,0:T(8,128)(2,1)S(1)} fusion(bf16[32,1,48,384]{3,2,0,1:T(8,128)(2,1)} %bitcast.5), kind=kLoop, calls=%fused_computation | loop fusion | bytes 1474560 | tf_op jit(solution)/shard_map/slice | solution.py:293
  1.3 1.5 %collective-permute-start.1 = (bf16[32,48,384]{2,1,0:T(8,128)(2,1)}, bf16[32,48,384]{2,1,0:T(8,128)(2,1)S(1)}, u32[]{:S(2)}, u32[]{:S(2)}) collective-permute-start(bf16[32,48,384]{2,1,0:T(8,128)(2,1)} %bitcast.6), channel_id=1, source_target_pairs={{0,1},{1,0},{2,3},{3,2},{4,5},{5,4},{6,7},{7,6},{8,9},{9,8},{10,11... | collective-permute-start | bytes 3538952 | tf_op jit(solution)/shard_map/ppermute | solution.py:296
  2.8 3.7 %collective-permute-start.2 = (bf16[20,48,384]{2,1,0:T(8,128)(2,1)S(1)}, bf16[20,48,384]{2,1,0:T(8,128)(2,1)S(1)}, u32[]{:S(2)}, u32[]{:S(2)}) collective-permute-start(bf16[20,48,384]{2,1,0:T(8,128)(2,1)S(1)} %slice_bitcast_fusion), channel_id=1, source_target_pairs={{0,127},{1,2},{2,1},{3,4},{4,3},{5,6},{6,5},{7,8},{8,7},{9,10},{10... | collective-permute-start | bytes 2211848 | tf_op jit(solution)/shard_map/ppermute | solution.py:294
  6.5 1.1 %slice.14 = bf16[12,48,384]{2,1,0:T(8,128)(2,1)S(1)} slice(bf16[32,48,384]{2,1,0:T(8,128)(2,1)} %bitcast.7), slice={[20:32], [0:48], [0:384]} | slice | bytes 884736 | tf_op jit(solution)/shard_map/slice | solution.py:295
  7.5 0.1 collective-permute-start.3
  7.6 0.0 copy-done.5
  7.6 0.0 copy-done.6
  7.7 0.0 collective-permute-done.1.twin
  7.7 0.0 copy-done.2
  7.7 0.0 copy-done.4
  7.7 0.0 copy-start
  7.7 3.3 %copy-done = bf16[3,3,3,384,384]{4,3,2,1,0:T(8,128)(2,1)S(1)} copy-done((bf16[3,3,3,384,384]{4,3,2,1,0:T(8,128)(2,1)S(1)}, bf16[3,3,3,384,384]{4,3,2,1,0:T(8,128)(2,1)}, u32[]{:S(2)}) %copy-start) | copy-done | bytes 7962648
  11.0 0.0 copy-start.1
  11.0 12.7 %shard_map.57 = (f32[32,48,384]{2,1,0:T(8,128)S(1)}, s32[1]{0:T(128)}) custom-call(s32[16]{0:T(128)S(1)} %copy-done.4, bf16[32,48,384]{2,1,0:T(8,128)(2,1)S(1)} %bitcast.8, bf16[32,48,384]{2,1,0:T(8,128)(2,1)S(1)} %collective-permute-done.1.twin, bf16[3,3,3,384,384]{4,3,2,1,0:T(8,128)(2,1)S(1)} %copy-done, f32[1,384]{1,0:T(1,128)S(1)} %reshape.10.gain, ...), custom_call_target="tpu_custom_call" | custom-call | tf_op jit(solution)/shard_map/pallas_call | solution.py:104
  23.6 3.9 %collective-permute-done.2.far.early_far = bf16[20,48,384]{2,1,0:T(8,128)(2,1)S(1)} collective-permute-done((bf16[20,48,384]{2,1,0:T(8,128)(2,1)S(1)}, bf16[20,48,384]{2,1,0:T(8,128)(2,1)S(1)}, u32[]{:S(2)}, u32[]{:S(2)}) %collective-permute-start.2) | collective-permute-done | bytes 737312 | tf_op jit(solution)/shard_map/ppermute | solution.py:294
  27.5 0.0 copy-done.1
  27.5 4.0 %shard_map.58.early = bf16[20,48,384]{2,1,0:T(8,128)(2,1)S(1)} custom-call(bf16[20,48,384]{2,1,0:T(8,128)(2,1)S(1)} %collective-permute-done.2.far.early_far, f32[32,48,384]{2,1,0:T(8,128)S(1)} %get-tuple-element.29.partial, bf16[3,3,3,384,384]{4,3,2,1,0:T(8,128)(2,1)S(1)} %copy-done.1, f32[1,384]{1,0:T(1,128)S(1)} %reshape.10.gain), custom_call_target="tpu_custom_call" | custom-call | tf_op jit(solution)/shard_map/pallas_call | solution.py:184
  31.5 1.5 %collective-permute-done.3.far = bf16[12,48,384]{2,1,0:T(8,128)(2,1)S(1)} collective-permute-done((bf16[12,48,384]{2,1,0:T(8,128)(2,1)S(1)}, bf16[12,48,384]{2,1,0:T(8,128)(2,1)S(1)}, u32[]{:S(2)}, u32[]{:S(2)}) %collective-permute-start.3) | collective-permute-done | bytes 442400 | tf_op jit(solution)/shard_map/ppermute | solution.py:295
  33.0 3.9 %shard_map.59 = (bf16[16,3,48,384]{3,2,1,0:T(8,128)(2,1)S(1)}, bf16[16,4,48,384]{3,2,1,0:T(8,128)(2,1)S(1)}) custom-call(s32[1]{0:T(128)} %get-tuple-element.27.fits, s32[16]{0:T(128)S(1)} %copy-done.4, bf16[20,48,384]{2,1,0:T(8,128)(2,1)S(1)} %collective-permute-done.2.far.early_far, bf16[12,48,384]{2,1,0:T(8,128)(2,1)S(1)} %collective-permute-done.3.far, ...), custom_call_target="tpu_custom_call" | custom-call | tf_op jit(solution)/shard_map/pallas_call | solution.py:196
  37.5 35.9 %conditional.1 = (bf16[4,16,48,384]{3,2,1,0:T(8,128)(2,1)S(1)}) conditional(s32[]{:T(128)} %bitcast.3, (bf16[16,4,48,384]{3,2,1,0:T(8,128)(2,1)S(1)}, s32[16]{0:T(128)S(1)}) %tuple.20, (bf16[16,3,48,384]{3,2,1,0:T(8,128)(2,1)S(1)}, s32[16]{0:T(128)S(1)}) %tuple.21), branch_computations={%region_0.0_spmd, %region_1.0_spmd} | conditional | bytes 5898288 | solution.py:302
  37.5 32.3 %all_to_all.9.arrived = bf16[16,3,48,384]{3,2,1,0:T(8,128)(2,1)S(1)} all-to-all(bf16[16,3,48,384]{3,2,1,0:T(8,128)(2,1)S(1)} %get-tuple-element.19), channel_id=1, replica_groups=mesh['ha'=8,'tc'=8,'core'=2] {'tc','core'}, dimensions={0} | all-to-all | bytes 3538944 | tf_op jit(solution)/shard_map/cond/branch_1_fun/all_to_all | solution.py:249
  69.9 0.6 branch_1_fun.2
  70.5 0.5 collective-permute-start
  71.0 1.6 %collective-permute-done.other = bf16[16,1,48,384]{3,2,1,0:T(8,128)(2,1)S(1)} collective-permute-done((bf16[16,1,48,384]{3,2,1,0:T(8,128)(2,1)S(1)}, bf16[16,1,48,384]{3,2,1,0:T(8,128)(2,1)S(1)}, u32[]{:S(2)}, u32[]{:S(2)}) %collective-permute-start) | collective-permute-done | bytes 589856 | tf_op jit(solution)/shard_map/cond/branch_1_fun/ppermute | solution.py:275
  72.6 0.8 %branch_1_fun.3 = bf16[4,16,48,384]{3,2,1,0:T(8,128)(2,1)S(1)} custom-call(s32[16]{0:T(128)S(1)} %get-tuple-element.18.starts, bf16[16,3,48,384]{3,2,1,0:T(8,128)(2,1)S(1)} %all_to_all.9.arrived, bf16[16,1,48,384]{3,2,1,0:T(8,128)(2,1)S(1)} %collective-permute-done.other), custom_call_target="tpu_custom_call" | custom-call | tf_op jit(solution)/shard_map/cond/branch_1_fun/pallas_call | solution.py:239
  73.4 0.0 copy-start.3
  73.4 1.4 %copy-done.3 = bf16[4,16,48,384]{3,2,1,0:T(8,128)(2,1)} copy-done((bf16[4,16,48,384]{3,2,1,0:T(8,128)(2,1)}, bf16[4,16,48,384]{3,2,1,0:T(8,128)(2,1)S(1)}, u32[]{:S(2)}) %copy-start.3) | copy-done | bytes 2359320
  (2 shorter events, 0.0 us)
Async XLA Ops:
  0.0 7.7 %copy-start.2 = (bf16[32,1,48,384]{3,2,1,0:T(8,128)(2,1)S(1)}, bf16[32,1,48,384]{3,2,1,0:T(8,128)(2,1)}, u32[]{:S(2)}) copy-start(bf16[32,1,48,384]{3,2,1,0:T(8,128)(2,1)} %param.7) | copy-start | bytes 3538948
  0.0 7.6 %copy-start.5 = (f32[384]{0:T(512)S(1)}, f32[384]{0:T(512)}, u32[]{:S(2)}) copy-start(f32[384]{0:T(512)} %param.9) | copy-start | bytes 4612
  0.0 7.6 %copy-start.6 = (f32[384]{0:T(512)S(1)}, f32[384]{0:T(512)}, u32[]{:S(2)}) copy-start(f32[384]{0:T(512)} %param.11) | copy-start | bytes 4612
  0.0 7.7 %copy-start.4 = (s32[16]{0:T(128)S(1)}, s32[16]{0:T(128)}, u32[]{:S(2)}) copy-start(s32[16]{0:T(128)} %starts.3) | copy-start | bytes 196
  1.3 6.4 %collective-permute-start.1 = (bf16[32,48,384]{2,1,0:T(8,128)(2,1)}, bf16[32,48,384]{2,1,0:T(8,128)(2,1)S(1)}, u32[]{:S(2)}, u32[]{:S(2)}) collective-permute-start(bf16[32,48,384]{2,1,0:T(8,128)(2,1)} %bitcast.6), channel_id=1, source_target_pairs={{0,1},{1,0},{2,3},{3,2},{4,5},{5,4},{6,7},{7,6},{8,9},{9,8},{10,11... | collective-permute-start | bytes 3538952 | tf_op jit(solution)/shard_map/ppermute | solution.py:296
  2.8 24.7 %collective-permute-start.2 = (bf16[20,48,384]{2,1,0:T(8,128)(2,1)S(1)}, bf16[20,48,384]{2,1,0:T(8,128)(2,1)S(1)}, u32[]{:S(2)}, u32[]{:S(2)}) collective-permute-start(bf16[20,48,384]{2,1,0:T(8,128)(2,1)S(1)} %slice_bitcast_fusion), channel_id=1, source_target_pairs={{0,127},{1,2},{2,1},{3,4},{4,3},{5,6},{6,5},{7,8},{8,7},{9,10},{10... | collective-permute-start | bytes 2211848 | tf_op jit(solution)/shard_map/ppermute | solution.py:294
  7.5 25.5 %collective-permute-start.3 = (bf16[12,48,384]{2,1,0:T(8,128)(2,1)S(1)}, bf16[12,48,384]{2,1,0:T(8,128)(2,1)S(1)}, u32[]{:S(2)}, u32[]{:S(2)}) collective-permute-start(bf16[12,48,384]{2,1,0:T(8,128)(2,1)S(1)} %slice.14), channel_id=1, source_target_pairs={{0,127},{1,2},{2,1},{3,4},{4,3},{5,6},{6,5},{7,8},{8,7},{9,10},{10... | collective-permute-start | bytes 1327112 | tf_op jit(solution)/shard_map/ppermute | solution.py:295
  7.7 3.3 %copy-start = (bf16[3,3,3,384,384]{4,3,2,1,0:T(8,128)(2,1)S(1)}, bf16[3,3,3,384,384]{4,3,2,1,0:T(8,128)(2,1)}, u32[]{:S(2)}) copy-start(bf16[3,3,3,384,384]{4,3,2,1,0:T(8,128)(2,1)} %weight.5) | copy-start | bytes 23887876
  11.0 16.6 %copy-start.1 = (bf16[3,3,3,384,384]{4,3,2,1,0:T(8,128)(2,1)S(1)}, bf16[3,3,3,384,384]{4,3,2,1,0:T(8,128)(2,1)}, u32[]{:S(2)}) copy-start(bf16[3,3,3,384,384]{4,3,2,1,0:T(8,128)(2,1)} %weight.5) | copy-start | bytes 23887876
  70.5 2.1 %collective-permute-start = (bf16[16,1,48,384]{3,2,1,0:T(8,128)(2,1)S(1)}, bf16[16,1,48,384]{3,2,1,0:T(8,128)(2,1)S(1)}, u32[]{:S(2)}, u32[]{:S(2)}) collective-permute-start(bf16[16,1,48,384]{3,2,1,0:T(8,128)(2,1)S(1)} %branch_1_fun.2), channel_id=1, source_target_pairs={{0,1},{1,0},{2,3},{3,2},{4,5},{5,4},{6,7},{7,6},{8,9},{9,8},{10,11... | collective-permute-start | bytes 1769480 | tf_op jit(solution)/shard_map/cond/branch_1_fun/ppermute | solution.py:275
  73.4 1.4 %copy-start.3 = (bf16[4,16,48,384]{3,2,1,0:T(8,128)(2,1)}, bf16[4,16,48,384]{3,2,1,0:T(8,128)(2,1)S(1)}, u32[]{:S(2)}) copy-start(bf16[4,16,48,384]{3,2,1,0:T(8,128)(2,1)S(1)} %get-tuple-element.41) | copy-start | bytes 7077892

commit v11 on v10

--- a/solution.py
+++ b/solution.py
@@ -69,12 +69,7 @@
 ):
     total, cols, _ = own.shape
     core = lax.axis_index("core")
-    groups = starts.shape[0]
-    most = functools.reduce(
-        jnp.maximum,
-        [after_of(starts, j + 1, total) - starts[j] for j in range(0, groups, 2)],
-    )
-    fits[0] = (most <= 2 * (FMAX - 1)).astype(jnp.int32)
+    fits[0] = few_suffice(starts, total).astype(jnp.int32)
     clear_sides(sums, cols)
     for act in (own_act, twin_act):
         act[pl.ds(0, HIST)] = jnp.zeros((HIST,) + act.shape[1:], act.dtype)
@@ -139,8 +134,13 @@
     return (partial[pl.ds(begin, count)] + convolved).astype(jnp.bfloat16)
 
 
-def early_kernel(far, partial, weight, gain, out, act, sums):
+def first_kernel(far, partial, weight, gain, out, act, sums):
     out[...] = far_frames(0, far, None, partial, weight, gain, act, sums)
+
+
+def second_kernel(recent, far, partial, weight, gain, out, act, sums):
+    begin = recent.shape[0]
+    out[...] = far_frames(begin, far, recent, partial, weight, gain, act, sums)
 
 
 def after_of(starts, group, total):
@@ -148,24 +148,34 @@
     return jnp.where(group + 1 < groups, starts[jnp.minimum(group + 1, groups - 1)], total)
 
 
+def few_suffice(starts, total):
+    most = functools.reduce(
+        jnp.maximum,
+        [after_of(starts, j + 1, total) - starts[j] for j in range(0, starts.shape[0], 2)],
+    )
+    return most <= 2 * (FMAX - 1)
+
+
 def late_kernel(
-    fits, starts, early_far, far, early, partial, weight, gain, few, many, act, sums, result
+    starts, recent, far, first, second, partial, weight, gain, few, many, act, sums, result
 ):
-    cut = early.shape[0]
+    cut = first.shape[0] + second.shape[0]
     count, cols, chans = far.shape
-    result[pl.ds(0, cut)] = early[...]
+    result[pl.ds(0, first.shape[0])] = first[...]
+    result[pl.ds(first.shape[0], second.shape[0])] = second[...]
     result[pl.ds(cut + count, FMAX)] = jnp.zeros((FMAX, cols, chans), result.dtype)
     result[pl.ds(cut, count)] = far_frames(
-        cut, far, early_far, partial, weight, gain, act, sums
+        cut, far, recent, partial, weight, gain, act, sums
     )
     total = cut + count
-
-    @pl.when(fits[0] == 0)
+    enough = few_suffice(starts, total)
+
+    @pl.when(jnp.logical_not(enough))
     def _():
         for j in range(many.shape[0]):
             many[j] = result[pl.ds(jnp.clip(starts[j], 0, total), FMAX)]
 
-    @pl.when(fits[0] == 1)
+    @pl.when(enough)
     def _():
         slots = few.shape[1]
         for j in range(few.shape[0]):
@@ -180,18 +190,19 @@
     ]
 
 
-def early_rows(far, partial, weight, gain):
-    return pl.pallas_call(
-        early_kernel,
+def earlier_rows(kernel, *args):
+    far = args[-4]
+    return pl.pallas_call(
+        kernel,
         out_shape=jax.ShapeDtypeStruct(far.shape, jnp.bfloat16),
-        in_specs=[VMEM_SPEC] * 4,
+        in_specs=[VMEM_SPEC] * len(args),
         out_specs=VMEM_SPEC,
         scratch_shapes=far_scratch(*far.shape),
         compiler_params=pltpu.CompilerParams(vmem_limit_bytes=FAR_VMEM_BYTES),
-    )(far, partial, weight, gain)
-
-
-def late_rows(fits, starts, early_far, far, early, partial, weight, gain):
+    )(*args)
+
+
+def late_rows(starts, recent, far, first, second, partial, weight, gain):
     total, cols, chans = partial.shape
     return pl.pallas_call(
         late_kernel,
@@ -199,12 +210,12 @@
             jax.ShapeDtypeStruct((starts.shape[0], slots, cols, chans), jnp.bfloat16)
             for slots in (FMAX - 1, FMAX)
         ],
-        in_specs=[SMEM_SPEC] * 2 + [VMEM_SPEC] * 6,
+        in_specs=[SMEM_SPEC] + [VMEM_SPEC] * 7,
         out_specs=[VMEM_SPEC] * 2,
         scratch_shapes=far_scratch(*far.shape)
         + [pltpu.VMEM((total + FMAX, cols, chans), jnp.bfloat16)],
         compiler_params=pltpu.CompilerParams(vmem_limit_bytes=FAR_VMEM_BYTES),
-    )(fits, starts, early_far, far, early, partial, weight, gain)
+    )(starts, recent, far, first, second, partial, weight, gain)
 
 
 def unpack_kernel(total, starts, arrived, other, out):
@@ -289,15 +300,17 @@
     gain = norm_gain.reshape(1, -1)
     bias = conv_bias.reshape(1, -1)
     pairs = [(r, (r + 1) % rows if r % 2 else (r - 1) % rows) for r in range(rows)]
-    cut = total * 5 // 8
-    front, own = lax.optimization_barrier((own[:cut], own))
-    early_far = lax.ppermute(front, ("ha", "tc", "core"), pairs)
-    late_far = lax.ppermute(own[cut:], ("ha", "tc", "core"), pairs)
+    cuts = (0, total * 3 // 8, total * 3 // 4, total)
+    parts = [own[begin:end] for begin, end in zip(cuts, cuts[1:])]
+    parts[0], own = lax.optimization_barrier((parts[0], own))
+    parts[1:] = [own[begin:end] for begin, end in zip(cuts[1:], cuts[2:])]
+    fars = [lax.ppermute(part, ("ha", "tc", "core"), pairs) for part in parts]
     twin = lax.ppermute(own, "core", [(0, 1), (1, 0)])
     partial, fits = near_rows(group_start, own, twin, conv_weight, gain, bias)
-    early = early_rows(early_far, partial, conv_weight, gain)
+    first = earlier_rows(first_kernel, fars[0], partial, conv_weight, gain)
+    second = earlier_rows(second_kernel, fars[0], fars[1], partial, conv_weight, gain)
     few, many = late_rows(
-        fits, group_start, early_far, late_far, early, partial, conv_weight, gain
+        group_start, fars[1], fars[2], first, second, partial, conv_weight, gain
     )
     return lax.switch(
         fits[0],

time: 75.1 us -> 78 us (1.039)
  waiting for transfers between devices: 7.04 us -> 1.64 us
  blocking collectives: 32.3 us -> 36.9 us
  starting transfers between devices: 5.74 us -> 9.07 us
  local copies, waits for them, and re-layouts: 7.02 us -> 7.88 us
    ppermute x2 -> x3, waiting for transfers between devices: 5.41 us -> 0.01 us  [on_device(): fars = [lax.ppermute(part, ('ha', 'tc', 'core'), pairs) for part in parts]]
    all_to_all x1, blocking collectives: 32.3 us -> 36.9 us  [regroup(): lax.all_to_all(packed, ('tc', 'core'), split_axis=0, concat_axis=0, tiled...]
    ppermute x2 -> x3, starting transfers between devices: 3.77 us -> 7.08 us  [on_device(): fars = [lax.ppermute(part, ('ha', 'tc', 'core'), pairs) for part in parts]]
    pallas_call x1, Pallas kernels: 3.86 us -> 2.51 us  [late_rows(): pl.pallas_call(late_kernel, out_shape=[jax.ShapeDtypeStruct((starts.shape...]
    pallas_call x1 -> x2, Pallas kernels: 3.96 us -> 4.89 us  [earlier_rows(): pl.pallas_call(kernel, out_shape=jax.ShapeDtypeStruct(far.shape, jnp.bflo...]
    slice x2 -> x3, local copies, waits for them, and re-layouts: 2.34 us -> 3.2 us  [the longest x2 2.05 us: on_device(): parts[1:] = [own[begin:end] for begin, end in zip(cuts[1:], cuts[2:])]]
  transfers between devices with their start and end apart: 4 -> 5, of which waited for: 3 -> 1; matrix products, arithmetic and copies ran while one was open for 1% -> 3% of each run, Pallas kernels for 22% -> 23%
where the time goes in v11:
time: 78 us; the launch traced here: 77.8 us
  blocking collectives  36.9 us (47%)
  Pallas kernels  21.5 us (28%)
  starting transfers between devices  9.07 us (12%)
  local copies, waits for them, and re-layouts  7.88 us (10%)
  waiting for transfers between devices  1.64 us (2%)
  between operations  0.79 us (1%)
    all_to_all x1, blocking collectives, regroup(): lax.all_to_all(packed, ('tc', 'core'), split_axis=0, concat_axis=0, tiled...  36.9 us
    pallas_call x1, Pallas kernels, near_rows(): pl.pallas_call(near_kernel, out_shape=[jax.ShapeDtypeStruct(own.shape, jn...  12.6 us
    ppermute x3, starting transfers between devices, on_device(): fars = [lax.ppermute(part, ('ha', 'tc', 'core'), pairs) for part in parts]  7.08 us
    pallas_call x2, Pallas kernels, earlier_rows(): pl.pallas_call(kernel, out_shape=jax.ShapeDtypeStruct(far.shape, jnp.bflo...  4.89 us
    unnamed x14, local copies, waits for them, and re-layouts  4.67 us
    pallas_call x1, Pallas kernels, late_rows(): pl.pallas_call(late_kernel, out_shape=[jax.ShapeDtypeStruct((starts.shape...  2.51 us
    slice x2, local copies, waits for them, and re-layouts, on_device(): parts[1:] = [own[begin:end] for begin, end in zip(cuts[1:], cuts[2:])]  2.05 us
    ppermute x1, waiting for transfers between devices, send_few(): other = lax.ppermute(pick(total, starts, arrived), 'core', [(0, 1), (1, 0)])  1.63 us
  transfers between devices with their start and end apart: 5, of which 1 were waited for; matrix products, arithmetic and copies ran while one was open for 3% of the time, Pallas kernels for 23%

profile of v11, /device:TPU:1, one launch (start us, length us, event | category | flops | bytes accessed | tf_op | source)
XLA Modules:
  0.0 77.8 jit_solution(7530994925226956830)
XLA Ops:
  0.0 0.0 copy-start.2
  0.0 0.0 copy-start.5
  0.0 0.0 copy-start.6
  0.0 0.0 copy-start.4
  0.0 1.2 %slice_bitcast_fusion = bf16[12,48,384]{2,1,0:T(8,128)(2,1)S(1)} fusion(bf16[32,1,48,384]{3,2,0,1:T(8,128)(2,1)} %bitcast.5), kind=kLoop, calls=%fused_computation | loop fusion | bytes 884736 | tf_op jit(solution)/shard_map/slice | solution.py:304
  1.2 1.5 %collective-permute-start.1 = (bf16[32,48,384]{2,1,0:T(8,128)(2,1)}, bf16[32,48,384]{2,1,0:T(8,128)(2,1)S(1)}, u32[]{:S(2)}, u32[]{:S(2)}) collective-permute-start(bf16[32,48,384]{2,1,0:T(8,128)(2,1)} %bitcast.6), channel_id=1, source_target_pairs={{0,1},{1,0},{2,3},{3,2},{4,5},{5,4},{6,7},{7,6},{8,9},{9,8},{10,11... | collective-permute-start | bytes 3538952 | tf_op jit(solution)/shard_map/ppermute | solution.py:308
  2.7 3.7 %collective-permute-start.4 = (bf16[12,48,384]{2,1,0:T(8,128)(2,1)S(1)}, bf16[12,48,384]{2,1,0:T(8,128)(2,1)S(1)}, u32[]{:S(2)}, u32[]{:S(2)}) collective-permute-start(bf16[12,48,384]{2,1,0:T(8,128)(2,1)S(1)} %slice_bitcast_fusion), channel_id=1, source_target_pairs={{0,127},{1,2},{2,1},{3,4},{4,3},{5,6},{6,5},{7,8},{8,7},{9,10},{10... | collective-permute-start | bytes 1327112 | tf_op jit(solution)/shard_map/ppermute | solution.py:307
  6.3 1.1 %slice.17 = bf16[12,48,384]{2,1,0:T(8,128)(2,1)S(1)} slice(bf16[32,48,384]{2,1,0:T(8,128)(2,1)} %bitcast.7), slice={[12:24], [0:48], [0:384]} | slice | bytes 884736 | tf_op jit(solution)/shard_map/slice | solution.py:306
  7.4 0.1 collective-permute-start.2
  7.5 1.0 %slice.18 = bf16[8,48,384]{2,1,0:T(8,128)(2,1)S(1)} slice(bf16[32,48,384]{2,1,0:T(8,128)(2,1)} %bitcast.8), slice={[24:32], [0:48], [0:384]} | slice | bytes 589824 | tf_op jit(solution)/shard_map/slice | solution.py:306
  8.5 3.3 %collective-permute-start.3 = (bf16[8,48,384]{2,1,0:T(8,128)(2,1)S(1)}, bf16[8,48,384]{2,1,0:T(8,128)(2,1)S(1)}, u32[]{:S(2)}, u32[]{:S(2)}) collective-permute-start(bf16[8,48,384]{2,1,0:T(8,128)(2,1)S(1)} %slice.18), channel_id=1, source_target_pairs={{0,127},{1,2},{2,1},{3,4},{4,3},{5,6},{6,5},{7,8},{8,7},{9,10},{10... | collective-permute-start | bytes 884744 | tf_op jit(solution)/shard_map/ppermute | solution.py:307
  11.8 0.0 copy-done.5
  11.8 0.0 copy-done.6
  11.8 0.0 collective-permute-done.1.twin
  11.8 0.0 copy-done.2
  11.8 0.0 copy-done.4
  11.8 0.0 copy-start
  11.9 3.3 %copy-done = bf16[3,3,3,384,384]{4,3,2,1,0:T(8,128)(2,1)S(1)} copy-done((bf16[3,3,3,384,384]{4,3,2,1,0:T(8,128)(2,1)S(1)}, bf16[3,3,3,384,384]{4,3,2,1,0:T(8,128)(2,1)}, u32[]{:S(2)}) %copy-start) | copy-done | bytes 7962648
  15.1 0.0 copy-start.1
  15.1 12.6 %shard_map.57 = (f32[32,48,384]{2,1,0:T(8,128)S(1)}, s32[1]{0:T(128)}) custom-call(s32[16]{0:T(128)S(1)} %copy-done.4, bf16[32,48,384]{2,1,0:T(8,128)(2,1)S(1)} %bitcast.9, bf16[32,48,384]{2,1,0:T(8,128)(2,1)S(1)} %collective-permute-done.1.twin, bf16[3,3,3,384,384]{4,3,2,1,0:T(8,128)(2,1)S(1)} %copy-done, f32[1,384]{1,0:T(1,128)S(1)} %reshape.10.gain, ...), custom_call_target="tpu_custom_call" | custom-call | tf_op jit(solution)/shard_map/pallas_call | solution.py:99
  27.8 0.0 collective-permute-done.4.far.recent
  27.8 0.0 copy-done.1
  27.8 2.4 %shard_map.58.first = bf16[12,48,384]{2,1,0:T(8,128)(2,1)S(1)} custom-call(bf16[12,48,384]{2,1,0:T(8,128)(2,1)S(1)} %collective-permute-done.4.far.recent, f32[32,48,384]{2,1,0:T(8,128)S(1)} %get-tuple-element.29.partial, bf16[3,3,3,384,384]{4,3,2,1,0:T(8,128)(2,1)S(1)} %copy-done.1, f32[1,384]{1,0:T(1,128)S(1)} %reshape.10.gain), custom_call_target="tpu_custom_call" | custom-call | tf_op jit(solution)/shard_map/pallas_call | solution.py:195
  30.2 0.0 collective-permute-done.2.far.recent
  30.2 2.5 %shard_map.59.second = bf16[12,48,384]{2,1,0:T(8,128)(2,1)S(1)} custom-call(bf16[12,48,384]{2,1,0:T(8,128)(2,1)S(1)} %collective-permute-done.4.far.recent, bf16[12,48,384]{2,1,0:T(8,128)(2,1)S(1)} %collective-permute-done.2.far.recent, f32[32,48,384]{2,1,0:T(8,128)S(1)} %get-tuple-element.29.partial, bf16[3,3,3,384,384]{4,3,2,1,0:T(8,128)(2,1)S(1)} %copy-done.1, ...), custom_call_target="tpu_custom_call" | custom-call | tf_op jit(solution)/shard_map/pallas_call | solution.py:195
  32.7 0.0 collective-permute-done.3.far
  32.7 2.5 %shard_map.60 = (bf16[16,3,48,384]{3,2,1,0:T(8,128)(2,1)S(1)}, bf16[16,4,48,384]{3,2,1,0:T(8,128)(2,1)S(1)}) custom-call(s32[16]{0:T(128)S(1)} %copy-done.4, bf16[12,48,384]{2,1,0:T(8,128)(2,1)S(1)} %collective-permute-done.2.far.recent, bf16[8,48,384]{2,1,0:T(8,128)(2,1)S(1)} %collective-permute-done.3.far, bf16[12,48,384]{2,1,0:T(8,128)(2,1)S(1)} %shard_map.58.first, ...), custom_call_target="tpu_custom_call" | custom-call | tf_op jit(solution)/shard_map/pallas_call | solution.py:207
  35.9 40.5 %conditional.1 = (bf16[4,16,48,384]{3,2,1,0:T(8,128)(2,1)S(1)}) conditional(s32[]{:T(128)} %bitcast.3, (bf16[16,4,48,384]{3,2,1,0:T(8,128)(2,1)S(1)}, s32[16]{0:T(128)S(1)}) %tuple.20, (bf16[16,3,48,384]{3,2,1,0:T(8,128)(2,1)S(1)}, s32[16]{0:T(128)S(1)}) %tuple.21), branch_computations={%region_0.0_spmd, %region_1.0_spmd} | conditional | bytes 5898288 | solution.py:315
  35.9 36.9 %all_to_all.9.arrived = bf16[16,3,48,384]{3,2,1,0:T(8,128)(2,1)S(1)} all-to-all(bf16[16,3,48,384]{3,2,1,0:T(8,128)(2,1)S(1)} %get-tuple-element.19), channel_id=1, replica_groups=mesh['ha'=8,'tc'=8,'core'=2] {'tc','core'}, dimensions={0} | all-to-all | bytes 3538944 | tf_op jit(solution)/shard_map/cond/branch_1_fun/all_to_all | solution.py:260
  72.8 0.6 branch_1_fun.2
  73.4 0.5 collective-permute-start
  73.9 1.6 %collective-permute-done.other = bf16[16,1,48,384]{3,2,1,0:T(8,128)(2,1)S(1)} collective-permute-done((bf16[16,1,48,384]{3,2,1,0:T(8,128)(2,1)S(1)}, bf16[16,1,48,384]{3,2,1,0:T(8,128)(2,1)S(1)}, u32[]{:S(2)}, u32[]{:S(2)}) %collective-permute-start) | collective-permute-done | bytes 589856 | tf_op jit(solution)/shard_map/cond/branch_1_fun/ppermute | solution.py:286
  75.5 0.8 %branch_1_fun.3 = bf16[4,16,48,384]{3,2,1,0:T(8,128)(2,1)S(1)} custom-call(s32[16]{0:T(128)S(1)} %get-tuple-element.18.starts, bf16[16,3,48,384]{3,2,1,0:T(8,128)(2,1)S(1)} %all_to_all.9.arrived, bf16[16,1,48,384]{3,2,1,0:T(8,128)(2,1)S(1)} %collective-permute-done.other), custom_call_target="tpu_custom_call" | custom-call | tf_op jit(solution)/shard_map/cond/branch_1_fun/pallas_call | solution.py:250
  76.4 0.0 copy-start.3
  76.4 1.4 %copy-done.3 = bf16[4,16,48,384]{3,2,1,0:T(8,128)(2,1)} copy-done((bf16[4,16,48,384]{3,2,1,0:T(8,128)(2,1)}, bf16[4,16,48,384]{3,2,1,0:T(8,128)(2,1)S(1)}, u32[]{:S(2)}) %copy-start.3) | copy-done | bytes 2359320
  (2 shorter events, 0.0 us)
Async XLA Ops:
  0.0 11.8 %copy-start.2 = (bf16[32,1,48,384]{3,2,1,0:T(8,128)(2,1)S(1)}, bf16[32,1,48,384]{3,2,1,0:T(8,128)(2,1)}, u32[]{:S(2)}) copy-start(bf16[32,1,48,384]{3,2,1,0:T(8,128)(2,1)} %param.7) | copy-start | bytes 3538948
  0.0 11.8 %copy-start.5 = (f32[384]{0:T(512)S(1)}, f32[384]{0:T(512)}, u32[]{:S(2)}) copy-start(f32[384]{0:T(512)} %param.9) | copy-start | bytes 4612
  0.0 11.8 %copy-start.6 = (f32[384]{0:T(512)S(1)}, f32[384]{0:T(512)}, u32[]{:S(2)}) copy-start(f32[384]{0:T(512)} %param.11) | copy-start | bytes 4612
  0.0 11.8 %copy-start.4 = (s32[16]{0:T(128)S(1)}, s32[16]{0:T(128)}, u32[]{:S(2)}) copy-start(s32[16]{0:T(128)} %starts.3) | copy-start | bytes 196
  1.2 10.6 %collective-permute-start.1 = (bf16[32,48,384]{2,1,0:T(8,128)(2,1)}, bf16[32,48,384]{2,1,0:T(8,128)(2,1)S(1)}, u32[]{:S(2)}, u32[]{:S(2)}) collective-permute-start(bf16[32,48,384]{2,1,0:T(8,128)(2,1)} %bitcast.6), channel_id=1, source_target_pairs={{0,1},{1,0},{2,3},{3,2},{4,5},{5,4},{6,7},{7,6},{8,9},{9,8},{10,11... | collective-permute-start | bytes 3538952 | tf_op jit(solution)/shard_map/ppermute | solution.py:308
  2.7 25.1 %collective-permute-start.4 = (bf16[12,48,384]{2,1,0:T(8,128)(2,1)S(1)}, bf16[12,48,384]{2,1,0:T(8,128)(2,1)S(1)}, u32[]{:S(2)}, u32[]{:S(2)}) collective-permute-start(bf16[12,48,384]{2,1,0:T(8,128)(2,1)S(1)} %slice_bitcast_fusion), channel_id=1, source_target_pairs={{0,127},{1,2},{2,1},{3,4},{4,3},{5,6},{6,5},{7,8},{8,7},{9,10},{10... | collective-permute-start | bytes 1327112 | tf_op jit(solution)/shard_map/ppermute | solution.py:307
  7.4 22.8 %collective-permute-start.2 = (bf16[12,48,384]{2,1,0:T(8,128)(2,1)S(1)}, bf16[12,48,384]{2,1,0:T(8,128)(2,1)S(1)}, u32[]{:S(2)}, u32[]{:S(2)}) collective-permute-start(bf16[12,48,384]{2,1,0:T(8,128)(2,1)S(1)} %slice.17), channel_id=1, source_target_pairs={{0,127},{1,2},{2,1},{3,4},{4,3},{5,6},{6,5},{7,8},{8,7},{9,10},{10... | collective-permute-start | bytes 1327112 | tf_op jit(solution)/shard_map/ppermute | solution.py:307
  8.5 24.2 %collective-permute-start.3 = (bf16[8,48,384]{2,1,0:T(8,128)(2,1)S(1)}, bf16[8,48,384]{2,1,0:T(8,128)(2,1)S(1)}, u32[]{:S(2)}, u32[]{:S(2)}) collective-permute-start(bf16[8,48,384]{2,1,0:T(8,128)(2,1)S(1)} %slice.18), channel_id=1, source_target_pairs={{0,127},{1,2},{2,1},{3,4},{4,3},{5,6},{6,5},{7,8},{8,7},{9,10},{10... | collective-permute-start | bytes 884744 | tf_op jit(solution)/shard_map/ppermute | solution.py:307
  11.8 3.3 %copy-start = (bf16[3,3,3,384,384]{4,3,2,1,0:T(8,128)(2,1)S(1)}, bf16[3,3,3,384,384]{4,3,2,1,0:T(8,128)(2,1)}, u32[]{:S(2)}) copy-start(bf16[3,3,3,384,384]{4,3,2,1,0:T(8,128)(2,1)} %weight.7) | copy-start | bytes 23887876
  15.1 12.7 %copy-start.1 = (bf16[3,3,3,384,384]{4,3,2,1,0:T(8,128)(2,1)S(1)}, bf16[3,3,3,384,384]{4,3,2,1,0:T(8,128)(2,1)}, u32[]{:S(2)}) copy-start(bf16[3,3,3,384,384]{4,3,2,1,0:T(8,128)(2,1)} %weight.7) | copy-start | bytes 23887876
  73.4 2.1 %collective-permute-start = (bf16[16,1,48,384]{3,2,1,0:T(8,128)(2,1)S(1)}, bf16[16,1,48,384]{3,2,1,0:T(8,128)(2,1)S(1)}, u32[]{:S(2)}, u32[]{:S(2)}) collective-permute-start(bf16[16,1,48,384]{3,2,1,0:T(8,128)(2,1)S(1)} %branch_1_fun.2), channel_id=1, source_target_pairs={{0,1},{1,0},{2,3},{3,2},{4,5},{5,4},{6,7},{7,6},{8,9},{9,8},{10,11... | collective-permute-start | bytes 1769480 | tf_op jit(solution)/shard_map/cond/branch_1_fun/ppermute | solution.py:286
  76.4 1.4 %copy-start.3 = (bf16[4,16,48,384]{3,2,1,0:T(8,128)(2,1)}, bf16[4,16,48,384]{3,2,1,0:T(8,128)(2,1)S(1)}, u32[]{:S(2)}) copy-start(bf16[4,16,48,384]{3,2,1,0:T(8,128)(2,1)S(1)} %get-tuple-element.42) | copy-start | bytes 7077892

commit v12 on v10

--- a/solution.py
+++ b/solution.py
@@ -69,12 +69,7 @@
 ):
     total, cols, _ = own.shape
     core = lax.axis_index("core")
-    groups = starts.shape[0]
-    most = functools.reduce(
-        jnp.maximum,
-        [after_of(starts, j + 1, total) - starts[j] for j in range(0, groups, 2)],
-    )
-    fits[0] = (most <= 2 * (FMAX - 1)).astype(jnp.int32)
+    fits[0] = few_suffice(starts, total).astype(jnp.int32)
     clear_sides(sums, cols)
     for act in (own_act, twin_act):
         act[pl.ds(0, HIST)] = jnp.zeros((HIST,) + act.shape[1:], act.dtype)
@@ -148,24 +143,33 @@
     return jnp.where(group + 1 < groups, starts[jnp.minimum(group + 1, groups - 1)], total)
 
 
+def few_suffice(starts, total):
+    most = functools.reduce(
+        jnp.maximum,
+        [after_of(starts, j + 1, total) - starts[j] for j in range(0, starts.shape[0], 2)],
+    )
+    return most <= 2 * (FMAX - 1)
+
+
 def late_kernel(
-    fits, starts, early_far, far, early, partial, weight, gain, few, many, act, sums, result
+    starts, recent, far, early, partial, weight, gain, few, many, act, sums, result
 ):
     cut = early.shape[0]
     count, cols, chans = far.shape
     result[pl.ds(0, cut)] = early[...]
     result[pl.ds(cut + count, FMAX)] = jnp.zeros((FMAX, cols, chans), result.dtype)
     result[pl.ds(cut, count)] = far_frames(
-        cut, far, early_far, partial, weight, gain, act, sums
+        cut, far, recent, partial, weight, gain, act, sums
     )
     total = cut + count
-
-    @pl.when(fits[0] == 0)
+    enough = few_suffice(starts, total)
+
+    @pl.when(jnp.logical_not(enough))
     def _():
         for j in range(many.shape[0]):
             many[j] = result[pl.ds(jnp.clip(starts[j], 0, total), FMAX)]
 
-    @pl.when(fits[0] == 1)
+    @pl.when(enough)
     def _():
         slots = few.shape[1]
         for j in range(few.shape[0]):
@@ -191,7 +195,7 @@
     )(far, partial, weight, gain)
 
 
-def late_rows(fits, starts, early_far, far, early, partial, weight, gain):
+def late_rows(starts, recent, far, early, partial, weight, gain):
     total, cols, chans = partial.shape
     return pl.pallas_call(
         late_kernel,
@@ -199,12 +203,12 @@
             jax.ShapeDtypeStruct((starts.shape[0], slots, cols, chans), jnp.bfloat16)
             for slots in (FMAX - 1, FMAX)
         ],
-        in_specs=[SMEM_SPEC] * 2 + [VMEM_SPEC] * 6,
+        in_specs=[SMEM_SPEC] + [VMEM_SPEC] * 6,
         out_specs=[VMEM_SPEC] * 2,
         scratch_shapes=far_scratch(*far.shape)
         + [pltpu.VMEM((total + FMAX, cols, chans), jnp.bfloat16)],
         compiler_params=pltpu.CompilerParams(vmem_limit_bytes=FAR_VMEM_BYTES),
-    )(fits, starts, early_far, far, early, partial, weight, gain)
+    )(starts, recent, far, early, partial, weight, gain)
 
 
 def unpack_kernel(total, starts, arrived, other, out):
@@ -297,7 +301,7 @@
     partial, fits = near_rows(group_start, own, twin, conv_weight, gain, bias)
     early = early_rows(early_far, partial, conv_weight, gain)
     few, many = late_rows(
-        fits, group_start, early_far, late_far, early, partial, conv_weight, gain
+        group_start, early_far, late_far, early, partial, conv_weight, gain
     )
     return lax.switch(
         fits[0],

time: 75.1 us -> 74.4 us (level)
  no operation moved by 1% of the time
where the time goes in v12:
time: 74.4 us; the launch traced here: 74.2 us
  blocking collectives  32.3 us (43%)
  Pallas kernels  21.2 us (28%)
  waiting for transfers between devices  7.05 us (9%)
  local copies, waits for them, and re-layouts  7.02 us (9%)
  starting transfers between devices  5.74 us (8%)
  between operations  0.77 us (1%)
    all_to_all x1, blocking collectives, regroup(): lax.all_to_all(packed, ('tc', 'core'), split_axis=0, concat_axis=0, tiled...  32.3 us
    pallas_call x1, Pallas kernels, near_rows(): pl.pallas_call(near_kernel, out_shape=[jax.ShapeDtypeStruct(own.shape, jn...  12.7 us
    unnamed x14, local copies, waits for them, and re-layouts  4.67 us
    pallas_call x1, Pallas kernels, early_rows(): pl.pallas_call(early_kernel, out_shape=jax.ShapeDtypeStruct(far.shape, jn...  3.95 us
    ppermute x1, waiting for transfers between devices, on_device(): early_far = lax.ppermute(front, ('ha', 'tc', 'core'), pairs)  3.9 us
    ppermute x1, starting transfers between devices, on_device(): early_far = lax.ppermute(front, ('ha', 'tc', 'core'), pairs)  3.67 us
    pallas_call x1, Pallas kernels, late_rows(): pl.pallas_call(late_kernel, out_shape=[jax.ShapeDtypeStruct((starts.shape...  3.22 us
    ppermute x1, waiting for transfers between devices, send_few(): other = lax.ppermute(pick(total, starts, arrived), 'core', [(0, 1), (1, 0)])  1.63 us
  transfers between devices with their start and end apart: 4, of which 3 were waited for; matrix products, arithmetic and copies ran while one was open for 1% of the time, Pallas kernels for 22%

profile of v12, /device:TPU:1, one launch (start us, length us, event | category | flops | bytes accessed | tf_op | source)
XLA Modules:
  0.0 74.2 jit_solution(16819265280016833785)
XLA Ops:
  0.0 0.0 copy-start.2
  0.0 0.0 copy-start.5
  0.0 0.0 copy-start.6
  0.0 0.0 copy-start.4
  0.0 1.3 %slice_bitcast_fusion = bf16[20,48,384]{2,1,0:T(8,128)(2,1)S(1)} fusion(bf16[32,1,48,384]{3,2,0,1:T(8,128)(2,1)} %bitcast.5), kind=kLoop, calls=%fused_computation | loop fusion | bytes 1474560 | tf_op jit(solution)/shard_map/slice | solution.py:297
  1.3 1.5 %collective-permute-start.1 = (bf16[32,48,384]{2,1,0:T(8,128)(2,1)}, bf16[32,48,384]{2,1,0:T(8,128)(2,1)S(1)}, u32[]{:S(2)}, u32[]{:S(2)}) collective-permute-start(bf16[32,48,384]{2,1,0:T(8,128)(2,1)} %bitcast.6), channel_id=1, source_target_pairs={{0,1},{1,0},{2,3},{3,2},{4,5},{5,4},{6,7},{7,6},{8,9},{9,8},{10,11... | collective-permute-start | bytes 3538952 | tf_op jit(solution)/shard_map/ppermute | solution.py:300
  2.8 3.7 %collective-permute-start.2 = (bf16[20,48,384]{2,1,0:T(8,128)(2,1)S(1)}, bf16[20,48,384]{2,1,0:T(8,128)(2,1)S(1)}, u32[]{:S(2)}, u32[]{:S(2)}) collective-permute-start(bf16[20,48,384]{2,1,0:T(8,128)(2,1)S(1)} %slice_bitcast_fusion), channel_id=1, source_target_pairs={{0,127},{1,2},{2,1},{3,4},{4,3},{5,6},{6,5},{7,8},{8,7},{9,10},{10... | collective-permute-start | bytes 2211848 | tf_op jit(solution)/shard_map/ppermute | solution.py:298
  6.5 1.1 %slice.14 = bf16[12,48,384]{2,1,0:T(8,128)(2,1)S(1)} slice(bf16[32,48,384]{2,1,0:T(8,128)(2,1)} %bitcast.7), slice={[20:32], [0:48], [0:384]} | slice | bytes 884736 | tf_op jit(solution)/shard_map/slice | solution.py:299
  7.5 0.1 collective-permute-start.3
  7.6 0.0 copy-done.5
  7.6 0.0 copy-done.6
  7.7 0.0 collective-permute-done.1.twin
  7.7 0.0 copy-done.2
  7.7 0.0 copy-done.4
  7.7 0.0 copy-start
  7.7 3.3 %copy-done = bf16[3,3,3,384,384]{4,3,2,1,0:T(8,128)(2,1)S(1)} copy-done((bf16[3,3,3,384,384]{4,3,2,1,0:T(8,128)(2,1)S(1)}, bf16[3,3,3,384,384]{4,3,2,1,0:T(8,128)(2,1)}, u32[]{:S(2)}) %copy-start) | copy-done | bytes 7962648
  11.0 0.0 copy-start.1
  11.0 12.7 %shard_map.57 = (f32[32,48,384]{2,1,0:T(8,128)S(1)}, s32[1]{0:T(128)}) custom-call(s32[16]{0:T(128)S(1)} %copy-done.4, bf16[32,48,384]{2,1,0:T(8,128)(2,1)S(1)} %bitcast.8, bf16[32,48,384]{2,1,0:T(8,128)(2,1)S(1)} %collective-permute-done.1.twin, bf16[3,3,3,384,384]{4,3,2,1,0:T(8,128)(2,1)S(1)} %copy-done, f32[1,384]{1,0:T(1,128)S(1)} %reshape.10.gain, ...), custom_call_target="tpu_custom_call" | custom-call | tf_op jit(solution)/shard_map/pallas_call | solution.py:99
  23.6 3.9 %collective-permute-done.2.far.recent = bf16[20,48,384]{2,1,0:T(8,128)(2,1)S(1)} collective-permute-done((bf16[20,48,384]{2,1,0:T(8,128)(2,1)S(1)}, bf16[20,48,384]{2,1,0:T(8,128)(2,1)S(1)}, u32[]{:S(2)}, u32[]{:S(2)}) %collective-permute-start.2) | collective-permute-done | bytes 737312 | tf_op jit(solution)/shard_map/ppermute | solution.py:298
  27.5 0.0 copy-done.1
  27.5 3.9 %shard_map.58.early = bf16[20,48,384]{2,1,0:T(8,128)(2,1)S(1)} custom-call(bf16[20,48,384]{2,1,0:T(8,128)(2,1)S(1)} %collective-permute-done.2.far.recent, f32[32,48,384]{2,1,0:T(8,128)S(1)} %get-tuple-element.29.partial, bf16[3,3,3,384,384]{4,3,2,1,0:T(8,128)(2,1)S(1)} %copy-done.1, f32[1,384]{1,0:T(1,128)S(1)} %reshape.10.gain), custom_call_target="tpu_custom_call" | custom-call | tf_op jit(solution)/shard_map/pallas_call | solution.py:188
  31.5 1.5 %collective-permute-done.3.far = bf16[12,48,384]{2,1,0:T(8,128)(2,1)S(1)} collective-permute-done((bf16[12,48,384]{2,1,0:T(8,128)(2,1)S(1)}, bf16[12,48,384]{2,1,0:T(8,128)(2,1)S(1)}, u32[]{:S(2)}, u32[]{:S(2)}) %collective-permute-start.3) | collective-permute-done | bytes 442400 | tf_op jit(solution)/shard_map/ppermute | solution.py:299
  33.0 3.2 %shard_map.59 = (bf16[16,3,48,384]{3,2,1,0:T(8,128)(2,1)S(1)}, bf16[16,4,48,384]{3,2,1,0:T(8,128)(2,1)S(1)}) custom-call(s32[16]{0:T(128)S(1)} %copy-done.4, bf16[20,48,384]{2,1,0:T(8,128)(2,1)S(1)} %collective-permute-done.2.far.recent, bf16[12,48,384]{2,1,0:T(8,128)(2,1)S(1)} %collective-permute-done.3.far, bf16[20,48,384]{2,1,0:T(8,128)(2,1)S(1)} %shard_map.58.early, ...), custom_call_target="tpu_custom_call" | custom-call | tf_op jit(solution)/shard_map/pallas_call | solution.py:200
  36.9 35.9 %conditional.1 = (bf16[4,16,48,384]{3,2,1,0:T(8,128)(2,1)S(1)}) conditional(s32[]{:T(128)} %bitcast.3, (bf16[16,4,48,384]{3,2,1,0:T(8,128)(2,1)S(1)}, s32[16]{0:T(128)S(1)}) %tuple.20, (bf16[16,3,48,384]{3,2,1,0:T(8,128)(2,1)S(1)}, s32[16]{0:T(128)S(1)}) %tuple.21), branch_computations={%region_0.0_spmd, %region_1.0_spmd} | conditional | bytes 5898288 | solution.py:306
  36.9 32.3 %all_to_all.9.arrived = bf16[16,3,48,384]{3,2,1,0:T(8,128)(2,1)S(1)} all-to-all(bf16[16,3,48,384]{3,2,1,0:T(8,128)(2,1)S(1)} %get-tuple-element.19), channel_id=1, replica_groups=mesh['ha'=8,'tc'=8,'core'=2] {'tc','core'}, dimensions={0} | all-to-all | bytes 3538944 | tf_op jit(solution)/shard_map/cond/branch_1_fun/all_to_all | solution.py:253
  69.2 0.6 branch_1_fun.2
  69.8 0.5 collective-permute-start
  70.3 1.6 %collective-permute-done.other = bf16[16,1,48,384]{3,2,1,0:T(8,128)(2,1)S(1)} collective-permute-done((bf16[16,1,48,384]{3,2,1,0:T(8,128)(2,1)S(1)}, bf16[16,1,48,384]{3,2,1,0:T(8,128)(2,1)S(1)}, u32[]{:S(2)}, u32[]{:S(2)}) %collective-permute-start) | collective-permute-done | bytes 589856 | tf_op jit(solution)/shard_map/cond/branch_1_fun/ppermute | solution.py:279
  72.0 0.8 %branch_1_fun.3 = bf16[4,16,48,384]{3,2,1,0:T(8,128)(2,1)S(1)} custom-call(s32[16]{0:T(128)S(1)} %get-tuple-element.18.starts, bf16[16,3,48,384]{3,2,1,0:T(8,128)(2,1)S(1)} %all_to_all.9.arrived, bf16[16,1,48,384]{3,2,1,0:T(8,128)(2,1)S(1)} %collective-permute-done.other), custom_call_target="tpu_custom_call" | custom-call | tf_op jit(solution)/shard_map/cond/branch_1_fun/pallas_call | solution.py:243
  72.8 0.0 copy-start.3
  72.8 1.4 %copy-done.3 = bf16[4,16,48,384]{3,2,1,0:T(8,128)(2,1)} copy-done((bf16[4,16,48,384]{3,2,1,0:T(8,128)(2,1)}, bf16[4,16,48,384]{3,2,1,0:T(8,128)(2,1)S(1)}, u32[]{:S(2)}) %copy-start.3) | copy-done | bytes 2359320
  (2 shorter events, 0.0 us)
Async XLA Ops:
  0.0 7.7 %copy-start.2 = (bf16[32,1,48,384]{3,2,1,0:T(8,128)(2,1)S(1)}, bf16[32,1,48,384]{3,2,1,0:T(8,128)(2,1)}, u32[]{:S(2)}) copy-start(bf16[32,1,48,384]{3,2,1,0:T(8,128)(2,1)} %param.7) | copy-start | bytes 3538948
  0.0 7.6 %copy-start.5 = (f32[384]{0:T(512)S(1)}, f32[384]{0:T(512)}, u32[]{:S(2)}) copy-start(f32[384]{0:T(512)} %param.9) | copy-start | bytes 4612
  0.0 7.6 %copy-start.6 = (f32[384]{0:T(512)S(1)}, f32[384]{0:T(512)}, u32[]{:S(2)}) copy-start(f32[384]{0:T(512)} %param.11) | copy-start | bytes 4612
  0.0 7.7 %copy-start.4 = (s32[16]{0:T(128)S(1)}, s32[16]{0:T(128)}, u32[]{:S(2)}) copy-start(s32[16]{0:T(128)} %starts.3) | copy-start | bytes 196
  1.3 6.4 %collective-permute-start.1 = (bf16[32,48,384]{2,1,0:T(8,128)(2,1)}, bf16[32,48,384]{2,1,0:T(8,128)(2,1)S(1)}, u32[]{:S(2)}, u32[]{:S(2)}) collective-permute-start(bf16[32,48,384]{2,1,0:T(8,128)(2,1)} %bitcast.6), channel_id=1, source_target_pairs={{0,1},{1,0},{2,3},{3,2},{4,5},{5,4},{6,7},{7,6},{8,9},{9,8},{10,11... | collective-permute-start | bytes 3538952 | tf_op jit(solution)/shard_map/ppermute | solution.py:300
  2.8 24.7 %collective-permute-start.2 = (bf16[20,48,384]{2,1,0:T(8,128)(2,1)S(1)}, bf16[20,48,384]{2,1,0:T(8,128)(2,1)S(1)}, u32[]{:S(2)}, u32[]{:S(2)}) collective-permute-start(bf16[20,48,384]{2,1,0:T(8,128)(2,1)S(1)} %slice_bitcast_fusion), channel_id=1, source_target_pairs={{0,127},{1,2},{2,1},{3,4},{4,3},{5,6},{6,5},{7,8},{8,7},{9,10},{10... | collective-permute-start | bytes 2211848 | tf_op jit(solution)/shard_map/ppermute | solution.py:298
  7.5 25.5 %collective-permute-start.3 = (bf16[12,48,384]{2,1,0:T(8,128)(2,1)S(1)}, bf16[12,48,384]{2,1,0:T(8,128)(2,1)S(1)}, u32[]{:S(2)}, u32[]{:S(2)}) collective-permute-start(bf16[12,48,384]{2,1,0:T(8,128)(2,1)S(1)} %slice.14), channel_id=1, source_target_pairs={{0,127},{1,2},{2,1},{3,4},{4,3},{5,6},{6,5},{7,8},{8,7},{9,10},{10... | collective-permute-start | bytes 1327112 | tf_op jit(solution)/shard_map/ppermute | solution.py:299
  7.7 3.3 %copy-start = (bf16[3,3,3,384,384]{4,3,2,1,0:T(8,128)(2,1)S(1)}, bf16[3,3,3,384,384]{4,3,2,1,0:T(8,128)(2,1)}, u32[]{:S(2)}) copy-start(bf16[3,3,3,384,384]{4,3,2,1,0:T(8,128)(2,1)} %weight.5) | copy-start | bytes 23887876
  11.0 16.6 %copy-start.1 = (bf16[3,3,3,384,384]{4,3,2,1,0:T(8,128)(2,1)S(1)}, bf16[3,3,3,384,384]{4,3,2,1,0:T(8,128)(2,1)}, u32[]{:S(2)}) copy-start(bf16[3,3,3,384,384]{4,3,2,1,0:T(8,128)(2,1)} %weight.5) | copy-start | bytes 23887876
  69.8 2.1 %collective-permute-start = (bf16[16,1,48,384]{3,2,1,0:T(8,128)(2,1)S(1)}, bf16[16,1,48,384]{3,2,1,0:T(8,128)(2,1)S(1)}, u32[]{:S(2)}, u32[]{:S(2)}) collective-permute-start(bf16[16,1,48,384]{3,2,1,0:T(8,128)(2,1)S(1)} %branch_1_fun.2), channel_id=1, source_target_pairs={{0,1},{1,0},{2,3},{3,2},{4,5},{5,4},{6,7},{7,6},{8,9},{9,8},{10,11... | collective-permute-start | bytes 1769480 | tf_op jit(solution)/shard_map/cond/branch_1_fun/ppermute | solution.py:279
  72.8 1.4 %copy-start.3 = (bf16[4,16,48,384]{3,2,1,0:T(8,128)(2,1)}, bf16[4,16,48,384]{3,2,1,0:T(8,128)(2,1)S(1)}, u32[]{:S(2)}) copy-start(bf16[4,16,48,384]{3,2,1,0:T(8,128)(2,1)S(1)} %get-tuple-element.41) | copy-start | bytes 7077892

commit v13 on v12

--- a/solution.py
+++ b/solution.py
@@ -211,42 +211,78 @@
     )(starts, recent, far, early, partial, weight, gain)
 
 
-def unpack_kernel(total, starts, arrived, other, out):
-    slots = arrived.shape[1]
+def slots_of(starts, total, slots):
     core = lax.axis_index("core")
     group = lax.axis_index("tc") * lax.axis_size("core") + core
     start = starts[group]
     after = after_of(starts, group, total)
-    length = after - start
     held = start
     if slots < FMAX:
         held = jnp.clip(jnp.where(core == 1, after - slots, start), 0, total - slots)
+    found = []
     for k in range(FMAX):
         slot = start + k - held
         inside = jnp.logical_and(slot >= 0, slot < slots)
-
-        @pl.when(jnp.logical_and(k < length, inside))
+        found.append((k < after - start, inside, jnp.clip(slot, 0, slots - 1)))
+    return found
+
+
+def unpack_kernel(total, starts, arrived, out, blank, sems):
+    found = slots_of(starts, total, arrived.shape[1])
+    blank[...] = jnp.zeros(blank.shape, blank.dtype)
+    for k, (used, inside, slot) in enumerate(found):
+
+        @pl.when(jnp.logical_and(used, inside))
         def _():
-            out[k] = arrived[:, jnp.clip(slot, 0, slots - 1)]
-
-        @pl.when(jnp.logical_and(k < length, jnp.logical_not(inside)))
+            pltpu.make_async_copy(arrived.at[:, slot], out.at[k], sems.at[k]).start()
+
+        @pl.when(jnp.logical_not(used))
         def _():
-            out[k] = other[:, 0]
-
-        @pl.when(k >= length)
+            pltpu.make_async_copy(blank, out.at[k], sems.at[k]).start()
+
+    for k, (used, inside, slot) in enumerate(found):
+
+        @pl.when(jnp.logical_or(inside, jnp.logical_not(used)))
         def _():
-            out[k] = jnp.zeros(out.shape[1:], out.dtype)
-
-
-def unpack(total, starts, arrived, other):
+            pltpu.make_async_copy(blank, out.at[k], sems.at[k]).wait()
+
+
+def unpack(total, starts, arrived):
     rows, _, cols, chans = arrived.shape
     return pl.pallas_call(
         functools.partial(unpack_kernel, total),
         out_shape=jax.ShapeDtypeStruct((FMAX, rows, cols, chans), arrived.dtype),
-        in_specs=[SMEM_SPEC, VMEM_SPEC, VMEM_SPEC],
-        out_specs=VMEM_SPEC,
+        in_specs=[SMEM_SPEC, VMEM_SPEC],
+        out_specs=HBM_SPEC,
+        scratch_shapes=[
+            pltpu.VMEM((rows, cols, chans), arrived.dtype),
+            pltpu.SemaphoreType.DMA((FMAX,)),
+        ],
         compiler_params=pltpu.CompilerParams(vmem_limit_bytes=UNPACK_VMEM_BYTES),
-    )(starts, arrived, other)
+    )(starts, arrived)
+
+
+def patch_kernel(total, starts, other, partial, out, sem):
+    del partial
+    for k, (used, inside, _) in enumerate(slots_of(starts, total, FMAX - 1)):
+
+        @pl.when(jnp.logical_and(used, jnp.logical_not(inside)))
+        def _():
+            copy = pltpu.make_async_copy(other.at[:, 0], out.at[k], sem)
+            copy.start()
+            copy.wait()
+
+
+def patch(total, starts, other, partial):
+    return pl.pallas_call(
+        functools.partial(patch_kernel, total),
+        out_shape=jax.ShapeDtypeStruct(partial.shape, partial.dtype),
+        in_specs=[SMEM_SPEC, VMEM_SPEC, HBM_SPEC],
+        out_specs=HBM_SPEC,
+        scratch_shapes=[pltpu.SemaphoreType.DMA],
+        input_output_aliases={2: 0},
+        compiler_params=pltpu.CompilerParams(vmem_limit_bytes=UNPACK_VMEM_BYTES),
+    )(starts, other, partial)
 
 
 def regroup(packed):
@@ -277,13 +313,13 @@
     del many
     arrived = regroup(few)
     other = lax.ppermute(pick(total, starts, arrived), "core", [(0, 1), (1, 0)])
-    return unpack(total, starts, arrived, other)
+    return patch(total, starts, other, unpack(total, starts, arrived))
 
 
 def send_many(total, few, many, starts):
     del few
     arrived = regroup(many)
-    return unpack(total, starts, arrived, arrived[:, :1])
+    return unpack(total, starts, arrived)
 
 
 def on_device(latent, group_start, norm_gain, conv_weight, conv_bias):

time: 74.4 us -> 73.2 us (0.984)
  Pallas kernels: 21.2 us -> 23 us
  waiting for transfers between devices: 7.05 us -> 5.42 us
  local copies, waits for them, and re-layouts: 7.02 us -> 5.62 us
    ppermute x1, waiting for transfers between devices: 1.63 us -> 0.01 us  [send_few(): other = lax.ppermute(pick(total, starts, arrived), 'core', [(0, 1), (1, 0)])]
    unnamed x14 -> x12, local copies, waits for them, and re-layouts: 4.67 us -> 3.27 us
    pallas_call x1, Pallas kernels: 0.82 us -> 1.99 us  [unpack(): pl.pallas_call(functools.partial(unpack_kernel, total), out_shape=jax.Sha...]
  transfers between devices with their start and end apart: 4 -> 4, of which waited for: 3 -> 2; matrix products, arithmetic and copies ran while one was open for 1% -> 1% of each run, Pallas kernels for 22% -> 26%
where the time goes in v13:
time: 73.2 us; the launch traced here: 72.9 us
  blocking collectives  32.3 us (44%)
  Pallas kernels  23 us (31%)
  starting transfers between devices  5.74 us (8%)
  local copies, waits for them, and re-layouts  5.62 us (8%)
  waiting for transfers between devices  5.42 us (7%)
  between operations  0.76 us (1%)
    all_to_all x1, blocking collectives, regroup(): lax.all_to_all(packed, ('tc', 'core'), split_axis=0, concat_axis=0, tiled...  32.3 us
    pallas_call x1, Pallas kernels, near_rows(): pl.pallas_call(near_kernel, out_shape=[jax.ShapeDtypeStruct(own.shape, jn...  12.7 us
    pallas_call x1, Pallas kernels, early_rows(): pl.pallas_call(early_kernel, out_shape=jax.ShapeDtypeStruct(far.shape, jn...  3.95 us
    ppermute x1, waiting for transfers between devices, on_device(): early_far = lax.ppermute(front, ('ha', 'tc', 'core'), pairs)  3.9 us
    ppermute x1, starting transfers between devices, on_device(): early_far = lax.ppermute(front, ('ha', 'tc', 'core'), pairs)  3.67 us
    unnamed x12, local copies, waits for them, and re-layouts  3.27 us
    pallas_call x1, Pallas kernels, late_rows(): pl.pallas_call(late_kernel, out_shape=[jax.ShapeDtypeStruct((starts.shape...  3.22 us
    pallas_call x1, Pallas kernels, unpack(): pl.pallas_call(functools.partial(unpack_kernel, total), out_shape=jax.Sha...  1.99 us
  transfers between devices with their start and end apart: 4, of which 2 were waited for; matrix products, arithmetic and copies ran while one was open for 1% of the time, Pallas kernels for 26%

profile of v13, /device:TPU:1, one launch (start us, length us, event | category | flops | bytes accessed | tf_op | source)
XLA Modules:
  0.0 72.9 jit_solution(2129465173336385730)
XLA Ops:
  0.0 0.0 copy-start.2
  0.0 0.0 copy-start.4
  0.0 0.0 copy-start.5
  0.0 0.0 copy-start.3
  0.0 1.3 %slice_bitcast_fusion = bf16[20,48,384]{2,1,0:T(8,128)(2,1)S(1)} fusion(bf16[32,1,48,384]{3,2,0,1:T(8,128)(2,1)} %bitcast.5), kind=kLoop, calls=%fused_computation | loop fusion | bytes 1474560 | tf_op jit(solution)/shard_map/slice | solution.py:333
  1.3 1.5 %collective-permute-start.1 = (bf16[32,48,384]{2,1,0:T(8,128)(2,1)}, bf16[32,48,384]{2,1,0:T(8,128)(2,1)S(1)}, u32[]{:S(2)}, u32[]{:S(2)}) collective-permute-start(bf16[32,48,384]{2,1,0:T(8,128)(2,1)} %bitcast.6), channel_id=1, source_target_pairs={{0,1},{1,0},{2,3},{3,2},{4,5},{5,4},{6,7},{7,6},{8,9},{9,8},{10,11... | collective-permute-start | bytes 3538952 | tf_op jit(solution)/shard_map/ppermute | solution.py:336
  2.8 3.7 %collective-permute-start.2 = (bf16[20,48,384]{2,1,0:T(8,128)(2,1)S(1)}, bf16[20,48,384]{2,1,0:T(8,128)(2,1)S(1)}, u32[]{:S(2)}, u32[]{:S(2)}) collective-permute-start(bf16[20,48,384]{2,1,0:T(8,128)(2,1)S(1)} %slice_bitcast_fusion), channel_id=1, source_target_pairs={{0,127},{1,2},{2,1},{3,4},{4,3},{5,6},{6,5},{7,8},{8,7},{9,10},{10... | collective-permute-start | bytes 2211848 | tf_op jit(solution)/shard_map/ppermute | solution.py:334
  6.5 1.1 %slice.11 = bf16[12,48,384]{2,1,0:T(8,128)(2,1)S(1)} slice(bf16[32,48,384]{2,1,0:T(8,128)(2,1)} %bitcast.7), slice={[20:32], [0:48], [0:384]} | slice | bytes 884736 | tf_op jit(solution)/shard_map/slice | solution.py:335
  7.5 0.1 collective-permute-start.3
  7.6 0.0 copy-done.4
  7.6 0.0 copy-done.5
  7.7 0.0 collective-permute-done.1.twin
  7.7 0.0 copy-done.2
  7.7 0.0 copy-done.3
  7.7 0.0 copy-start
  7.7 3.3 %copy-done = bf16[3,3,3,384,384]{4,3,2,1,0:T(8,128)(2,1)S(1)} copy-done((bf16[3,3,3,384,384]{4,3,2,1,0:T(8,128)(2,1)S(1)}, bf16[3,3,3,384,384]{4,3,2,1,0:T(8,128)(2,1)}, u32[]{:S(2)}) %copy-start) | copy-done | bytes 7962648
  11.0 0.0 copy-start.1
  11.0 12.7 %shard_map.57 = (f32[32,48,384]{2,1,0:T(8,128)S(1)}, s32[1]{0:T(128)}) custom-call(s32[16]{0:T(128)S(1)} %copy-done.3, bf16[32,48,384]{2,1,0:T(8,128)(2,1)S(1)} %bitcast.8, bf16[32,48,384]{2,1,0:T(8,128)(2,1)S(1)} %collective-permute-done.1.twin, bf16[3,3,3,384,384]{4,3,2,1,0:T(8,128)(2,1)S(1)} %copy-done, f32[1,384]{1,0:T(1,128)S(1)} %reshape.10.gain, ...), custom_call_target="tpu_custom_call" | custom-call | tf_op jit(solution)/shard_map/pallas_call | solution.py:99
  23.6 3.9 %collective-permute-done.2.far.recent = bf16[20,48,384]{2,1,0:T(8,128)(2,1)S(1)} collective-permute-done((bf16[20,48,384]{2,1,0:T(8,128)(2,1)S(1)}, bf16[20,48,384]{2,1,0:T(8,128)(2,1)S(1)}, u32[]{:S(2)}, u32[]{:S(2)}) %collective-permute-start.2) | collective-permute-done | bytes 737312 | tf_op jit(solution)/shard_map/ppermute | solution.py:334
  27.5 0.0 copy-done.1
  27.5 3.9 %shard_map.58.early = bf16[20,48,384]{2,1,0:T(8,128)(2,1)S(1)} custom-call(bf16[20,48,384]{2,1,0:T(8,128)(2,1)S(1)} %collective-permute-done.2.far.recent, f32[32,48,384]{2,1,0:T(8,128)S(1)} %get-tuple-element.29.partial, bf16[3,3,3,384,384]{4,3,2,1,0:T(8,128)(2,1)S(1)} %copy-done.1, f32[1,384]{1,0:T(1,128)S(1)} %reshape.10.gain), custom_call_target="tpu_custom_call" | custom-call | tf_op jit(solution)/shard_map/pallas_call | solution.py:188
  31.5 1.5 %collective-permute-done.3.far = bf16[12,48,384]{2,1,0:T(8,128)(2,1)S(1)} collective-permute-done((bf16[12,48,384]{2,1,0:T(8,128)(2,1)S(1)}, bf16[12,48,384]{2,1,0:T(8,128)(2,1)S(1)}, u32[]{:S(2)}, u32[]{:S(2)}) %collective-permute-start.3) | collective-permute-done | bytes 442400 | tf_op jit(solution)/shard_map/ppermute | solution.py:335
  33.0 3.2 %shard_map.59 = (bf16[16,3,48,384]{3,2,1,0:T(8,128)(2,1)S(1)}, bf16[16,4,48,384]{3,2,1,0:T(8,128)(2,1)S(1)}) custom-call(s32[16]{0:T(128)S(1)} %copy-done.3, bf16[20,48,384]{2,1,0:T(8,128)(2,1)S(1)} %collective-permute-done.2.far.recent, bf16[12,48,384]{2,1,0:T(8,128)(2,1)S(1)} %collective-permute-done.3.far, bf16[20,48,384]{2,1,0:T(8,128)(2,1)S(1)} %shard_map.58.early, ...), custom_call_target="tpu_custom_call" | custom-call | tf_op jit(solution)/shard_map/pallas_call | solution.py:200
  36.9 36.0 %conditional.1 = (bf16[4,16,48,384]{3,2,1,0:T(8,128)(2,1)}) conditional(s32[]{:T(128)} %bitcast.3, (bf16[16,4,48,384]{3,2,1,0:T(8,128)(2,1)S(1)}, s32[16]{0:T(128)S(1)}) %tuple.19, (bf16[16,3,48,384]{3,2,1,0:T(8,128)(2,1)S(1)}, s32[16]{0:T(128)S(1)}) %tuple.20), branch_computations={%region_0.0_spmd, %region_1.0_spmd} | conditional | bytes 5898288 | solution.py:342
  36.9 32.3 %all_to_all.9.arrived = bf16[16,3,48,384]{3,2,1,0:T(8,128)(2,1)S(1)} all-to-all(bf16[16,3,48,384]{3,2,1,0:T(8,128)(2,1)S(1)} %get-tuple-element.19), channel_id=1, replica_groups=mesh['ha'=8,'tc'=8,'core'=2] {'tc','core'}, dimensions={0} | all-to-all | bytes 3538944 | tf_op jit(solution)/shard_map/cond/branch_1_fun/all_to_all | solution.py:289
  69.2 0.6 branch_1_fun.3
  69.8 0.5 collective-permute-start
  70.3 2.0 %branch_1_fun.4.partial = bf16[4,16,48,384]{3,2,1,0:T(8,128)(2,1)} custom-call(s32[16]{0:T(128)S(1)} %get-tuple-element.18.starts, bf16[16,3,48,384]{3,2,1,0:T(8,128)(2,1)S(1)} %all_to_all.9.arrived), custom_call_target="tpu_custom_call" | custom-call | tf_op jit(solution)/shard_map/cond/branch_1_fun/pallas_call | solution.py:252
  72.3 0.0 collective-permute-done.other
  72.3 0.6 branch_1_fun.5
  (2 shorter events, 0.0 us)
Async XLA Ops:
  0.0 7.7 %copy-start.2 = (bf16[32,1,48,384]{3,2,1,0:T(8,128)(2,1)S(1)}, bf16[32,1,48,384]{3,2,1,0:T(8,128)(2,1)}, u32[]{:S(2)}) copy-start(bf16[32,1,48,384]{3,2,1,0:T(8,128)(2,1)} %param.7) | copy-start | bytes 3538948
  0.0 7.6 %copy-start.4 = (f32[384]{0:T(512)S(1)}, f32[384]{0:T(512)}, u32[]{:S(2)}) copy-start(f32[384]{0:T(512)} %param.9) | copy-start | bytes 4612
  0.0 7.6 %copy-start.5 = (f32[384]{0:T(512)S(1)}, f32[384]{0:T(512)}, u32[]{:S(2)}) copy-start(f32[384]{0:T(512)} %param.11) | copy-start | bytes 4612
  0.0 7.7 %copy-start.3 = (s32[16]{0:T(128)S(1)}, s32[16]{0:T(128)}, u32[]{:S(2)}) copy-start(s32[16]{0:T(128)} %starts.3) | copy-start | bytes 196
  1.3 6.4 %collective-permute-start.1 = (bf16[32,48,384]{2,1,0:T(8,128)(2,1)}, bf16[32,48,384]{2,1,0:T(8,128)(2,1)S(1)}, u32[]{:S(2)}, u32[]{:S(2)}) collective-permute-start(bf16[32,48,384]{2,1,0:T(8,128)(2,1)} %bitcast.6), channel_id=1, source_target_pairs={{0,1},{1,0},{2,3},{3,2},{4,5},{5,4},{6,7},{7,6},{8,9},{9,8},{10,11... | collective-permute-start | bytes 3538952 | tf_op jit(solution)/shard_map/ppermute | solution.py:336
  2.8 24.7 %collective-permute-start.2 = (bf16[20,48,384]{2,1,0:T(8,128)(2,1)S(1)}, bf16[20,48,384]{2,1,0:T(8,128)(2,1)S(1)}, u32[]{:S(2)}, u32[]{:S(2)}) collective-permute-start(bf16[20,48,384]{2,1,0:T(8,128)(2,1)S(1)} %slice_bitcast_fusion), channel_id=1, source_target_pairs={{0,127},{1,2},{2,1},{3,4},{4,3},{5,6},{6,5},{7,8},{8,7},{9,10},{10... | collective-permute-start | bytes 2211848 | tf_op jit(solution)/shard_map/ppermute | solution.py:334
  7.5 25.5 %collective-permute-start.3 = (bf16[12,48,384]{2,1,0:T(8,128)(2,1)S(1)}, bf16[12,48,384]{2,1,0:T(8,128)(2,1)S(1)}, u32[]{:S(2)}, u32[]{:S(2)}) collective-permute-start(bf16[12,48,384]{2,1,0:T(8,128)(2,1)S(1)} %slice.11), channel_id=1, source_target_pairs={{0,127},{1,2},{2,1},{3,4},{4,3},{5,6},{6,5},{7,8},{8,7},{9,10},{10... | collective-permute-start | bytes 1327112 | tf_op jit(solution)/shard_map/ppermute | solution.py:335
  7.7 3.3 %copy-start = (bf16[3,3,3,384,384]{4,3,2,1,0:T(8,128)(2,1)S(1)}, bf16[3,3,3,384,384]{4,3,2,1,0:T(8,128)(2,1)}, u32[]{:S(2)}) copy-start(bf16[3,3,3,384,384]{4,3,2,1,0:T(8,128)(2,1)} %weight.5) | copy-start | bytes 23887876
  11.0 16.6 %copy-start.1 = (bf16[3,3,3,384,384]{4,3,2,1,0:T(8,128)(2,1)S(1)}, bf16[3,3,3,384,384]{4,3,2,1,0:T(8,128)(2,1)}, u32[]{:S(2)}) copy-start(bf16[3,3,3,384,384]{4,3,2,1,0:T(8,128)(2,1)} %weight.5) | copy-start | bytes 23887876
  69.8 2.5 %collective-permute-start = (bf16[16,1,48,384]{3,2,1,0:T(8,128)(2,1)S(1)}, bf16[16,1,48,384]{3,2,1,0:T(8,128)(2,1)S(1)}, u32[]{:S(2)}, u32[]{:S(2)}) collective-permute-start(bf16[16,1,48,384]{3,2,1,0:T(8,128)(2,1)S(1)} %branch_1_fun.3), channel_id=1, source_target_pairs={{0,1},{1,0},{2,3},{3,2},{4,5},{5,4},{6,7},{7,6},{8,9},{9,8},{10,11... | collective-permute-start | bytes 1769480 | tf_op jit(solution)/shard_map/cond/branch_1_fun/ppermute | solution.py:315

commit v14 on v13

--- a/solution.py
+++ b/solution.py
@@ -47,21 +47,22 @@
         axis=1,
     )
     part = jnp.dot(lhs, taps_of(weight, row_taps), preferred_element_type=jnp.float32)
-    for e in range(3):
-        sums[e, pl.ds(0, count), 8 : cols + 8, :] = part[:, e * chans : (e + 1) * chans].reshape(
-            count, cols, chans
-        )
+    left, middle, right = (
+        part[:, e * chans : (e + 1) * chans].reshape(count, cols, chans) for e in range(3)
+    )
+    sums[0, pl.ds(0, count), 8 : cols + 8, :] = left
+    sums[1, pl.ds(0, count), 8 : cols + 8, :] = right
     return (
         sums[0, pl.ds(0, count), 7 : cols + 7, :]
-        + sums[1, pl.ds(0, count), 8 : cols + 8, :]
-        + sums[2, pl.ds(0, count), 9 : cols + 9, :]
+        + middle
+        + sums[1, pl.ds(0, count), 9 : cols + 9, :]
     )
 
 
 def clear_sides(sums, cols):
     shape = (sums.shape[1], 1, sums.shape[3])
     sums[0, :, 7:8, :] = jnp.zeros(shape, jnp.float32)
-    sums[2, :, cols + 8 : cols + 9, :] = jnp.zeros(shape, jnp.float32)
+    sums[1, :, cols + 8 : cols + 9, :] = jnp.zeros(shape, jnp.float32)
 
 
 def near_kernel(
@@ -107,7 +108,7 @@
         scratch_shapes=[
             pltpu.VMEM((HIST + total, cols, chans), jnp.bfloat16),
             pltpu.VMEM((HIST + total, cols, chans), jnp.bfloat16),
-            pltpu.VMEM((3, STEP, cols + 16, chans), jnp.float32),
+            pltpu.VMEM((2, STEP, cols + 16, chans), jnp.float32),
         ],
         compiler_params=pltpu.CompilerParams(vmem_limit_bytes=NEAR_VMEM_BYTES),
     )(starts, own, twin, weight, gain, bias)
@@ -180,7 +181,7 @@
 def far_scratch(count, cols, chans):
     return [
         pltpu.VMEM((HIST + count, cols, chans), jnp.bfloat16),
-        pltpu.VMEM((3, count, cols + 16, chans), jnp.float32),
+        pltpu.VMEM((2, count, cols + 16, chans), jnp.float32),
     ]
 
 

time: 73.2 us -> 73.2 us (level)
  transfers between devices with their start and end apart: 4 -> 4, of which waited for: 2 -> 2; matrix products, arithmetic and copies ran while one was open for 1% -> 1% of each run, Pallas kernels for 26% -> 25%
where the time goes in v14:
time: 73.2 us; the launch traced here: 72.9 us
  blocking collectives  32.3 us (44%)
  Pallas kernels  23 us (31%)
  starting transfers between devices  5.74 us (8%)
  local copies, waits for them, and re-layouts  5.62 us (8%)
  waiting for transfers between devices  5.44 us (7%)
  between operations  0.76 us (1%)
    all_to_all x1, blocking collectives, regroup(): lax.all_to_all(packed, ('tc', 'core'), split_axis=0, concat_axis=0, tiled...  32.3 us
    pallas_call x1, Pallas kernels, near_rows(): pl.pallas_call(near_kernel, out_shape=[jax.ShapeDtypeStruct(own.shape, jn...  12.6 us
    pallas_call x1, Pallas kernels, early_rows(): pl.pallas_call(early_kernel, out_shape=jax.ShapeDtypeStruct(far.shape, jn...  3.95 us
    ppermute x1, waiting for transfers between devices, on_device(): early_far = lax.ppermute(front, ('ha', 'tc', 'core'), pairs)  3.91 us
    ppermute x1, starting transfers between devices, on_device(): early_far = lax.ppermute(front, ('ha', 'tc', 'core'), pairs)  3.67 us
    unnamed x12, local copies, waits for them, and re-layouts  3.27 us
    pallas_call x1, Pallas kernels, late_rows(): pl.pallas_call(late_kernel, out_shape=[jax.ShapeDtypeStruct((starts.shape...  3.24 us
    pallas_call x1, Pallas kernels, unpack(): pl.pallas_call(functools.partial(unpack_kernel, total), out_shape=jax.Sha...  1.99 us
  transfers between devices with their start and end apart: 4, of which 2 were waited for; matrix products, arithmetic and copies ran while one was open for 1% of the time, Pallas kernels for 25%

profile of v14, /device:TPU:1, one launch (start us, length us, event | category | flops | bytes accessed | tf_op | source)
XLA Modules:
  0.0 72.9 jit_solution(833260721581888415)
XLA Ops:
  0.0 0.0 copy-start.2
  0.0 0.0 copy-start.4
  0.0 0.0 copy-start.5
  0.0 0.0 copy-start.3
  0.0 1.3 %slice_bitcast_fusion = bf16[20,48,384]{2,1,0:T(8,128)(2,1)S(1)} fusion(bf16[32,1,48,384]{3,2,0,1:T(8,128)(2,1)} %bitcast.5), kind=kLoop, calls=%fused_computation | loop fusion | bytes 1474560 | tf_op jit(solution)/shard_map/slice | solution.py:334
  1.3 1.5 %collective-permute-start.1 = (bf16[32,48,384]{2,1,0:T(8,128)(2,1)}, bf16[32,48,384]{2,1,0:T(8,128)(2,1)S(1)}, u32[]{:S(2)}, u32[]{:S(2)}) collective-permute-start(bf16[32,48,384]{2,1,0:T(8,128)(2,1)} %bitcast.6), channel_id=1, source_target_pairs={{0,1},{1,0},{2,3},{3,2},{4,5},{5,4},{6,7},{7,6},{8,9},{9,8},{10,11... | collective-permute-start | bytes 3538952 | tf_op jit(solution)/shard_map/ppermute | solution.py:337
  2.8 3.7 %collective-permute-start.2 = (bf16[20,48,384]{2,1,0:T(8,128)(2,1)S(1)}, bf16[20,48,384]{2,1,0:T(8,128)(2,1)S(1)}, u32[]{:S(2)}, u32[]{:S(2)}) collective-permute-start(bf16[20,48,384]{2,1,0:T(8,128)(2,1)S(1)} %slice_bitcast_fusion), channel_id=1, source_target_pairs={{0,127},{1,2},{2,1},{3,4},{4,3},{5,6},{6,5},{7,8},{8,7},{9,10},{10... | collective-permute-start | bytes 2211848 | tf_op jit(solution)/shard_map/ppermute | solution.py:335
  6.5 1.1 %slice.11 = bf16[12,48,384]{2,1,0:T(8,128)(2,1)S(1)} slice(bf16[32,48,384]{2,1,0:T(8,128)(2,1)} %bitcast.7), slice={[20:32], [0:48], [0:384]} | slice | bytes 884736 | tf_op jit(solution)/shard_map/slice | solution.py:336
  7.5 0.1 collective-permute-start.3
  7.6 0.0 copy-done.4
  7.6 0.0 copy-done.5
  7.7 0.0 collective-permute-done.1.twin
  7.7 0.0 copy-done.2
  7.7 0.0 copy-done.3
  7.7 0.0 copy-start
  7.7 3.3 %copy-done = bf16[3,3,3,384,384]{4,3,2,1,0:T(8,128)(2,1)S(1)} copy-done((bf16[3,3,3,384,384]{4,3,2,1,0:T(8,128)(2,1)S(1)}, bf16[3,3,3,384,384]{4,3,2,1,0:T(8,128)(2,1)}, u32[]{:S(2)}) %copy-start) | copy-done | bytes 7962648
  11.0 0.0 copy-start.1
  11.0 12.6 %shard_map.57 = (f32[32,48,384]{2,1,0:T(8,128)S(1)}, s32[1]{0:T(128)}) custom-call(s32[16]{0:T(128)S(1)} %copy-done.3, bf16[32,48,384]{2,1,0:T(8,128)(2,1)S(1)} %bitcast.8, bf16[32,48,384]{2,1,0:T(8,128)(2,1)S(1)} %collective-permute-done.1.twin, bf16[3,3,3,384,384]{4,3,2,1,0:T(8,128)(2,1)S(1)} %copy-done, f32[1,384]{1,0:T(1,128)S(1)} %reshape.10.gain, ...), custom_call_target="tpu_custom_call" | custom-call | tf_op jit(solution)/shard_map/pallas_call | solution.py:100
  23.6 3.9 %collective-permute-done.2.far.recent = bf16[20,48,384]{2,1,0:T(8,128)(2,1)S(1)} collective-permute-done((bf16[20,48,384]{2,1,0:T(8,128)(2,1)S(1)}, bf16[20,48,384]{2,1,0:T(8,128)(2,1)S(1)}, u32[]{:S(2)}, u32[]{:S(2)}) %collective-permute-start.2) | collective-permute-done | bytes 737312 | tf_op jit(solution)/shard_map/ppermute | solution.py:335
  27.5 0.0 copy-done.1
  27.5 3.9 %shard_map.58.early = bf16[20,48,384]{2,1,0:T(8,128)(2,1)S(1)} custom-call(bf16[20,48,384]{2,1,0:T(8,128)(2,1)S(1)} %collective-permute-done.2.far.recent, f32[32,48,384]{2,1,0:T(8,128)S(1)} %get-tuple-element.29.partial, bf16[3,3,3,384,384]{4,3,2,1,0:T(8,128)(2,1)S(1)} %copy-done.1, f32[1,384]{1,0:T(1,128)S(1)} %reshape.10.gain), custom_call_target="tpu_custom_call" | custom-call | tf_op jit(solution)/shard_map/pallas_call | solution.py:189
  31.5 1.5 %collective-permute-done.3.far = bf16[12,48,384]{2,1,0:T(8,128)(2,1)S(1)} collective-permute-done((bf16[12,48,384]{2,1,0:T(8,128)(2,1)S(1)}, bf16[12,48,384]{2,1,0:T(8,128)(2,1)S(1)}, u32[]{:S(2)}, u32[]{:S(2)}) %collective-permute-start.3) | collective-permute-done | bytes 442400 | tf_op jit(solution)/shard_map/ppermute | solution.py:336
  33.0 3.2 %shard_map.59 = (bf16[16,3,48,384]{3,2,1,0:T(8,128)(2,1)S(1)}, bf16[16,4,48,384]{3,2,1,0:T(8,128)(2,1)S(1)}) custom-call(s32[16]{0:T(128)S(1)} %copy-done.3, bf16[20,48,384]{2,1,0:T(8,128)(2,1)S(1)} %collective-permute-done.2.far.recent, bf16[12,48,384]{2,1,0:T(8,128)(2,1)S(1)} %collective-permute-done.3.far, bf16[20,48,384]{2,1,0:T(8,128)(2,1)S(1)} %shard_map.58.early, ...), custom_call_target="tpu_custom_call" | custom-call | tf_op jit(solution)/shard_map/pallas_call | solution.py:201
  36.9 36.0 %conditional.1 = (bf16[4,16,48,384]{3,2,1,0:T(8,128)(2,1)}) conditional(s32[]{:T(128)} %bitcast.3, (bf16[16,4,48,384]{3,2,1,0:T(8,128)(2,1)S(1)}, s32[16]{0:T(128)S(1)}) %tuple.19, (bf16[16,3,48,384]{3,2,1,0:T(8,128)(2,1)S(1)}, s32[16]{0:T(128)S(1)}) %tuple.20), branch_computations={%region_0.0_spmd, %region_1.0_spmd} | conditional | bytes 5898288 | solution.py:343
  36.9 32.3 %all_to_all.9.arrived = bf16[16,3,48,384]{3,2,1,0:T(8,128)(2,1)S(1)} all-to-all(bf16[16,3,48,384]{3,2,1,0:T(8,128)(2,1)S(1)} %get-tuple-element.19), channel_id=1, replica_groups=mesh['ha'=8,'tc'=8,'core'=2] {'tc','core'}, dimensions={0} | all-to-all | bytes 3538944 | tf_op jit(solution)/shard_map/cond/branch_1_fun/all_to_all | solution.py:290
  69.2 0.6 branch_1_fun.3
  69.9 0.5 collective-permute-start
  70.3 2.0 %branch_1_fun.4.partial = bf16[4,16,48,384]{3,2,1,0:T(8,128)(2,1)} custom-call(s32[16]{0:T(128)S(1)} %get-tuple-element.18.starts, bf16[16,3,48,384]{3,2,1,0:T(8,128)(2,1)S(1)} %all_to_all.9.arrived), custom_call_target="tpu_custom_call" | custom-call | tf_op jit(solution)/shard_map/cond/branch_1_fun/pallas_call | solution.py:253
  72.3 0.0 collective-permute-done.other
  72.4 0.6 branch_1_fun.5
  (2 shorter events, 0.0 us)
Async XLA Ops:
  0.0 7.7 %copy-start.2 = (bf16[32,1,48,384]{3,2,1,0:T(8,128)(2,1)S(1)}, bf16[32,1,48,384]{3,2,1,0:T(8,128)(2,1)}, u32[]{:S(2)}) copy-start(bf16[32,1,48,384]{3,2,1,0:T(8,128)(2,1)} %param.7) | copy-start | bytes 3538948
  0.0 7.6 %copy-start.4 = (f32[384]{0:T(512)S(1)}, f32[384]{0:T(512)}, u32[]{:S(2)}) copy-start(f32[384]{0:T(512)} %param.9) | copy-start | bytes 4612
  0.0 7.6 %copy-start.5 = (f32[384]{0:T(512)S(1)}, f32[384]{0:T(512)}, u32[]{:S(2)}) copy-start(f32[384]{0:T(512)} %param.11) | copy-start | bytes 4612
  0.0 7.7 %copy-start.3 = (s32[16]{0:T(128)S(1)}, s32[16]{0:T(128)}, u32[]{:S(2)}) copy-start(s32[16]{0:T(128)} %starts.3) | copy-start | bytes 196
  1.3 6.4 %collective-permute-start.1 = (bf16[32,48,384]{2,1,0:T(8,128)(2,1)}, bf16[32,48,384]{2,1,0:T(8,128)(2,1)S(1)}, u32[]{:S(2)}, u32[]{:S(2)}) collective-permute-start(bf16[32,48,384]{2,1,0:T(8,128)(2,1)} %bitcast.6), channel_id=1, source_target_pairs={{0,1},{1,0},{2,3},{3,2},{4,5},{5,4},{6,7},{7,6},{8,9},{9,8},{10,11... | collective-permute-start | bytes 3538952 | tf_op jit(solution)/shard_map/ppermute | solution.py:337
  2.8 24.7 %collective-permute-start.2 = (bf16[20,48,384]{2,1,0:T(8,128)(2,1)S(1)}, bf16[20,48,384]{2,1,0:T(8,128)(2,1)S(1)}, u32[]{:S(2)}, u32[]{:S(2)}) collective-permute-start(bf16[20,48,384]{2,1,0:T(8,128)(2,1)S(1)} %slice_bitcast_fusion), channel_id=1, source_target_pairs={{0,127},{1,2},{2,1},{3,4},{4,3},{5,6},{6,5},{7,8},{8,7},{9,10},{10... | collective-permute-start | bytes 2211848 | tf_op jit(solution)/shard_map/ppermute | solution.py:335
  7.5 25.5 %collective-permute-start.3 = (bf16[12,48,384]{2,1,0:T(8,128)(2,1)S(1)}, bf16[12,48,384]{2,1,0:T(8,128)(2,1)S(1)}, u32[]{:S(2)}, u32[]{:S(2)}) collective-permute-start(bf16[12,48,384]{2,1,0:T(8,128)(2,1)S(1)} %slice.11), channel_id=1, source_target_pairs={{0,127},{1,2},{2,1},{3,4},{4,3},{5,6},{6,5},{7,8},{8,7},{9,10},{10... | collective-permute-start | bytes 1327112 | tf_op jit(solution)/shard_map/ppermute | solution.py:336
  7.7 3.3 %copy-start = (bf16[3,3,3,384,384]{4,3,2,1,0:T(8,128)(2,1)S(1)}, bf16[3,3,3,384,384]{4,3,2,1,0:T(8,128)(2,1)}, u32[]{:S(2)}) copy-start(bf16[3,3,3,384,384]{4,3,2,1,0:T(8,128)(2,1)} %weight.5) | copy-start | bytes 23887876
  11.0 16.6 %copy-start.1 = (bf16[3,3,3,384,384]{4,3,2,1,0:T(8,128)(2,1)S(1)}, bf16[3,3,3,384,384]{4,3,2,1,0:T(8,128)(2,1)}, u32[]{:S(2)}) copy-start(bf16[3,3,3,384,384]{4,3,2,1,0:T(8,128)(2,1)} %weight.5) | copy-start | bytes 23887876
  69.9 2.5 %collective-permute-start = (bf16[16,1,48,384]{3,2,1,0:T(8,128)(2,1)S(1)}, bf16[16,1,48,384]{3,2,1,0:T(8,128)(2,1)S(1)}, u32[]{:S(2)}, u32[]{:S(2)}) collective-permute-start(bf16[16,1,48,384]{3,2,1,0:T(8,128)(2,1)S(1)} %branch_1_fun.3), channel_id=1, source_target_pairs={{0,1},{1,0},{2,3},{3,2},{4,5},{5,4},{6,7},{7,6},{8,9},{9,8},{10,11... | collective-permute-start | bytes 1769480 | tf_op jit(solution)/shard_map/cond/branch_1_fun/ppermute | solution.py:316
